TPU v7x, 32 devices: a whole 2x2x4 slice. The times are simulated.
32 devices in a mesh: parts: 2 (over x), view: 8 (over z, y), slab: 2 (over core).
Axes of the slice: x: 2, y: 2, z: 4, core: 2. Of those that a mesh axis runs over, the one named last changes fastest.
Arguments:
- activity: bfloat16 [128, 32, 256], P(('parts', 'view'), 'slab'), parts along dimension 0, may hold values from 0.6 to 11.2
- histo_counts: int32 [32, 64, 32, 256], P(('parts', 'view'), None, 'slab'), parts along dimension 0, may hold values from 0 to 22
- background: bfloat16 [32, 32, 256], P(('parts', 'view'), 'slab'), parts along dimension 0, may hold values from 0.5 to 2
- blur_values: bfloat16 [16, 3, 256, 32], P('view'), may hold values from 0.0041503906 to 0.020751953
- band_start: int32 [16, 3, 256], P('view'), may hold values from 0 to 224, as said below
Outputs:
- gradient: float32 [128, 32, 256], P(('parts', 'view'), 'slab'), parts along dimension 0
There are 2 independent parts, one for each index of `parts`. A program takes and returns all parts, laid end to end along the dimension named above; an argument that names none is the same for every part. Nothing has to cross between parts.
Inputs may be any that keep to these rules, and one draw needn't show every extreme that they name: Each band lies inside the matrix: columns band_start to band_start + 31.
All inputs are finite; a program needn't handle non-finite values.
Results may differ from a plain program's by a relative error of at most 0.0003.
Values may be sent and summed in bfloat16 or wider, within the bound.
No kernel may reach another device: no remote copies, remote signals or barrier semaphores. Data moves between devices by JAX's collectives and lax.ppermute only.
A program may use at most 64 MiB of HBM per device.

v0:
```python
import jax
import jax.numpy as jnp
from jax import lax
from jax.sharding import PartitionSpec as P


def padded_2(shard, sides, width):
    for axis, dim in sides:
        size, length = (lax.axis_size(axis), shard.shape[dim])
        up = [(i, (i + 1) % size) for i in range(size - 1)]
        down = [(j, i) for i, j in up]
        last = lax.slice_in_dim(shard, length - width, length, axis=dim)
        leading = lax.slice_in_dim(shard, 0, width, axis=dim)
        before = lax.ppermute(last, axis, up)
        after = lax.ppermute(leading, axis, down)
        shard = jnp.concatenate([before, shard, after], axis=dim)
    return shard


def blur_matrix(band_values, band_starts):
    width_x = band_values.shape[0]
    band_width = band_values.shape[1]
    columns = jnp.arange(width_x, dtype=jnp.int32)
    distance = columns[None, :] - band_starts[:, None]
    selector = (
        distance[:, :, None] == jnp.arange(band_width, dtype=jnp.int32)[None, None, :]
    ).astype(jnp.float32)
    return jnp.einsum("ik,ijk->ij", band_values.astype(jnp.float32), selector).astype(jnp.bfloat16)


def per_device(activity, histo_counts, background, blur_values, band_start):
    source = padded_2(activity, (("slab", 1),), 1)
    gathered = lax.all_gather(source, "view", axis=0, tiled=True)
    rows_y = gathered.shape[0]
    slices = gathered.shape[1] - 2
    width_x = gathered.shape[2]
    prepared = []
    for view_index in range(histo_counts.shape[0]):
        matrices = [
            blur_matrix(blur_values[view_index, tap_index], band_start[view_index, tap_index])
            for tap_index in range(3)
        ]
        summed = jnp.zeros((rows_y * slices, width_x), jnp.float32)
        for tap_index in range(3):
            shifted = gathered[:, tap_index : tap_index + slices, :].reshape(-1, width_x)
            summed = summed + jnp.dot(
                shifted, matrices[tap_index].T, preferred_element_type=jnp.float32
            )
        expected = (
            summed.reshape(rows_y, slices, width_x)
            + background[view_index].astype(jnp.float32)[None]
        )
        ratio_bf = (histo_counts[view_index].astype(jnp.float32) / expected - 1.0).astype(
            jnp.bfloat16
        )
        widened = padded_2(ratio_bf, (("slab", 1),), 1)
        edge_terms = None
        prepared.append((widened, matrices, edge_terms))
    gathered_sum = jnp.zeros((rows_y, slices, width_x), jnp.float32)
    for widened, matrices, edge_terms in prepared:
        back_sum = jnp.zeros((rows_y * slices, width_x), jnp.float32)
        for tap_index in range(3):
            shifted = widened[:, 2 - tap_index : 2 - tap_index + slices, :].reshape(-1, width_x)
            back_sum = back_sum + jnp.dot(
                shifted, matrices[tap_index], preferred_element_type=jnp.float32
            )
        back_sum = back_sum.reshape(rows_y, slices, width_x)
        gathered_sum = gathered_sum + back_sum
    return lax.psum_scatter(gathered_sum, "view", scatter_dimension=0, tiled=True)


def solution(mesh):
    placed = (
        P(("parts", "view"), "slab", None),
        P(("parts", "view"), None, "slab", None),
        P(("parts", "view"), "slab", None),
        P("view", None, None, None),
        P("view", None, None),
    )
    return jax.shard_map(
        per_device,
        mesh=mesh,
        in_specs=placed,
        out_specs=P(("parts", "view"), "slab", None),
        check_vma=False,
    )
```

profile of v0, /device:TPU:0, one launch (start us, length us, event | category | flops | bytes accessed | tf_op | source)
XLA Modules:
  0.0 152.2 jit_solution(17783178895907580288)
XLA Ops:
  6.5 0.9 copy.45
  7.4 1.3 collective-permute-start.1
  8.7 3.2 %collective-permute-start = (bf16[8,1,256]{2,0,1:T(8,128)(2,1)S(1)}, bf16[8,1,256]{2,0,1:T(8,128)(2,1)S(1)}, u32[]{:S(2)}, u32[]{:S(2)}) collective-permute-start(bf16[8,1,256]{2,0,1:T(8,128)(2,1)S(1)} %get-tuple-element.26), channel_id=1, source_target_pairs={{0,1},{2,3},{4,5},{6,7},{8,9},{10,11},{12,13},{14,15},{16,17},{18,... | collective-permute-start | bytes 12296 | tf_op jit(solution)/shard_map/ppermute | solution.py:14
  11.9 1.8 %slice_convert_fusion.1 = (f32[1,64,16,256]{3,2,1,0:T(8,128)S(1)}, f32[1,64,16,256]{3,2,1,0:T(8,128)S(1)}) fusion(s32[2,64,16,256]{3,2,1,0:T(8,128)} %param.6), kind=kLoop, calls=%fused_computation.42 | loop fusion | flops 524288 | bytes 4194304 | tf_op jit(solution)/shard_map/convert_element_type | solution.py:53
  13.7 0.8 copy.51
  14.6 0.8 copy.53
  15.5 0.8 copy.55
  16.4 0.8 copy.57
  17.3 0.8 copy.59
  18.1 0.8 copy.61
  19.0 2.4 %fusion = bf16[256,1,256]{2,1,0:T(2,128)(2,1)S(1)} fusion(bf16[256,32,1]{1,2,0:T(2,128)(2,1)} %copy.51, s32[256,256]{1,0:T(8,128)S(1)} %iota_subtract_fusion.5), kind=kOutput, calls=%fused_computation.6 | convolution fusion | flops 6291456 | bytes 409600 | tf_op jit(solution)/shard_map/ik,ijk->ij/dot_general | solution.py:28
  21.4 1.4 fusion.1
  22.9 1.4 fusion.2
  24.3 1.4 fusion.3
  25.8 1.4 fusion.4
  27.2 1.4 fusion.5
  28.7 33.7 %all_gather.3 = bf16[64,18,256]{2,0,1:T(8,128)(2,1)S(1)} all-gather(bf16[8,18,256]{2,0,1:T(8,128)(2,1)S(1)} %pad_maximum_fusion.4), channel_id=1, replica_groups=mesh['parts'=2,'view'=8,'slab'=2] {'view'}, dimensions={0}, use_global_device_ids=true | all-gather | bytes 663552 | tf_op jit(solution)/shard_map/all_gather | solution.py:33
  63.5 0.3 fusion.25
  64.2 0.3 convolution_add_fusion.5
  64.8 0.4 fusion.22
  65.2 0.4 fusion.17
  65.6 1.2 copy-done
  66.8 0.6 fusion.24
  67.5 1.3 collective-permute-start.4
  68.8 3.0 %collective-permute-start.5 = (bf16[64,1,256]{2,1,0:T(2,128)(2,1)S(1)}, bf16[64,1,256]{2,1,0:T(2,128)(2,1)S(1)}, u32[]{:S(2)}, u32[]{:S(2)}) collective-permute-start(bf16[64,1,256]{2,1,0:T(2,128)(2,1)S(1)} %get-tuple-element.19), channel_id=1, source_target_pairs={{0,1},{2,3},{4,5},{6,7},{8,9},{10,11},{12,13},{14,15},{16,17},{18,... | collective-permute-start | bytes 98312 | tf_op jit(solution)/shard_map/ppermute | solution.py:14
  72.3 1.3 collective-permute-start.2
  73.6 3.0 %collective-permute-start.3 = (bf16[64,1,256]{2,1,0:T(2,128)(2,1)S(1)}, bf16[64,1,256]{2,1,0:T(2,128)(2,1)S(1)}, u32[]{:S(2)}, u32[]{:S(2)}) collective-permute-start(bf16[64,1,256]{2,1,0:T(2,128)(2,1)S(1)} %get-tuple-element.15), channel_id=1, source_target_pairs={{0,1},{2,3},{4,5},{6,7},{8,9},{10,11},{12,13},{14,15},{16,17},{18,... | collective-permute-start | bytes 98312 | tf_op jit(solution)/shard_map/ppermute | solution.py:14
  76.9 0.5 pad_maximum_fusion.1
  77.8 0.5 pad_maximum_fusion.3
  78.6 0.3 fusion.12
  79.0 1.3 fusion.14
  80.3 65.1 %reduce-scatter.2.cloned.1.call-done = f32[8,16,256]{2,1,0:T(8,128)} async-done(((f32[64,16,256]{2,1,0:T(8,128)}), f32[8,16,256]{2,1,0:T(8,128)}) %reduce-scatter.2.cloned.1.call-update) | async-done | bytes 131088 | tf_op jit(solution)/shard_map/reduce_scatter | solution.py:69
  (48 shorter events, 3.8 us)
Async XLA Ops:
  6.5 138.9 %reduce-scatter.2.cloned.1.call-start = ((), (), s32[]{:S(2)}) async-start(), calls=%async_computation.1 | async-start | bytes 1179648 | tf_op jit(solution)/shard_map/reduce_scatter | solution.py:69
  7.4 21.3 %collective-permute-start.1 = (bf16[8,1,256]{2,0,1:T(8,128)(2,1)S(1)}, bf16[8,1,256]{2,0,1:T(8,128)(2,1)S(1)}, u32[]{:S(2)}, u32[]{:S(2)}) collective-permute-start(bf16[8,1,256]{2,0,1:T(8,128)(2,1)S(1)} %get-tuple-element.27), channel_id=1, source_target_pairs={{1,0},{3,2},{5,4},{7,6},{9,8},{11,10},{13,12},{15,14},{17,16},{19,... | collective-permute-start | bytes 12296 | tf_op jit(solution)/shard_map/ppermute | solution.py:15
  8.7 5.0 %copy-start.6 = (bf16[2,3,256,32]{2,3,1,0:T(8,128)(2,1)S(1)}, bf16[2,3,256,32]{2,3,1,0:T(8,128)(2,1)}, u32[]{:S(2)}) copy-start(bf16[2,3,256,32]{2,3,1,0:T(8,128)(2,1)} %param.8) | copy-start | bytes 294916
  8.7 5.8 %copy-start.8 = (s32[2,3,256]{2,0,1:T(2,128)S(1)}, s32[2,3,256]{2,0,1:T(2,128)}, u32[]{:S(2)}) copy-start(s32[2,3,256]{2,0,1:T(2,128)} %param.9) | copy-start | bytes 18436
  8.7 20.0 %collective-permute-start = (bf16[8,1,256]{2,0,1:T(8,128)(2,1)S(1)}, bf16[8,1,256]{2,0,1:T(8,128)(2,1)S(1)}, u32[]{:S(2)}, u32[]{:S(2)}) collective-permute-start(bf16[8,1,256]{2,0,1:T(8,128)(2,1)S(1)} %get-tuple-element.26), channel_id=1, source_target_pairs={{0,1},{2,3},{4,5},{6,7},{8,9},{10,11},{12,13},{14,15},{16,17},{18,... | collective-permute-start | bytes 12296 | tf_op jit(solution)/shard_map/ppermute | solution.py:14
  19.0 2.4 %copy-start.1 = (bf16[256,32,1]{1,2,0:T(2,128)(2,1)S(1)}, bf16[256,32,1]{1,2,0:T(2,128)(2,1)}, u32[]{:S(2)}) copy-start(bf16[256,32,1]{1,2,0:T(2,128)(2,1)} %copy.53) | copy-start | bytes 49156
  21.4 1.4 copy-start.2
  22.9 1.4 copy-start.3
  24.3 1.4 copy-start.4
  25.8 1.4 copy-start.5
  27.2 1.5 copy-start.7
  65.2 1.6 %copy-start = (s32[2,64,16,256]{3,2,1,0:T(8,128)S(1)}, s32[2,64,16,256]{3,2,1,0:T(8,128)}, u32[]{:S(2)}) copy-start(s32[2,64,16,256]{3,2,1,0:T(8,128)} %param.6) | copy-start | bytes 6291460
  67.5 9.4 %collective-permute-start.4 = (bf16[64,1,256]{2,1,0:T(2,128)(2,1)S(1)}, bf16[64,1,256]{2,1,0:T(2,128)(2,1)S(1)}, u32[]{:S(2)}, u32[]{:S(2)}) collective-permute-start(bf16[64,1,256]{2,1,0:T(2,128)(2,1)S(1)} %get-tuple-element.18), channel_id=1, source_target_pairs={{1,0},{3,2},{5,4},{7,6},{9,8},{11,10},{13,12},{15,14},{17,16},{19,... | collective-permute-start | bytes 98312 | tf_op jit(solution)/shard_map/ppermute | solution.py:15
  68.8 8.1 %collective-permute-start.5 = (bf16[64,1,256]{2,1,0:T(2,128)(2,1)S(1)}, bf16[64,1,256]{2,1,0:T(2,128)(2,1)S(1)}, u32[]{:S(2)}, u32[]{:S(2)}) collective-permute-start(bf16[64,1,256]{2,1,0:T(2,128)(2,1)S(1)} %get-tuple-element.19), channel_id=1, source_target_pairs={{0,1},{2,3},{4,5},{6,7},{8,9},{10,11},{12,13},{14,15},{16,17},{18,... | collective-permute-start | bytes 98312 | tf_op jit(solution)/shard_map/ppermute | solution.py:14
  72.3 5.5 %collective-permute-start.2 = (bf16[64,1,256]{2,1,0:T(2,128)(2,1)S(1)}, bf16[64,1,256]{2,1,0:T(2,128)(2,1)S(1)}, u32[]{:S(2)}, u32[]{:S(2)}) collective-permute-start(bf16[64,1,256]{2,1,0:T(2,128)(2,1)S(1)} %get-tuple-element.14), channel_id=1, source_target_pairs={{1,0},{3,2},{5,4},{7,6},{9,8},{11,10},{13,12},{15,14},{17,16},{19,... | collective-permute-start | bytes 98312 | tf_op jit(solution)/shard_map/ppermute | solution.py:15
  73.6 4.2 %collective-permute-start.3 = (bf16[64,1,256]{2,1,0:T(2,128)(2,1)S(1)}, bf16[64,1,256]{2,1,0:T(2,128)(2,1)S(1)}, u32[]{:S(2)}, u32[]{:S(2)}) collective-permute-start(bf16[64,1,256]{2,1,0:T(2,128)(2,1)S(1)} %get-tuple-element.15), channel_id=1, source_target_pairs={{0,1},{2,3},{4,5},{6,7},{8,9},{10,11},{12,13},{14,15},{16,17},{18,... | collective-permute-start | bytes 98312 | tf_op jit(solution)/shard_map/ppermute | solution.py:14
Sparse Core Ops, SparseCore 0:
  80.4 64.9 reduce-scatter.1
where the time goes:
time: 153 us; the launch traced here: 152 us
  waiting for transfers between devices  65.1 us (43%)
  blocking collectives  33.7 us (22%)
  matrix products  14.6 us (10%)
  between operations  13.7 us (9%)
  starting transfers between devices  13.1 us (9%)
  local copies, waits for them, and re-layouts  8.05 us (5%)
  other arithmetic  4 us (3%)
    reduce_scatter x1, waiting for transfers between devices, per_device(): lax.psum_scatter(gathered_sum, 'view', scatter_dimension=0, tiled=True)  65.1 us
    all_gather x1, blocking collectives, per_device(): gathered = lax.all_gather(source, 'view', axis=0, tiled=True)  33.7 us
    dot_general x6, matrix products, blur_matrix(): jnp.einsum('ik,ijk->ij', band_values.astype(jnp.float32), selector)  9.59 us
    ppermute x3, starting transfers between devices, padded_2(): before = lax.ppermute(last, axis, up)  9.22 us
    squeeze x7, local copies, waits for them, and re-layouts, per_device(): blur_values[view_index, tap_index]  4.68 us
    ppermute x3, starting transfers between devices, padded_2(): after = lax.ppermute(leading, axis, down)  3.88 us
  transfers between devices with their start and end apart: 7, of which 1 were waited for; matrix products, arithmetic and copies ran while one was open for 12% of the time, Pallas kernels for 0%

commit v1 on v0

v1 whole, which is shorter than its diff:
```python
import functools

import jax
import jax.numpy as jnp
from jax import lax
from jax.experimental import pallas as pl
from jax.experimental.pallas import tpu as pltpu
from jax.sharding import PartitionSpec as P

VMEM = pl.BlockSpec(memory_space=pltpu.VMEM)
SMEM = pl.BlockSpec(memory_space=pltpu.SMEM)
BF16, F32, I32 = jnp.bfloat16, jnp.float32, jnp.int32


def build_kernel(values_ref, starts_ref, out_ref):
    views, taps, band, width = values_ref.shape
    for view in range(views):
        for tap in range(taps):
            start = starts_ref[view * taps + tap : view * taps + tap + 1, :]
            moved = jnp.concatenate(
                [values_ref[view, tap].astype(F32), jnp.zeros((8, width), F32)], axis=0
            )
            for step in (1, 2, 4):
                moved = jnp.where((start & step) != 0, pltpu.roll(moved, step, 0), moved)
            step = 8
            while step < width:
                length = moved.shape[0]
                longer = min(length + step, width)
                zeros = jnp.zeros((step, width), F32)
                down = jnp.concatenate([zeros, moved], axis=0)[:longer]
                stay = jnp.concatenate([moved, zeros], axis=0)[:longer]
                moved = jnp.where((start & step) != 0, down, stay)
                step *= 2
            out_ref[view, tap] = moved.astype(BF16)


def build(values, starts):
    views, taps, _, width = values.shape
    return pl.pallas_call(
        build_kernel,
        out_shape=jax.ShapeDtypeStruct((views, taps, width, width), BF16),
        in_specs=[VMEM, VMEM],
        out_specs=VMEM,
        cost_estimate=pl.CostEstimate(
            flops=views * taps * width * width * 8,
            bytes_accessed=views * taps * width * width * 2,
            transcendentals=0,
        ),
    )(values, starts)


def rows_kernel(groups, blocks, flags_ref, source_ref, *refs):
    taps, full, width = source_ref.shape
    ins, (outs, (ratio_ref, first_ref, last_ref)) = (
        refs[: 5 * groups],
        (refs[5 * groups : 5 * groups + blocks], refs[5 * groups + blocks :]),
    )
    rows, slices = ratio_ref.shape[1] - 0, outs[0].shape[1]
    rows = full // (slices + 2)
    main = rows * slices
    views = []
    for group in range(groups):
        counts_ref, edge_ref, back_ref, back_edge_ref, matrix_ref = ins[5 * group : 5 * group + 5]
        for view in range(counts_ref.shape[0]):
            at = len(views)
            expected = jnp.dot(source_ref[0], matrix_ref[view, 0], preferred_element_type=F32)
            for tap in range(1, taps):
                expected += jnp.dot(
                    source_ref[tap], matrix_ref[view, tap], preferred_element_type=F32
                )
            inner = expected[:main].reshape(rows, slices, width) + back_ref[view].astype(F32)[None]
            counts = counts_ref[view].astype(F32).reshape(rows, slices, width)
            ratio_ref[at, :main] = (counts / inner - 1.0).astype(BF16).reshape(main, width)
            for side in range(2):
                low = main + side * rows
                outer = (
                    expected[low : low + rows]
                    + back_edge_ref[view, side : side + 1].astype(F32)
                )
                ratio = edge_ref[view, side].astype(F32) / outer - 1.0
                ratio = jnp.where(flags_ref[side] != 0, ratio, 0.0)
                ratio_ref[at, low : low + rows] = ratio.astype(BF16)
            views.append((matrix_ref, view))

    def back(tap, start, stop):
        total = None
        for at, (matrix_ref, view) in enumerate(views):
            term = lax.dot_general(
                ratio_ref[at, start:stop],
                matrix_ref[view, tap],
                (((1,), (1,)), ((), ())),
                preferred_element_type=F32,
            )
            total = term if total is None else total + term
        return total

    first = back(0, 0, full)
    first_ref[:, :slices, :] = first[:main].reshape(rows, slices, width)
    first_ref[:, slices, :] = first[main + rows :]
    last = back(2, 0, main + rows)
    last_ref[:, 8 : 8 + slices, :] = last[:main].reshape(rows, slices, width)
    last_ref[:, 7, :] = last[main:]
    middle = back(1, 0, main).reshape(rows, slices, width)
    total = middle + first_ref[:, 1 : 1 + slices, :] + last_ref[:, 7 : 7 + slices, :]
    each = rows // blocks
    for block in range(blocks):
        outs[block][...] = total[block * each : (block + 1) * each]


def row_terms(flags, source, groups, blocks, rows, slices):
    taps, full, width = source.shape
    n_views = sum(group[0].shape[0] for group in groups)
    flops = 4 * n_views * taps * full * width * width
    return pl.pallas_call(
        functools.partial(rows_kernel, len(groups), blocks),
        out_shape=[jax.ShapeDtypeStruct((rows // blocks, slices, width), F32)] * blocks,
        in_specs=[SMEM] + [VMEM] * (1 + 5 * len(groups)),
        out_specs=[VMEM] * blocks,
        scratch_shapes=[
            pltpu.VMEM((n_views, full, width), BF16),
            pltpu.VMEM((rows, slices + 8, width), F32),
            pltpu.VMEM((rows, slices + 8, width), F32),
        ],
        compiler_params=pltpu.CompilerParams(vmem_limit_bytes=24 * 1024 * 1024),
        cost_estimate=pl.CostEstimate(flops=flops, bytes_accessed=4 * full * width, transcendentals=0),
    )(flags, source, *[x for group in groups for x in group])


def per_device(activity, histo_counts, background, blur_values, band_start):
    each, slices, width = activity.shape
    views, taps, _, band = blur_values.shape
    n_slab, slab = lax.axis_size("slab"), lax.axis_index("slab")
    n_view, at_view = lax.axis_size("view"), lax.axis_index("view")
    pairs = 2 if n_view % 2 == 0 else 1
    line = n_view // pairs
    at_line, side = at_view // pairs, at_view % pairs
    xor = line & (line - 1) == 0

    def peer(at, k):
        return at ^ k if xor else (at + k) % line

    def across(k, towards):
        moves = [(i, peer(i // pairs, k) * pairs + i % pairs) for i in range(n_view)]
        return moves if towards else [(j, i) for i, j in moves]

    other = [(i, i ^ 1) for i in range(n_view)]

    counts = histo_counts.reshape(views, line, pairs, each, slices, width)

    def edges(at, length):
        pick = lambda x, axis, n: lax.slice_in_dim(
            x, 0 if at == 0 else slices - n, n if at == 0 else slices, axis=axis
        )
        return jnp.concatenate(
            [
                pick(activity, 1, 2).reshape(-1, width),
                pick(counts, 4, 1).astype(BF16).reshape(-1, width),
                pick(background, 1, 1).reshape(-1, width),
            ],
            axis=0,
        )

    if n_slab == 2:
        swapped = lax.ppermute(
            jnp.where(slab == 0, edges(1, 0), edges(0, 0)), "slab", [(0, 1), (1, 0)]
        )[None]
    elif n_slab > 2:
        up = [(i, i + 1) for i in range(n_slab - 1)]
        swapped = jnp.stack(
            [
                lax.ppermute(edges(1, 0), "slab", up),
                lax.ppermute(edges(0, 0), "slab", [(j, i) for i, j in up]),
            ]
        )
    else:
        swapped = jnp.zeros((1, each * (2 + views * line * pairs) + views, width), BF16)
    n_edges = swapped.shape[0]
    has = jnp.stack([slab > 0, slab < n_slab - 1])

    def sides(x):
        both = jnp.concatenate([x, x], axis=0) if n_edges == 1 else x
        return jnp.where(has.reshape((2,) + (1,) * (x.ndim - 1)), both, jnp.zeros_like(both))

    cut = [2 * each, 2 * each + views * line * pairs * each]
    edge_activity = sides(swapped[:, : cut[0]].reshape(n_edges, each, 2, width))
    edge_counts = swapped[:, cut[0] : cut[1]].reshape(n_edges, views, line, pairs, each, width)
    edge_back = swapped[:, cut[1] :]

    def rows_of(x, k, of_side, axis):
        x = lax.dynamic_slice_in_dim(x, peer(at_line, k), 1, axis=axis)
        x = lax.dynamic_slice_in_dim(x, of_side, 1, axis=axis + 1)
        return x.reshape(x.shape[:axis] + x.shape[axis + 2 :])

    def gather_rows(x, ks, of_side, axis):
        return jnp.stack([rows_of(x, k, of_side, axis) for k in ks], axis=axis)

    halves = [h for h in (range(line // 2, line), range(line // 2)) if len(h)]
    values = jnp.swapaxes(blur_values, 2, 3)
    starts = band_start.reshape(views * taps, width)

    theirs = []
    if pairs == 2:
        for ks in halves:
            sent = gather_rows(counts, ks, 1 - side, 1).astype(BF16)
            theirs.append(lax.ppermute(sent, "view", other))
        edge_out = gather_rows(edge_counts, range(line), 1 - side, 2)
        exact = width <= 256
        pieces = [values.reshape(-1, width), background.reshape(-1, width), edge_back.reshape(-1, width)]
        pieces += [edge_out.reshape(-1, width)]
        if exact:
            pieces.append(starts.astype(BF16))
        sizes = [p.shape[0] for p in pieces]
        arrived = lax.ppermute(jnp.concatenate(pieces, axis=0), "view", other)
        parts, low = [], 0
        for size in sizes:
            parts.append(arrived[low : low + size])
            low += size
        their_starts = parts[4].astype(I32) if exact else lax.ppermute(starts, "view", other)

    padded = jnp.concatenate([edge_activity[0], activity, edge_activity[1]], axis=1)
    blocks = [padded] + [
        lax.ppermute(padded, "view", across(k, False)) for k in range(1, line)
    ]

    mine_matrices = build(values, starts)
    if pairs == 2:
        their_matrices = build(parts[0].reshape(values.shape), their_starts)

    flags = has.astype(I32)
    back_edges = lambda x: jnp.swapaxes(sides(x.reshape(n_edges, views, width)), 0, 1)
    terms = {}
    for at, ks in enumerate(halves):
        rows = len(ks) * each
        taken = jnp.concatenate([blocks[k] for k in ks], axis=0)
        source = jnp.stack(
            [
                jnp.concatenate(
                    [
                        taken[:, 1 + t : 1 + t + slices].reshape(-1, width),
                        taken[:, t],
                        taken[:, slices + 1 + t],
                    ],
                    axis=0,
                )
                for t in range(taps)
            ]
        )

        def group(rows_counts, edge, back, back_edge, matrices):
            edge = jnp.moveaxis(sides(edge), 0, 1).reshape(views, 2, rows, width)
            return (
                rows_counts.reshape(views, rows * slices, width),
                edge,
                back.reshape(views, slices, width),
                back_edges(back_edge),
                matrices,
            )

        groups = [
            group(
                gather_rows(counts, ks, side, 1).astype(BF16),
                gather_rows(edge_counts, ks, side, 2),
                background,
                edge_back,
                mine_matrices,
            )
        ]
        if pairs == 2:
            edge_in = parts[3].reshape(n_edges, views, line, each, width)[:, :, ks[0] : ks[-1] + 1]
            groups.append(group(theirs[at], edge_in, parts[1], parts[2], their_matrices))
        outs = row_terms(flags, source, groups, len(ks), rows, slices)
        terms.update(zip(ks, outs))
    total = terms[0]
    for k in reversed(range(1, line)):
        total = total + lax.ppermute(terms[k], "view", across(k, True))
    return total


def solution(mesh):
    placed = (
        P(("parts", "view"), "slab", None),
        P(("parts", "view"), None, "slab", None),
        P(("parts", "view"), "slab", None),
        P("view", None, None, None),
        P("view", None, None),
    )
    return jax.shard_map(
        per_device,
        mesh=mesh,
        in_specs=placed,
        out_specs=P(("parts", "view"), "slab", None),
        check_vma=False,
    )
```

time: 153 us -> 49.6 us (0.32)
  waiting for transfers between devices: 65.1 us -> 14.8 us
  blocking collectives: 33.7 us -> 0 us
  matrix products: 14.6 us -> 0 us
  between operations: 13.7 us -> 0.42 us
  Pallas kernels: 0 us -> 7.49 us
  other arithmetic: 4 us -> 6.37 us
  local copies, waits for them, and re-layouts: 8.05 us -> 6.24 us
    reduce_scatter x1 -> x0, waiting for transfers between devices: 65.1 us -> none  [per_device(): lax.psum_scatter(gathered_sum, 'view', scatter_dimension=0, tiled=True)]
    all_gather x1 -> x0, blocking collectives: 33.7 us -> none  [per_device(): gathered = lax.all_gather(source, 'view', axis=0, tiled=True)]
    ppermute x6 -> x10, waiting for transfers between devices: 0.02 us -> 14.8 us  [the longest x3 6.33 us: per_device(): lax.ppermute(padded, 'view', across(k, False))]
    dot_general x18 -> x0, matrix products: 14.6 us -> none  [the longest x6 9.59 us: blur_matrix(): jnp.einsum('ik,ijk->ij', band_values.astype(jnp.float32), selector)]
    pallas_call x0 -> x4, Pallas kernels: none -> 7.49 us  [the longest x2 4.16 us: build(): pl.pallas_call(build_kernel, out_shape=jax.ShapeDtypeStruct((views, taps,...]
    another operation x0 -> x14, other arithmetic: none -> 4.68 us
    squeeze x7 -> x2, local copies, waits for them, and re-layouts: 4.68 us -> 0.01 us  [the longest x1 0.01 us: per_device(): taken[:, t]]
    slice x5 -> x17, local copies, waits for them, and re-layouts: 0.4 us -> 3.43 us  [the longest x3 0.9 us: edges(): lax.slice_in_dim(x, 0 if at == 0 else slices - n, n if at == 0 else slice...]
  transfers between devices with their start and end apart: 7 -> 10, of which waited for: 1 -> 5; matrix products, arithmetic and copies ran while one was open for 12% -> 13% of each run, Pallas kernels for 0% -> 15%
where the time goes in v1:
time: 49.6 us; the launch traced here: 49.2 us
  waiting for transfers between devices  14.8 us (30%)
  starting transfers between devices  13.9 us (28%)
  Pallas kernels  7.49 us (15%)
  other arithmetic  6.37 us (13%)
  local copies, waits for them, and re-layouts  6.24 us (13%)
    ppermute x3, waiting for transfers between devices, per_device(): lax.ppermute(padded, 'view', across(k, False))  6.33 us
    ppermute x3, waiting for transfers between devices, per_device(): total = total + lax.ppermute(terms[k], 'view', across(k, True))  5.52 us
    ppermute x3, starting transfers between devices, per_device(): lax.ppermute(padded, 'view', across(k, False))  4.74 us
    ppermute x3, starting transfers between devices, per_device(): total = total + lax.ppermute(terms[k], 'view', across(k, True))  4.5 us
    pallas_call x2, Pallas kernels, build(): pl.pallas_call(build_kernel, out_shape=jax.ShapeDtypeStruct((views, taps,...  4.16 us
    pallas_call x2, Pallas kernels, row_terms(): pl.pallas_call(functools.partial(rows_kernel, len(groups), blocks), out_s...  3.33 us
    ppermute x1, waiting for transfers between devices, per_device(): arrived = lax.ppermute(jnp.concatenate(pieces, axis=0), 'view', other)  2.94 us
    another operation x1, other arithmetic  2.71 us
  transfers between devices with their start and end apart: 10, of which 5 were waited for; matrix products, arithmetic and copies ran while one was open for 13% of the time, Pallas kernels for 15%

profile of v1, /device:TPU:0, one launch (start us, length us, event | category | flops | bytes accessed | tf_op | source)
XLA Modules:
  0.0 49.2 jit_solution(1206398350994138835)
XLA Ops:
  0.0 0.9 %fusion.20 = (bf16[2,1,256]{2,1,0:T(2,128)(2,1)S(1)}, bf16[2,1,256]{2,1,0:T(2,128)(2,1)S(1)}) fusion(bf16[2,16,256]{2,1,0:T(8,128)(2,1)} %refs_2_.3), kind=kLoop, calls=%fused_computation.83 | loop fusion | bytes 4096 | tf_op jit(solution)/shard_map/slice | solution.py:151
  0.9 2.7 %copy_convert_fusion = bf16[2,4,2,8,16,256]{5,3,2,1,0,4:T(8,128)(2,1)S(1)} fusion(s32[2,4,2,8,16,256]{5,4,3,2,1,0:T(8,128)} %bitcast.167), kind=kLoop, calls=%fused_computation | loop fusion | flops 524288 | bytes 3145728 | tf_op jit(solution)/shard_map/convert.17
  3.7 0.5 %collective-permute-start = (bf16[146,256]{1,0:T(8,128)(2,1)S(1)}, bf16[146,256]{1,0:T(8,128)(2,1)}, u32[]{:S(2)}, u32[]{:S(2)}) collective-permute-start(bf16[146,256]{1,0:T(8,128)(2,1)S(1)} %maximum_select_fusion), channel_id=1, source_target_pairs={{0,1},{1,0},{2,3},{3,2},{4,5},{5,4},{6,7},{7,6},{8,9},{9,8},{10,11... | collective-permute-start | bytes 224264 | tf_op jit(solution)/shard_map/ppermute | solution.py:164
  4.2 0.3 fusion.6
  4.6 0.7 %pad_maximum_fusion.3 = bf16[2,2,8,16,256]{4,3,2,1,0:T(8,128)(2,1)} fusion(bf16[2,1,8,16,256]{4,3,2,1,0:T(8,128)(2,1)S(1)} %get-tuple-element.18, bf16[2,1,8,16,256]{4,3,2,1,0:T(8,128)(2,1)S(1)} %get-tuple-element.19), kind=kLoop, calls=%fused_computation.4 | loop fusion | flops 131072 | bytes 524288 | tf_op jit(solution)/shard_map/stack | solution.py:195
  5.3 2.6 %collective-permute-start.2 = (bf16[2,2,8,16,256]{4,3,2,1,0:T(8,128)(2,1)}, bf16[2,2,8,16,256]{4,3,2,1,0:T(8,128)(2,1)S(1)}, u32[]{:S(2)}, u32[]{:S(2)}) collective-permute-start(bf16[2,2,8,16,256]{4,3,2,1,0:T(8,128)(2,1)} %pad_maximum_fusion.3), channel_id=1, source_target_pairs={{0,2},{2,0},{4,6},{6,4},{8,10},{10,8},{12,14},{14,12},{1,3},{3,1},... | collective-permute-start | bytes 786440 | tf_op jit(solution)/shard_map/ppermute | solution.py:205
  7.9 0.7 %pad_maximum_fusion.5 = bf16[2,2,8,16,256]{4,3,2,1,0:T(8,128)(2,1)} fusion(bf16[2,1,8,16,256]{4,3,2,1,0:T(8,128)(2,1)S(1)} %get-tuple-element.22, bf16[2,1,8,16,256]{4,3,2,1,0:T(8,128)(2,1)S(1)} %get-tuple-element.15), kind=kLoop, calls=%fused_computation.6 | loop fusion | flops 131072 | bytes 524288 | tf_op jit(solution)/shard_map/stack | solution.py:195
  8.7 0.6 %copy-done.6 = s32[6,256]{1,0:T(8,128)} copy-done((s32[6,256]{1,0:T(8,128)}, s32[6,256]{1,0:T(8,128)S(1)}, u32[]{:S(2)}) %copy-start.6) | copy-done | bytes 6168
  9.3 2.1 %shard_map.55.refs_4_ = bf16[2,3,256,256]{3,2,1,0:T(8,128)(2,1)} custom-call(bf16[2,3,32,256]{3,2,1,0:T(8,128)(2,1)} %bitcast.175, s32[6,256]{1,0:T(8,128)} %copy-done.6), custom_call_target="tpu_custom_call" | custom-call | flops 3145728 | bytes 786432 | tf_op jit(solution)/shard_map/pallas_call | solution.py:39
  11.4 0.1 fusion.14
  11.5 0.7 %slice.148 = bf16[1,16,256]{2,1,0:T(8,128)(2,1)S(1)} slice(bf16[1,146,256]{2,1,0:T(8,128)(2,1)} %bitcast.7), slice={[0:1], [0:16], [0:256]} | slice | bytes 16384 | tf_op jit(solution)/shard_map/slice | solution.py:185
  12.2 0.7 %slice_bitcast_fusion.9 = (bf16[2,256]{1,0:T(2,128)(2,1)S(1)}, bf16[1,2,256]{2,1,0:T(2,128)(2,1)S(1)}) fusion(bf16[1,146,256]{2,1,0:T(8,128)(2,1)} %bitcast.7), kind=kLoop, calls=%fused_computation.76 | loop fusion | bytes 3072
  12.9 0.8 %slice.154 = bf16[1,128,256]{2,1,0:T(8,128)(2,1)S(1)} slice(bf16[1,146,256]{2,1,0:T(8,128)(2,1)} %bitcast.7), slice={[0:1], [16:144], [0:256]} | slice | bytes 131072 | tf_op jit(solution)/shard_map/slice | solution.py:186
  13.8 0.1 maximum_select_fusion.5
  13.9 2.1 %collective-permute-start.1 = (bf16[8,20,256]{2,0,1:T(8,128)(2,1)S(1)}, bf16[8,20,256]{2,0,1:T(8,128)(2,1)S(1)}, u32[]{:S(2)}, u32[]{:S(2)}) collective-permute-start(bf16[8,20,256]{2,0,1:T(8,128)(2,1)S(1)} %pad_maximum_fusion.7), channel_id=1, source_target_pairs={{4,0},{6,2},{0,4},{2,6},{12,8},{14,10},{8,12},{10,14},{5,1},{7,3},... | collective-permute-start | bytes 245768 | tf_op jit(solution)/shard_map/ppermute | solution.py:222
  16.0 2.6 %collective-permute-start.4 = (bf16[8,20,256]{2,0,1:T(8,128)(2,1)S(1)}, bf16[8,20,256]{2,0,1:T(8,128)(2,1)S(1)}, u32[]{:S(2)}, u32[]{:S(2)}) collective-permute-start(bf16[8,20,256]{2,0,1:T(8,128)(2,1)S(1)} %pad_maximum_fusion.7), channel_id=1, source_target_pairs={{8,0},{10,2},{12,4},{14,6},{0,8},{2,10},{4,12},{6,14},{9,1},{11,3}... | collective-permute-start | bytes 245768 | tf_op jit(solution)/shard_map/ppermute | solution.py:222
  18.7 0.3 concatenate.69
  18.9 6.3 %collective-permute-done.4 = bf16[8,20,256]{2,0,1:T(8,128)(2,1)S(1)} collective-permute-done((bf16[8,20,256]{2,0,1:T(8,128)(2,1)S(1)}, bf16[8,20,256]{2,0,1:T(8,128)(2,1)S(1)}, u32[]{:S(2)}, u32[]{:S(2)}) %collective-permute-start.4) | collective-permute-done | bytes 81952 | tf_op jit(solution)/shard_map/ppermute | solution.py:222
  25.2 1.5 %collective-permute-start.3 = (bf16[296,256]{1,0:T(8,128)(2,1)S(1)}, bf16[296,256]{1,0:T(8,128)(2,1)S(1)}, u32[]{:S(2)}, u32[]{:S(2)}) collective-permute-start(bf16[296,256]{1,0:T(8,128)(2,1)S(1)} %concatenate.69), channel_id=1, source_target_pairs={{0,2},{2,0},{4,6},{6,4},{8,10},{10,8},{12,14},{14,12},{1,3},{3,1},... | collective-permute-start | bytes 454664 | tf_op jit(solution)/shard_map/ppermute | solution.py:213
  27.5 2.9 %collective-permute-done.3 = bf16[296,256]{1,0:T(8,128)(2,1)S(1)} collective-permute-done((bf16[296,256]{1,0:T(8,128)(2,1)S(1)}, bf16[296,256]{1,0:T(8,128)(2,1)S(1)}, u32[]{:S(2)}, u32[]{:S(2)}) %collective-permute-start.3) | collective-permute-done | bytes 151584 | tf_op jit(solution)/shard_map/ppermute | solution.py:213
  30.5 0.1 fusion.11
  30.5 0.6 %slice_convert_fusion.starts_ref = s32[6,256]{1,0:T(8,128)} fusion(bf16[296,256]{1,0:T(8,128)(2,1)S(1)} %collective-permute-done.3), kind=kLoop, calls=%fused_computation.67 | loop fusion | flops 1536 | bytes 9216 | tf_op jit(solution)/shard_map/convert_element_type | solution.py:218
  31.2 0.6 %slice.160 = bf16[192,256]{1,0:T(8,128)(2,1)} slice(bf16[296,256]{1,0:T(8,128)(2,1)S(1)} %collective-permute-done.3), slice={[0:192], [0:256]} | slice | bytes 196608 | tf_op jit(solution)/shard_map/slice | solution.py:216
  31.8 2.1 %shard_map.56.refs_9_ = bf16[2,3,256,256]{3,2,1,0:T(8,128)(2,1)} custom-call(bf16[2,3,32,256]{3,2,1,0:T(8,128)(2,1)} %bitcast.177, s32[6,256]{1,0:T(8,128)} %slice_convert_fusion.starts_ref), custom_call_target="tpu_custom_call" | custom-call | flops 3145728 | bytes 786432 | tf_op jit(solution)/shard_map/pallas_call | solution.py:39
  34.0 1.1 %copy-done.1 = bf16[2,3,256,256]{3,2,1,0:T(8,128)(2,1)S(1)} copy-done((bf16[2,3,256,256]{3,2,1,0:T(8,128)(2,1)S(1)}, bf16[2,3,256,256]{3,2,1,0:T(8,128)(2,1)}, u32[]{:S(2)}) %copy-start.1) | copy-done | bytes 786456
  35.1 1.7 %shard_map.57 = (f32[8,16,256]{2,1,0:T(8,128)S(1)}, f32[8,16,256]{2,1,0:T(8,128)S(1)}) custom-call(s32[2]{0:T(128)S(1)} %get-tuple-element.13.flags_ref, bf16[3,288,256]{2,1,0:T(8,128)(2,1)S(1)} %pad_maximum_fusion.source_ref, bf16[2,256,256]{2,1,0:T(8,128)(2,1)S(1)} %bitcast.161, bf16[2,2,16,256]{3,2,1,0:T(8,128)(2,1)S(1)} %get-tuple-element.64.refs_1_, ...), custom_call_target="tpu_custom_call" | custom-call | flops 905969664 | bytes 294912 | tf_op jit(solution)/shard_map/pallas_call | solution.py:114
  36.9 1.7 %shard_map.58 = (f32[8,16,256]{2,1,0:T(8,128)S(1)}, f32[8,16,256]{2,1,0:T(8,128)S(1)}) custom-call(s32[2]{0:T(128)S(1)} %get-tuple-element.13.flags_ref, bf16[3,288,256]{2,1,0:T(8,128)(2,1)S(1)} %pad_maximum_fusion.1.source_ref, bf16[2,256,256]{2,1,0:T(8,128)(2,1)S(1)} %bitcast.160, bf16[2,2,16,256]{3,2,1,0:T(8,128)(2,1)S(1)} %get-tuple-element.63.refs_1_, ...), custom_call_target="tpu_custom_call" | custom-call | flops 905969664 | bytes 294912 | tf_op jit(solution)/shard_map/pallas_call | solution.py:114
  38.6 3.1 %collective-permute-start.8 = (f32[8,16,256]{2,1,0:T(8,128)S(1)}, f32[8,16,256]{2,1,0:T(8,128)S(1)}, u32[]{:S(2)}, u32[]{:S(2)}) collective-permute-start(f32[8,16,256]{2,1,0:T(8,128)S(1)} %get-tuple-element.11), channel_id=1, source_target_pairs={{0,8},{2,10},{4,12},{6,14},{8,0},{10,2},{12,4},{14,6},{1,9},{3,11}... | collective-permute-start | bytes 393224 | tf_op jit(solution)/shard_map/ppermute | solution.py:275
  41.6 1.4 %collective-permute-start.7 = (f32[8,16,256]{2,1,0:T(8,128)S(1)}, f32[8,16,256]{2,1,0:T(8,128)S(1)}, u32[]{:S(2)}, u32[]{:S(2)}) collective-permute-start(f32[8,16,256]{2,1,0:T(8,128)S(1)} %get-tuple-element.10), channel_id=1, source_target_pairs={{0,12},{2,14},{4,8},{6,10},{8,4},{10,6},{12,0},{14,2},{1,13},{3,15... | collective-permute-start | bytes 393224 | tf_op jit(solution)/shard_map/ppermute | solution.py:275
  43.0 1.6 %collective-permute-done.8 = f32[8,16,256]{2,1,0:T(8,128)S(1)} collective-permute-done((f32[8,16,256]{2,1,0:T(8,128)S(1)}, f32[8,16,256]{2,1,0:T(8,128)S(1)}, u32[]{:S(2)}, u32[]{:S(2)}) %collective-permute-start.8) | collective-permute-done | bytes 131104 | tf_op jit(solution)/shard_map/ppermute | solution.py:275
  44.6 3.9 %collective-permute-done.7 = f32[8,16,256]{2,1,0:T(8,128)S(1)} collective-permute-done((f32[8,16,256]{2,1,0:T(8,128)S(1)}, f32[8,16,256]{2,1,0:T(8,128)S(1)}, u32[]{:S(2)}, u32[]{:S(2)}) %collective-permute-start.7) | collective-permute-done | bytes 131104 | tf_op jit(solution)/shard_map/ppermute | solution.py:275
  48.5 0.7 %add_add_fusion = f32[8,16,256]{2,1,0:T(8,128)} fusion(f32[8,16,256]{2,1,0:T(8,128)S(1)} %collective-permute-done.9, f32[8,16,256]{2,1,0:T(8,128)S(1)} %collective-permute-done.8, f32[8,16,256]{2,1,0:T(8,128)S(1)} %get-tuple-element.9, f32[8,16,256]{2,1,0:T(8,128)S(1)} %collective-permute-done.7), kind=kLoop, calls=%fused_computation.30 | loop fusion | flops 98304 | bytes 655360 | tf_op jit(solution)/shard_map/add | solution.py:275
  (69 shorter events, 1.1 us)
Async XLA Ops:
  0.0 4.2 %copy-start.3 = (s32[2,64,16,256]{3,2,1,0:T(8,128)S(1)}, s32[2,64,16,256]{3,2,1,0:T(8,128)}, u32[]{:S(2)}) copy-start(s32[2,64,16,256]{3,2,1,0:T(8,128)} %param.6) | copy-start | bytes 6291460
  0.0 3.6 %copy-start.5 = (bf16[8,16,256]{2,1,0:T(8,128)(2,1)S(1)}, bf16[8,16,256]{2,1,0:T(8,128)(2,1)}, u32[]{:S(2)}) copy-start(bf16[8,16,256]{2,1,0:T(8,128)(2,1)} %param.5) | copy-start | bytes 196612
  3.7 7.8 %collective-permute-start = (bf16[146,256]{1,0:T(8,128)(2,1)S(1)}, bf16[146,256]{1,0:T(8,128)(2,1)}, u32[]{:S(2)}, u32[]{:S(2)}) collective-permute-start(bf16[146,256]{1,0:T(8,128)(2,1)S(1)} %maximum_select_fusion), channel_id=1, source_target_pairs={{0,1},{1,0},{2,3},{3,2},{4,5},{5,4},{6,7},{7,6},{8,9},{9,8},{10,11... | collective-permute-start | bytes 224264 | tf_op jit(solution)/shard_map/ppermute | solution.py:164
  4.2 4.4 %copy-start.7 = (s32[2,3,256]{2,0,1:T(2,128)S(1)}, s32[2,3,256]{2,0,1:T(2,128)}, u32[]{:S(2)}) copy-start(s32[2,3,256]{2,0,1:T(2,128)} %param.9) | copy-start | bytes 18436
  4.5 14.1 %copy-start.2 = (bf16[2,16,256]{2,1,0:T(8,128)(2,1)S(1)}, bf16[2,16,256]{2,1,0:T(8,128)(2,1)}, u32[]{:S(2)}) copy-start(bf16[2,16,256]{2,1,0:T(8,128)(2,1)} %refs_2_.3) | copy-start | bytes 49156
  4.5 14.1 %copy-start.4 = (bf16[2,3,256,32]{2,3,1,0:T(8,128)(2,1)S(1)}, bf16[2,3,256,32]{2,3,1,0:T(8,128)(2,1)}, u32[]{:S(2)}) copy-start(bf16[2,3,256,32]{2,3,1,0:T(8,128)(2,1)} %param.8) | copy-start | bytes 294916
  5.3 28.7 %collective-permute-start.2 = (bf16[2,2,8,16,256]{4,3,2,1,0:T(8,128)(2,1)}, bf16[2,2,8,16,256]{4,3,2,1,0:T(8,128)(2,1)S(1)}, u32[]{:S(2)}, u32[]{:S(2)}) collective-permute-start(bf16[2,2,8,16,256]{4,3,2,1,0:T(8,128)(2,1)} %pad_maximum_fusion.3), channel_id=1, source_target_pairs={{0,2},{2,0},{4,6},{6,4},{8,10},{10,8},{12,14},{14,12},{1,3},{3,1},... | collective-permute-start | bytes 786440 | tf_op jit(solution)/shard_map/ppermute | solution.py:205
  8.6 28.2 %collective-permute-start.6 = (bf16[2,2,8,16,256]{4,3,2,1,0:T(8,128)(2,1)}, bf16[2,2,8,16,256]{4,3,2,1,0:T(8,128)(2,1)S(1)}, u32[]{:S(2)}, u32[]{:S(2)}) collective-permute-start(bf16[2,2,8,16,256]{4,3,2,1,0:T(8,128)(2,1)} %pad_maximum_fusion.5), channel_id=1, source_target_pairs={{0,2},{2,0},{4,6},{6,4},{8,10},{10,8},{12,14},{14,12},{1,3},{3,1},... | collective-permute-start | bytes 786440 | tf_op jit(solution)/shard_map/ppermute | solution.py:205
  8.7 0.6 %copy-start.6 = (s32[6,256]{1,0:T(8,128)}, s32[6,256]{1,0:T(8,128)S(1)}, u32[]{:S(2)}) copy-start(s32[6,256]{1,0:T(8,128)S(1)} %reshape.124.starts_ref) | copy-start | bytes 18436
  13.9 13.0 %collective-permute-start.1 = (bf16[8,20,256]{2,0,1:T(8,128)(2,1)S(1)}, bf16[8,20,256]{2,0,1:T(8,128)(2,1)S(1)}, u32[]{:S(2)}, u32[]{:S(2)}) collective-permute-start(bf16[8,20,256]{2,0,1:T(8,128)(2,1)S(1)} %pad_maximum_fusion.7), channel_id=1, source_target_pairs={{4,0},{6,2},{0,4},{2,6},{12,8},{14,10},{8,12},{10,14},{5,1},{7,3},... | collective-permute-start | bytes 245768 | tf_op jit(solution)/shard_map/ppermute | solution.py:222
  16.0 9.2 %collective-permute-start.4 = (bf16[8,20,256]{2,0,1:T(8,128)(2,1)S(1)}, bf16[8,20,256]{2,0,1:T(8,128)(2,1)S(1)}, u32[]{:S(2)}, u32[]{:S(2)}) collective-permute-start(bf16[8,20,256]{2,0,1:T(8,128)(2,1)S(1)} %pad_maximum_fusion.7), channel_id=1, source_target_pairs={{8,0},{10,2},{12,4},{14,6},{0,8},{2,10},{4,12},{6,14},{9,1},{11,3}... | collective-permute-start | bytes 245768 | tf_op jit(solution)/shard_map/ppermute | solution.py:222
  18.6 8.2 %collective-permute-start.5 = (bf16[8,20,256]{2,0,1:T(8,128)(2,1)S(1)}, bf16[8,20,256]{2,0,1:T(8,128)(2,1)S(1)}, u32[]{:S(2)}, u32[]{:S(2)}) collective-permute-start(bf16[8,20,256]{2,0,1:T(8,128)(2,1)S(1)} %pad_maximum_fusion.7), channel_id=1, source_target_pairs={{12,0},{14,2},{8,4},{10,6},{4,8},{6,10},{0,12},{2,14},{13,1},{15,3... | collective-permute-start | bytes 245768 | tf_op jit(solution)/shard_map/ppermute | solution.py:222
  25.2 5.2 %collective-permute-start.3 = (bf16[296,256]{1,0:T(8,128)(2,1)S(1)}, bf16[296,256]{1,0:T(8,128)(2,1)S(1)}, u32[]{:S(2)}, u32[]{:S(2)}) collective-permute-start(bf16[296,256]{1,0:T(8,128)(2,1)S(1)} %concatenate.69), channel_id=1, source_target_pairs={{0,2},{2,0},{4,6},{6,4},{8,10},{10,8},{12,14},{14,12},{1,3},{3,1},... | collective-permute-start | bytes 454664 | tf_op jit(solution)/shard_map/ppermute | solution.py:213
  27.3 6.7 %copy-start = (bf16[2,3,256,256]{3,2,1,0:T(8,128)(2,1)S(1)}, bf16[2,3,256,256]{3,2,1,0:T(8,128)(2,1)}, u32[]{:S(2)}) copy-start(bf16[2,3,256,256]{3,2,1,0:T(8,128)(2,1)} %shard_map.55.refs_4_) | copy-start | bytes 2359300
  34.0 1.1 %copy-start.1 = (bf16[2,3,256,256]{3,2,1,0:T(8,128)(2,1)S(1)}, bf16[2,3,256,256]{3,2,1,0:T(8,128)(2,1)}, u32[]{:S(2)}) copy-start(bf16[2,3,256,256]{3,2,1,0:T(8,128)(2,1)} %shard_map.56.refs_9_) | copy-start | bytes 2359300
  36.8 6.2 %collective-permute-start.9 = (f32[8,16,256]{2,1,0:T(8,128)S(1)}, f32[8,16,256]{2,1,0:T(8,128)S(1)}, u32[]{:S(2)}, u32[]{:S(2)}) collective-permute-start(f32[8,16,256]{2,1,0:T(8,128)S(1)} %get-tuple-element.12), channel_id=1, source_target_pairs={{0,4},{2,6},{4,0},{6,2},{8,12},{10,14},{12,8},{14,10},{1,5},{3,7},... | collective-permute-start | bytes 393224 | tf_op jit(solution)/shard_map/ppermute | solution.py:275
  38.6 6.0 %collective-permute-start.8 = (f32[8,16,256]{2,1,0:T(8,128)S(1)}, f32[8,16,256]{2,1,0:T(8,128)S(1)}, u32[]{:S(2)}, u32[]{:S(2)}) collective-permute-start(f32[8,16,256]{2,1,0:T(8,128)S(1)} %get-tuple-element.11), channel_id=1, source_target_pairs={{0,8},{2,10},{4,12},{6,14},{8,0},{10,2},{12,4},{14,6},{1,9},{3,11}... | collective-permute-start | bytes 393224 | tf_op jit(solution)/shard_map/ppermute | solution.py:275
  41.6 6.9 %collective-permute-start.7 = (f32[8,16,256]{2,1,0:T(8,128)S(1)}, f32[8,16,256]{2,1,0:T(8,128)S(1)}, u32[]{:S(2)}, u32[]{:S(2)}) collective-permute-start(f32[8,16,256]{2,1,0:T(8,128)S(1)} %get-tuple-element.10), channel_id=1, source_target_pairs={{0,12},{2,14},{4,8},{6,10},{8,4},{10,6},{12,0},{14,2},{1,13},{3,15... | collective-permute-start | bytes 393224 | tf_op jit(solution)/shard_map/ppermute | solution.py:275

commit v2 on v0

v2 whole, which is shorter than its diff:
```python
import functools

import jax
import jax.numpy as jnp
from jax import lax
from jax.experimental import pallas as pl
from jax.experimental.pallas import tpu as pltpu
from jax.sharding import PartitionSpec as P

VMEM = pl.BlockSpec(memory_space=pltpu.VMEM)
BF16, F32, I32 = jnp.bfloat16, jnp.float32, jnp.int32


def padded_16(rows):
    return -(-rows // 16) * 16


class Plan:
    def __init__(self, activity, histo_counts, blur_values):
        self.each, self.slices, self.width = activity.shape
        self.views, self.taps, _, self.band = blur_values.shape
        self.n_slab = lax.axis_size("slab")
        self.n_view = lax.axis_size("view")
        self.pairs = 2 if self.n_view % 2 == 0 else 1
        self.line = self.n_view // self.pairs
        self.block = self.each * self.slices
        self.n_edges = 2 if self.n_slab > 2 else 1
        halves = (range(self.line // 2, self.line), range(self.line // 2))
        self.halves = [h for h in halves if len(h)]
        self.edge_counts = 2 * self.each
        self.edge_back = self.edge_counts + self.views * self.n_view * self.each
        self.edge_rows = self.edge_back + padded_16(self.views)
        self.bands = self.views * self.taps * self.band
        self.starts = self.bands + self.views * self.slices
        self.param_rows = self.starts + padded_16(2 * self.views * self.taps)
        self.first_counts = self.param_rows
        self.first_edges = self.first_counts + self.views * len(self.halves[0]) * self.block
        self.edges_each = self.views * self.line * self.each
        self.first_back = self.first_edges + self.n_edges * self.edges_each
        self.first_rows = self.first_back + self.n_edges * padded_16(self.views)

    def peer(self, at, k):
        xor = self.line & (self.line - 1) == 0
        return at ^ k if xor else (at + k) % self.line

    def across(self, k, towards):
        g = self.pairs
        moves = [(i, self.peer(i // g, k) * g + i % g) for i in range(self.n_view)]
        return moves if towards else [(j, i) for i, j in moves]

    def valid(self):
        slab = lax.axis_index("slab")
        return (slab > 0, slab < self.n_slab - 1)


def call(kernel, outs, *args, scratch=(), flops=0, specs=None):
    size = lambda xs: sum(x.size * x.dtype.itemsize for x in xs)
    return pl.pallas_call(
        kernel,
        out_shape=outs,
        in_specs=specs or [VMEM] * len(args),
        out_specs=[VMEM] * len(outs),
        scratch_shapes=list(scratch),
        compiler_params=pltpu.CompilerParams(vmem_limit_bytes=24 * 1024 * 1024),
        cost_estimate=pl.CostEstimate(
            flops=flops, bytes_accessed=size(args) + size(outs), transcendentals=0
        ),
    )(*args)


def pack_kernel(p, counts_ref, activity_ref, back_ref, edges_ref, tiles_ref, active_ref, backs_ref, sems):
    slab = lax.axis_index("slab")
    last, tile = p.slices - 1, min(8, p.slices)
    copies = [
        pltpu.make_async_copy(activity_ref, active_ref, sems.at[0]),
        pltpu.make_async_copy(back_ref, backs_ref, sems.at[1]),
    ]
    for slot in range(p.n_edges):
        first = (slot == 0) if p.n_edges == 2 else (slab == 0)
        low = jnp.where(first, p.slices - tile, 0)
        copies.append(
            pltpu.make_async_copy(
                counts_ref.at[:, :, :, pl.ds(pl.multiple_of(low, tile), tile), :],
                tiles_ref.at[slot],
                sems.at[2 + slot],
            )
        )
    for copy in copies:
        copy.start()
    copies[0].wait()
    copies[1].wait()
    activity = active_ref[...].astype(F32)
    back = backs_ref[...].astype(F32)
    for slot in range(p.n_edges):
        copies[2 + slot].wait()

        def edge(high, low):
            if p.n_edges == 2:
                return high if slot == 0 else low
            return jnp.where(slab == 0, high, low)

        for j in range(2):
            edges_ref[slot, j * p.each : (j + 1) * p.each] = edge(
                activity[:, last - 1 + j, :], activity[:, j, :]
            )
        for v in range(p.views):
            for r in range(p.n_view):
                at = p.edge_counts + (v * p.n_view + r) * p.each
                edges_ref[slot, at : at + p.each] = edge(
                    tiles_ref[slot, v, r, :, tile - 1, :], tiles_ref[slot, v, r, :, 0, :]
                ).astype(F32)
            edges_ref[slot, p.edge_back + v : p.edge_back + v + 1] = edge(
                back[v, last : last + 1], back[v, 0:1]
            )
        tail = p.edge_rows - p.edge_back - p.views
        if tail:
            edges_ref[slot, p.edge_back + p.views :] = jnp.zeros((tail, p.width), F32)


def send_kernel(p, edges_ref, counts_ref, activity_ref, back_ref, values_ref, starts_ref, payload_ref, *outs):
    at = lax.axis_index("view")
    at_line, side = at // p.pairs, at % p.pairs
    payload_ref[: p.block] = activity_ref[...].reshape(p.block, p.width)
    for high, valid in enumerate(p.valid()):
        edge = edges_ref[min(high, p.n_edges - 1), : 2 * p.each]
        low = p.block + high * 2 * p.each
        payload_ref[low : low + 2 * p.each] = jnp.where(valid, edge, 0.0).astype(BF16)
    if p.pairs == 1:
        return
    (out,) = outs
    out[: p.bands] = values_ref[...].reshape(p.bands, p.width)
    out[p.bands : p.starts] = back_ref[...].reshape(p.views * p.slices, p.width)
    starts = starts_ref[...]
    pieces = [lax.shift_right_logical(starts, 7), starts & 127]
    tail = p.param_rows - p.starts - 2 * p.views * p.taps
    if tail:
        pieces.append(jnp.zeros((tail, p.width), I32))
    out[p.starts : p.param_rows] = jnp.concatenate(pieces, axis=0).astype(F32).astype(BF16)
    copy_counts(p, p.halves[0], counts_ref, out, p.first_counts)
    for e in range(p.n_edges):
        pieces = []
        for v in range(p.views):
            for k in range(p.line):
                row = p.peer(at_line, k) * 2 + (1 - side)
                start = p.edge_counts + (v * p.n_view + row) * p.each
                pieces.append(edges_ref[e, pl.ds(pl.multiple_of(start, p.each), p.each), :])
        low = p.first_edges + e * p.edges_each
        out[low : low + p.edges_each] = jnp.concatenate(pieces, axis=0).astype(BF16)
        low = p.first_back + e * padded_16(p.views)
        out[low : low + padded_16(p.views)] = edges_ref[
            e, p.edge_back : p.edge_back + padded_16(p.views)
        ].astype(BF16)


def copy_counts(p, ks, counts_ref, out, base):
    at = lax.axis_index("view")
    for v in range(p.views):
        for i, k in enumerate(ks):
            row = p.peer(at // p.pairs, k) * 2 + 1 - at % p.pairs
            low = base + (v * len(ks) + i) * p.block
            counts = counts_ref[v, row].astype(F32).astype(BF16)
            out[low : low + p.block] = counts.reshape(p.block, p.width)


def place_bands(values, start):
    width = values.shape[1]
    moved = jnp.concatenate([values, jnp.zeros((8, width), F32)], axis=0)
    for step in (1, 2, 4):
        moved = jnp.where((start & step) != 0, pltpu.roll(moved, step, 0), moved)
    step = 8
    while step < width:
        longer = min(moved.shape[0] + step, width)
        zeros = jnp.zeros((step, width), F32)
        down = jnp.concatenate([zeros, moved], axis=0)[:longer]
        stay = jnp.concatenate([moved, zeros], axis=0)[:longer]
        moved = jnp.where((start & step) != 0, down, stay)
        step *= 2
    return moved.astype(BF16)


def own_kernel(p, values_ref, starts_ref, counts_ref, *refs):
    blocks, outs, lifted_ref = refs[: p.line], refs[p.line : -1], refs[-1]
    matrix_ref, sources = outs[0], outs[1 : 1 + len(p.halves)]
    if p.pairs == 2:
        for ks, out in zip(p.halves[1:], outs[1 + len(p.halves) :]):
            copy_counts(p, ks, counts_ref, out, 0)
    for v in range(p.views):
        for t in range(p.taps):
            at = v * p.taps + t
            matrix_ref[v, t] = place_bands(
                values_ref[v, t].astype(F32), starts_ref[at : at + 1]
            )
    for ks, source_ref in zip(p.halves, sources):
        rows = len(ks) * p.each
        for i, k in enumerate(ks):
            low = i * p.each
            lifted_ref[low : low + p.each, 8 : 8 + p.slices, :] = (
                blocks[k][: p.block].astype(F32).reshape(p.each, p.slices, p.width)
            )
            edges = blocks[k][p.block :].astype(F32)
            for high in range(2):
                for j in range(2):
                    lifted_ref[low : low + p.each, (8 + p.slices if high else 6) + j, :] = edges[
                        (2 * high + j) * p.each : (2 * high + j + 1) * p.each
                    ]
        main = rows * p.slices
        for t in range(p.taps):
            source_ref[t, :main] = (
                lifted_ref[:rows, 7 + t : 7 + t + p.slices, :].astype(BF16).reshape(main, p.width)
            )
            source_ref[t, main:] = jnp.concatenate(
                [lifted_ref[:rows, 6 + t, :], lifted_ref[:rows, 7 + p.slices + t, :]], axis=0
            ).astype(BF16)


def their_kernel(p, params_ref, matrix_ref):
    starts = params_ref[p.starts : p.param_rows].astype(F32).astype(I32)
    n = p.views * p.taps
    starts = starts[:n] * 128 + starts[n : 2 * n]
    for v in range(p.views):
        for t in range(p.taps):
            at = v * p.taps + t
            values = params_ref[at * p.band : (at + 1) * p.band].astype(F32)
            matrix_ref[v, t] = place_bands(values, starts[at : at + 1])


def rows_kernel(p, half, source_ref, counts_ref, edges_ref, back_ref, matrix_ref, *refs):
    ks = p.halves[half]
    if p.pairs == 2:
        (their_ref, first_ref, their_matrix_ref), refs = refs[:3], refs[3:]
        base = p.first_counts if half == 0 else 0
    outs, (ratio_ref, up_ref, down_ref) = refs[: len(ks)], refs[len(ks) :]
    at = lax.axis_index("view")
    at_line, side = at // p.pairs, at % p.pairs
    rows = len(ks) * p.each
    main, full = rows * p.slices, rows * (p.slices + 2)
    views = []

    def view(matrix_ref, v, counts, back, edges, edge_backs):
        expected = None
        for t in range(p.taps):
            term = jnp.dot(source_ref[t], matrix_ref[v, t], preferred_element_type=F32)
            expected = term if expected is None else expected + term
        inner = expected[:main].reshape(rows, p.slices, p.width) + back[None]
        ratio = counts / inner - 1.0
        n = len(views)
        ratio_ref[n, :main] = ratio.astype(BF16).reshape(main, p.width)
        for high, valid in enumerate(p.valid()):
            low = main + high * rows
            e = min(high, p.n_edges - 1)
            ratio = edges[e] / (expected[low : low + rows] + edge_backs[e]) - 1.0
            ratio_ref[n, low : low + rows] = jnp.where(valid, ratio, 0.0).astype(BF16)
        views.append((matrix_ref, v))

    for v in range(p.views):
        counts, edges, edge_backs = [], [], []
        for k in ks:
            counts.append(counts_ref[v, p.peer(at_line, k) * p.pairs + side])
        for e in range(p.n_edges):
            pieces = []
            for k in ks:
                row = p.peer(at_line, k) * p.pairs + side
                start = p.edge_counts + (v * p.n_view + row) * p.each
                pieces.append(edges_ref[e, pl.ds(pl.multiple_of(start, p.each), p.each), :])
            edges.append(jnp.concatenate(pieces, axis=0))
            edge_backs.append(edges_ref[e, p.edge_back + v : p.edge_back + v + 1])
        counts = jnp.concatenate(counts, axis=0).astype(F32)
        view(matrix_ref, v, counts, back_ref[v].astype(F32), edges, edge_backs)
    if p.pairs == 2:
        for v in range(p.views):
            edges, edge_backs = [], []
            for e in range(p.n_edges):
                start = p.first_edges + e * p.edges_each + (v * p.line + ks[0]) * p.each
                edges.append(first_ref[start : start + rows].astype(F32))
                start = p.first_back + e * padded_16(p.views)
                backs = first_ref[start : start + padded_16(p.views)].astype(F32)
                edge_backs.append(backs[v : v + 1])
            counts = their_ref[base + v * main : base + (v + 1) * main].astype(F32)
            back = first_ref[p.bands + v * p.slices : p.bands + (v + 1) * p.slices].astype(F32)
            view(
                their_matrix_ref,
                v,
                counts.reshape(rows, p.slices, p.width),
                back,
                edges,
                edge_backs,
            )

    def project(tap, stop):
        total = None
        for n, (matrix_ref, v) in enumerate(views):
            term = lax.dot_general(
                ratio_ref[n, :stop],
                matrix_ref[v, tap],
                (((1,), (1,)), ((), ())),
                preferred_element_type=F32,
            )
            total = term if total is None else total + term
        return total

    part = project(0, full)
    up_ref[:, : p.slices, :] = part[:main].reshape(rows, p.slices, p.width)
    up_ref[:, p.slices, :] = part[main + rows :]
    part = project(2, main + rows)
    down_ref[:, 8 : 8 + p.slices, :] = part[:main].reshape(rows, p.slices, p.width)
    down_ref[:, 7, :] = part[main:]
    total = project(1, main).reshape(rows, p.slices, p.width)
    total = total + up_ref[:, 1 : 1 + p.slices, :] + down_ref[:, 7 : 7 + p.slices, :]
    for i, out in enumerate(outs):
        out[...] = total[i * p.each : (i + 1) * p.each]


def per_device(activity, histo_counts, background, blur_values, band_start):
    p = Plan(activity, histo_counts, blur_values)
    shape = jax.ShapeDtypeStruct
    part = lambda kernel, *static: functools.partial(kernel, p, *static)
    width = p.width
    counts = histo_counts.reshape(p.views, p.n_view, p.each, p.slices, width)
    values = jnp.swapaxes(blur_values, 2, 3)
    starts = band_start.reshape(p.views * p.taps, width)
    other = [(i, i ^ 1) for i in range(p.n_view)]

    edges = call(
        part(pack_kernel),
        [shape((p.n_edges, p.edge_rows, width), F32)],
        counts, activity, background,
        specs=[pl.BlockSpec(memory_space=pl.ANY)] * 3,
        scratch=[
            pltpu.VMEM((p.n_edges, p.views, p.n_view, p.each, min(8, p.slices), width), I32),
            pltpu.VMEM(activity.shape, BF16),
            pltpu.VMEM(background.shape, BF16),
            pltpu.SemaphoreType.DMA((2 + p.n_edges,)),
        ],
    )[0]
    if p.n_slab == 2:
        edges = lax.ppermute(edges, "slab", [(0, 1), (1, 0)])
    elif p.n_slab > 2:
        up = [(i, i + 1) for i in range(p.n_slab - 1)]
        down = [(j, i) for i, j in up]
        edges = jnp.stack([lax.ppermute(edges[0], "slab", up), lax.ppermute(edges[1], "slab", down)])
    outs = [shape((p.block + 4 * p.each, width), BF16)]
    if p.pairs == 2:
        outs.append(shape((p.first_rows, width), BF16))
    payload, *sent = call(
        part(send_kernel), outs, edges, counts, activity, background, values, starts
    )
    theirs = [lax.ppermute(x, "view", other) for x in sent]
    blocks = [payload] + [lax.ppermute(payload, "view", p.across(k, False)) for k in range(1, p.line)]

    matrices = shape((p.views, p.taps, width, width), BF16)
    most = max(len(h) for h in p.halves) * p.each
    outs = [matrices]
    outs += [shape((p.taps, len(h) * p.each * (p.slices + 2), width), BF16) for h in p.halves]
    if p.pairs == 2:
        outs += [shape((p.views * len(h) * p.block, width), BF16) for h in p.halves[1:]]
    matrix, *outs = call(
        part(own_kernel), outs, values, starts, counts, *blocks,
        scratch=[pltpu.VMEM((most, p.slices + 16, width), F32)],
    )
    sources, later = outs[: len(p.halves)], outs[len(p.halves) :]
    theirs += [lax.ppermute(x, "view", other) for x in later]
    if p.pairs == 2:
        (their_matrix,) = call(part(their_kernel), [matrices], theirs[0])

    terms = {}
    for half, ks in enumerate(p.halves):
        args = [sources[half], counts, edges, background, matrix]
        if p.pairs == 2:
            args += [theirs[half], theirs[0], their_matrix]
        rows = len(ks) * p.each
        full = rows * (p.slices + 2)
        n_views = p.views * p.pairs
        outs = call(
            part(rows_kernel, half),
            [shape((p.each, p.slices, width), F32)] * len(ks),
            *args,
            scratch=[
                pltpu.VMEM((n_views, full, width), BF16),
                pltpu.VMEM((rows, p.slices + 8, width), F32),
                pltpu.VMEM((rows, p.slices + 8, width), F32),
            ],
            flops=4 * n_views * p.taps * full * width * width,
        )
        terms.update(zip(ks, outs))
    total = terms[0]
    for k in reversed(range(1, p.line)):
        total = total + lax.ppermute(terms[k], "view", p.across(k, True))
    return total


def solution(mesh):
    placed = (
        P(("parts", "view"), "slab", None),
        P(("parts", "view"), None, "slab", None),
        P(("parts", "view"), "slab", None),
        P("view", None, None, None),
        P("view", None, None),
    )
    return jax.shard_map(
        per_device,
        mesh=mesh,
        in_specs=placed,
        out_specs=P(("parts", "view"), "slab", None),
        check_vma=False,
    )
```

time: 153 us -> 36.4 us (0.24)
  waiting for transfers between devices: 65.1 us -> 14.6 us
  blocking collectives: 33.7 us -> 0 us
  matrix products: 14.6 us -> 0 us
  between operations: 13.7 us -> 0.07 us
  local copies, waits for them, and re-layouts: 8.05 us -> 3.18 us
  Pallas kernels: 0 us -> 3.73 us
  other arithmetic: 4 us -> 0.7 us
    reduce_scatter x1 -> x0, waiting for transfers between devices: 65.1 us -> none  [per_device(): lax.psum_scatter(gathered_sum, 'view', scatter_dimension=0, tiled=True)]
    all_gather x1 -> x0, blocking collectives: 33.7 us -> none  [per_device(): gathered = lax.all_gather(source, 'view', axis=0, tiled=True)]
    dot_general x18 -> x0, matrix products: 14.6 us -> none  [the longest x6 9.59 us: blur_matrix(): jnp.einsum('ik,ijk->ij', band_values.astype(jnp.float32), selector)]
    ppermute x6 -> x9, waiting for transfers between devices: 0.02 us -> 14.6 us  [the longest x3 6.4 us: per_device(): lax.ppermute(payload, 'view', p.across(k, False))]
    squeeze x7 -> x0, local copies, waits for them, and re-layouts: 4.68 us -> none  [per_device(): blur_values[view_index, tap_index]]
    pallas_call x0 -> x6, Pallas kernels: none -> 3.73 us  [call(): pl.pallas_call(kernel, out_shape=outs, in_specs=specs or [VMEM] * len(arg...]
    convert_element_type x2 -> x0, other arithmetic: 2.38 us -> none  [the longest x1 1.79 us: per_device(): histo_counts[view_index].astype(jnp.float32) / expected - 1.0]
    ppermute x6 -> x9, starting transfers between devices: 13.1 us -> 13.9 us  [the longest x3 5.48 us: per_device(): total = total + lax.ppermute(terms[k], 'view', p.across(k, True))]
  transfers between devices with their start and end apart: 7 -> 9, of which waited for: 1 -> 6; matrix products, arithmetic and copies ran while one was open for 12% -> 0% of each run, Pallas kernels for 0% -> 9%
where the time goes in v2:
time: 36.4 us; the launch traced here: 36.1 us
  waiting for transfers between devices  14.6 us (40%)
  starting transfers between devices  13.9 us (38%)
  Pallas kernels  3.73 us (10%)
  local copies, waits for them, and re-layouts  3.18 us (9%)
  other arithmetic  0.7 us (2%)
    ppermute x3, waiting for transfers between devices, per_device(): lax.ppermute(payload, 'view', p.across(k, False))  6.4 us
    ppermute x3, waiting for transfers between devices, per_device(): total = total + lax.ppermute(terms[k], 'view', p.across(k, True))  5.66 us
    ppermute x3, starting transfers between devices, per_device(): total = total + lax.ppermute(terms[k], 'view', p.across(k, True))  5.48 us
    ppermute x3, starting transfers between devices, per_device(): lax.ppermute(payload, 'view', p.across(k, False))  4.39 us
    pallas_call x6, Pallas kernels, call(): pl.pallas_call(kernel, out_shape=outs, in_specs=specs or [VMEM] * len(arg...  3.73 us
    unnamed x17, local copies, waits for them, and re-layouts  3.17 us
    ppermute x1, starting transfers between devices, per_device(): theirs = [lax.ppermute(x, 'view', other) for x in sent]  2.95 us
    ppermute x1, waiting for transfers between devices, per_device(): theirs += [lax.ppermute(x, 'view', other) for x in later]  1.47 us
  transfers between devices with their start and end apart: 9, of which 6 were waited for; matrix products, arithmetic and copies ran while one was open for 0% of the time, Pallas kernels for 9%

profile of v2, /device:TPU:0, one launch (start us, length us, event | category | flops | bytes accessed | tf_op | source)
XLA Modules:
  0.0 36.1 jit_solution(900312032026891056)
XLA Ops:
  0.0 1.6 %copy-done = s32[2,64,16,256]{3,2,1,0:T(8,128)S(1)} copy-done((s32[2,64,16,256]{3,2,1,0:T(8,128)S(1)}, s32[2,64,16,256]{3,2,1,0:T(8,128)}, u32[]{:S(2)}) %copy-start) | copy-done | bytes 2097176
  1.6 0.7 %copy-done.3 = bf16[2,16,256]{2,1,0:T(8,128)(2,1)S(1)} copy-done((bf16[2,16,256]{2,1,0:T(8,128)(2,1)S(1)}, bf16[2,16,256]{2,1,0:T(8,128)(2,1)}, u32[]{:S(2)}) %copy-start.3) | copy-done | bytes 16408
  2.3 0.8 %copy-done.5 = bf16[8,16,256]{2,1,0:T(8,128)(2,1)S(1)} copy-done((bf16[8,16,256]{2,1,0:T(8,128)(2,1)S(1)}, bf16[8,16,256]{2,1,0:T(8,128)(2,1)}, u32[]{:S(2)}) %copy-start.5) | copy-done | bytes 65560
  3.2 0.0 copy-start.6
  3.2 0.4 %shard_map.55 = f32[1,160,256]{2,1,0:T(8,128)S(1)} custom-call(s32[2,8,8,16,256]{4,3,2,1,0:T(8,128)S(1)} %bitcast.2, bf16[8,16,256]{2,1,0:T(8,128)(2,1)S(1)} %copy-done.5, bf16[2,16,256]{2,1,0:T(8,128)(2,1)S(1)} %copy-done.3), custom_call_target="tpu_custom_call" | custom-call | bytes 2342912 | tf_op jit(solution)/shard_map/pallas_call | solution.py:58
  3.6 0.5 %collective-permute-start = (f32[1,160,256]{2,1,0:T(8,128)S(1)}, f32[1,160,256]{2,1,0:T(8,128)S(1)}, u32[]{:S(2)}, u32[]{:S(2)}) collective-permute-start(f32[1,160,256]{2,1,0:T(8,128)S(1)} %shard_map.55), channel_id=1, source_target_pairs={{0,1},{1,0},{2,3},{3,2},{4,5},{5,4},{6,7},{7,6},{8,9},{9,8},{10,11... | collective-permute-start | bytes 491528 | tf_op jit(solution)/shard_map/ppermute | solution.py:336
  4.1 0.0 copy-done.7
  4.1 1.0 %collective-permute-done.edges_ref = f32[1,160,256]{2,1,0:T(8,128)S(1)} collective-permute-done((f32[1,160,256]{2,1,0:T(8,128)S(1)}, f32[1,160,256]{2,1,0:T(8,128)S(1)}, u32[]{:S(2)}, u32[]{:S(2)}) %collective-permute-start) | collective-permute-done | bytes 163872 | tf_op jit(solution)/shard_map/ppermute | solution.py:336
  5.1 0.0 copy-done.1
  5.1 0.0 copy-done.6
  5.1 0.1 shard_map.56
  5.2 3.0 %collective-permute-start.5 = (bf16[832,256]{1,0:T(8,128)(2,1)S(1)}, bf16[832,256]{1,0:T(8,128)(2,1)S(1)}, u32[]{:S(2)}, u32[]{:S(2)}) collective-permute-start(bf16[832,256]{1,0:T(8,128)(2,1)S(1)} %get-tuple-element.19), channel_id=1, source_target_pairs={{0,2},{2,0},{4,6},{6,4},{8,10},{10,8},{12,14},{14,12},{1,3},{3,1},... | collective-permute-start | bytes 1277960 | tf_op jit(solution)/shard_map/ppermute | solution.py:347
  8.1 1.6 %collective-permute-start.1 = (bf16[160,256]{1,0:T(8,128)(2,1)S(1)}, bf16[160,256]{1,0:T(8,128)(2,1)S(1)}, u32[]{:S(2)}, u32[]{:S(2)}) collective-permute-start(bf16[160,256]{1,0:T(8,128)(2,1)S(1)} %get-tuple-element.15.refs_0_), channel_id=1, source_target_pairs={{4,0},{6,2},{0,4},{2,6},{12,8},{14,10},{8,12},{10,14},{5,1},{7,3},... | collective-permute-start | bytes 245768 | tf_op jit(solution)/shard_map/ppermute | solution.py:348
  9.7 2.6 %collective-permute-start.2 = (bf16[160,256]{1,0:T(8,128)(2,1)S(1)}, bf16[160,256]{1,0:T(8,128)(2,1)S(1)}, u32[]{:S(2)}, u32[]{:S(2)}) collective-permute-start(bf16[160,256]{1,0:T(8,128)(2,1)S(1)} %get-tuple-element.15.refs_0_), channel_id=1, source_target_pairs={{8,0},{10,2},{12,4},{14,6},{0,8},{2,10},{4,12},{6,14},{9,1},{11,3}... | collective-permute-start | bytes 245768 | tf_op jit(solution)/shard_map/ppermute | solution.py:348
  12.3 0.2 collective-permute-start.3
  12.5 0.1 collective-permute-done.1.refs_1_
  12.6 6.3 %collective-permute-done.2.refs_2_ = bf16[160,256]{1,0:T(8,128)(2,1)S(1)} collective-permute-done((bf16[160,256]{1,0:T(8,128)(2,1)S(1)}, bf16[160,256]{1,0:T(8,128)(2,1)S(1)}, u32[]{:S(2)}, u32[]{:S(2)}) %collective-permute-start.2) | collective-permute-done | bytes 81952 | tf_op jit(solution)/shard_map/ppermute | solution.py:348
  18.9 0.0 collective-permute-done.3.refs_3_
  18.9 0.7 %shard_map.57 = (bf16[2,3,256,256]{3,2,1,0:T(8,128)(2,1)S(1)}, bf16[3,288,256]{2,1,0:T(8,128)(2,1)S(1)}, bf16[3,288,256]{2,1,0:T(8,128)(2,1)S(1)}, bf16[512,256]{1,0:T(8,128)(2,1)S(1)}) custom-call(bf16[2,3,32,256]{3,2,1,0:T(8,128)(2,1)S(1)} %bitcast.8, s32[6,256]{1,0:T(8,128)S(1)} %reshape.6.starts_ref, s32[2,8,8,16,256]{4,3,2,1,0:T(8,128)S(1)} %bitcast.4, ...), custom_call_target="tpu_custom_call" | custom-call | bytes 4462592 | tf_op jit(solution)/shard_map/pallas_call | solution.py:58
  19.7 0.6 %collective-permute-start.4 = (bf16[512,256]{1,0:T(8,128)(2,1)S(1)}, bf16[512,256]{1,0:T(8,128)(2,1)S(1)}, u32[]{:S(2)}, u32[]{:S(2)}) collective-permute-start(bf16[512,256]{1,0:T(8,128)(2,1)S(1)} %get-tuple-element.18), channel_id=1, source_target_pairs={{0,2},{2,0},{4,6},{6,4},{8,10},{10,8},{12,14},{14,12},{1,3},{3,1},... | collective-permute-start | bytes 786440 | tf_op jit(solution)/shard_map/ppermute | solution.py:361
  20.2 0.0 collective-permute-done.5.params_ref.refs_1_.refs_0_
  20.2 0.3 shard_map.58.refs_2_
  20.5 1.1 %shard_map.60 = (f32[8,16,256]{2,1,0:T(8,128)S(1)}, f32[8,16,256]{2,1,0:T(8,128)S(1)}) custom-call(bf16[3,288,256]{2,1,0:T(8,128)(2,1)S(1)} %get-tuple-element.21.source_ref, s32[2,8,8,16,256]{4,3,2,1,0:T(8,128)S(1)} %bitcast.5, f32[1,160,256]{2,1,0:T(8,128)S(1)} %collective-permute-done.edges_ref, bf16[2,16,256]{2,1,0:T(8,128)(2,1)S(1)} %copy-done.4, ...), custom_call_target="tpu_custom_call" | custom-call | flops 905969664 | bytes 5406720 | tf_op jit(solution)/shard_map/pallas_call | solution.py:58
  21.7 2.5 %collective-permute-start.6 = (f32[8,16,256]{2,1,0:T(8,128)S(1)}, f32[8,16,256]{2,1,0:T(8,128)S(1)}, u32[]{:S(2)}, u32[]{:S(2)}) collective-permute-start(f32[8,16,256]{2,1,0:T(8,128)S(1)} %get-tuple-element.22), channel_id=1, source_target_pairs={{0,12},{2,14},{4,8},{6,10},{8,4},{10,6},{12,0},{14,2},{1,13},{3,15... | collective-permute-start | bytes 393224 | tf_op jit(solution)/shard_map/ppermute | solution.py:387
  24.2 0.4 %collective-permute-start.7 = (f32[8,16,256]{2,1,0:T(8,128)S(1)}, f32[8,16,256]{2,1,0:T(8,128)S(1)}, u32[]{:S(2)}, u32[]{:S(2)}) collective-permute-start(f32[8,16,256]{2,1,0:T(8,128)S(1)} %get-tuple-element.23), channel_id=1, source_target_pairs={{0,8},{2,10},{4,12},{6,14},{8,0},{10,2},{12,4},{14,6},{1,9},{3,11}... | collective-permute-start | bytes 393224 | tf_op jit(solution)/shard_map/ppermute | solution.py:387
  24.6 1.5 %collective-permute-done.4.refs_0_ = bf16[512,256]{1,0:T(8,128)(2,1)S(1)} collective-permute-done((bf16[512,256]{1,0:T(8,128)(2,1)S(1)}, bf16[512,256]{1,0:T(8,128)(2,1)S(1)}, u32[]{:S(2)}, u32[]{:S(2)}) %collective-permute-start.4) | collective-permute-done | bytes 262176 | tf_op jit(solution)/shard_map/ppermute | solution.py:361
  26.1 1.2 %shard_map.59 = (f32[8,16,256]{2,1,0:T(8,128)S(1)}, f32[8,16,256]{2,1,0:T(8,128)S(1)}) custom-call(bf16[3,288,256]{2,1,0:T(8,128)(2,1)S(1)} %get-tuple-element.16.source_ref, s32[2,8,8,16,256]{4,3,2,1,0:T(8,128)S(1)} %bitcast.6, f32[1,160,256]{2,1,0:T(8,128)S(1)} %collective-permute-done.edges_ref, bf16[2,16,256]{2,1,0:T(8,128)(2,1)S(1)} %copy-done.4, ...), custom_call_target="tpu_custom_call" | custom-call | flops 905969664 | bytes 5242880 | tf_op jit(solution)/shard_map/pallas_call | solution.py:58
  27.3 2.5 %collective-permute-start.8 = (f32[8,16,256]{2,1,0:T(8,128)S(1)}, f32[8,16,256]{2,1,0:T(8,128)S(1)}, u32[]{:S(2)}, u32[]{:S(2)}) collective-permute-start(f32[8,16,256]{2,1,0:T(8,128)S(1)} %get-tuple-element.24), channel_id=1, source_target_pairs={{0,4},{2,6},{4,0},{6,2},{8,12},{10,14},{12,8},{14,10},{1,5},{3,7},... | collective-permute-start | bytes 393224 | tf_op jit(solution)/shard_map/ppermute | solution.py:387
  29.8 0.0 collective-permute-done.6
  29.8 5.3 %collective-permute-done.7 = f32[8,16,256]{2,1,0:T(8,128)S(1)} collective-permute-done((f32[8,16,256]{2,1,0:T(8,128)S(1)}, f32[8,16,256]{2,1,0:T(8,128)S(1)}, u32[]{:S(2)}, u32[]{:S(2)}) %collective-permute-start.7) | collective-permute-done | bytes 131104 | tf_op jit(solution)/shard_map/ppermute | solution.py:387
  35.1 0.3 collective-permute-done.8
  35.4 0.7 %add_add_fusion = f32[8,16,256]{2,1,0:T(8,128)} fusion(f32[8,16,256]{2,1,0:T(8,128)S(1)} %collective-permute-done.8, f32[8,16,256]{2,1,0:T(8,128)S(1)} %collective-permute-done.7, f32[8,16,256]{2,1,0:T(8,128)S(1)} %get-tuple-element.20, f32[8,16,256]{2,1,0:T(8,128)S(1)} %collective-permute-done.6), kind=kLoop, calls=%fused_computation | loop fusion | flops 98304 | bytes 655360 | tf_op jit(solution)/shard_map/add | solution.py:387
  (11 shorter events, 0.0 us)
Async XLA Ops:
  0.0 1.6 %copy-start = (s32[2,64,16,256]{3,2,1,0:T(8,128)S(1)}, s32[2,64,16,256]{3,2,1,0:T(8,128)}, u32[]{:S(2)}) copy-start(s32[2,64,16,256]{3,2,1,0:T(8,128)} %param.6) | copy-start | bytes 6291460
  1.6 0.7 %copy-start.3 = (bf16[2,16,256]{2,1,0:T(8,128)(2,1)S(1)}, bf16[2,16,256]{2,1,0:T(8,128)(2,1)}, u32[]{:S(2)}) copy-start(bf16[2,16,256]{2,1,0:T(8,128)(2,1)} %back_ref.7) | copy-start | bytes 49156
  2.3 0.8 %copy-start.5 = (bf16[8,16,256]{2,1,0:T(8,128)(2,1)S(1)}, bf16[8,16,256]{2,1,0:T(8,128)(2,1)}, u32[]{:S(2)}) copy-start(bf16[8,16,256]{2,1,0:T(8,128)(2,1)} %activity_ref.3) | copy-start | bytes 196612
  3.1 0.9 %copy-start.7 = (s32[2,3,256]{2,0,1:T(2,128)S(1)}, s32[2,3,256]{2,0,1:T(2,128)}, u32[]{:S(2)}) copy-start(s32[2,3,256]{2,0,1:T(2,128)} %param.9) | copy-start | bytes 18436
  3.2 2.0 %copy-start.1 = (s32[2,64,16,256]{3,2,1,0:T(8,128)S(1)}, s32[2,64,16,256]{3,2,1,0:T(8,128)}, u32[]{:S(2)}) copy-start(s32[2,64,16,256]{3,2,1,0:T(8,128)} %param.6) | copy-start | bytes 6291460
  3.2 2.0 %copy-start.2 = (bf16[2,3,256,32]{2,3,1,0:T(8,128)(2,1)S(1)}, bf16[2,3,256,32]{2,3,1,0:T(8,128)(2,1)}, u32[]{:S(2)}) copy-start(bf16[2,3,256,32]{2,3,1,0:T(8,128)(2,1)} %param.8) | copy-start | bytes 294916
  3.2 2.0 %copy-start.4 = (bf16[2,16,256]{2,1,0:T(8,128)(2,1)S(1)}, bf16[2,16,256]{2,1,0:T(8,128)(2,1)}, u32[]{:S(2)}) copy-start(bf16[2,16,256]{2,1,0:T(8,128)(2,1)} %back_ref.7) | copy-start | bytes 49156
  3.2 2.0 %copy-start.6 = (bf16[8,16,256]{2,1,0:T(8,128)(2,1)S(1)}, bf16[8,16,256]{2,1,0:T(8,128)(2,1)}, u32[]{:S(2)}) copy-start(bf16[8,16,256]{2,1,0:T(8,128)(2,1)} %activity_ref.3) | copy-start | bytes 196612
  3.6 1.5 %collective-permute-start = (f32[1,160,256]{2,1,0:T(8,128)S(1)}, f32[1,160,256]{2,1,0:T(8,128)S(1)}, u32[]{:S(2)}, u32[]{:S(2)}) collective-permute-start(f32[1,160,256]{2,1,0:T(8,128)S(1)} %shard_map.55), channel_id=1, source_target_pairs={{0,1},{1,0},{2,3},{3,2},{4,5},{5,4},{6,7},{7,6},{8,9},{9,8},{10,11... | collective-permute-start | bytes 491528 | tf_op jit(solution)/shard_map/ppermute | solution.py:336
  5.2 15.0 %collective-permute-start.5 = (bf16[832,256]{1,0:T(8,128)(2,1)S(1)}, bf16[832,256]{1,0:T(8,128)(2,1)S(1)}, u32[]{:S(2)}, u32[]{:S(2)}) collective-permute-start(bf16[832,256]{1,0:T(8,128)(2,1)S(1)} %get-tuple-element.19), channel_id=1, source_target_pairs={{0,2},{2,0},{4,6},{6,4},{8,10},{10,8},{12,14},{14,12},{1,3},{3,1},... | collective-permute-start | bytes 1277960 | tf_op jit(solution)/shard_map/ppermute | solution.py:347
  8.1 4.4 %collective-permute-start.1 = (bf16[160,256]{1,0:T(8,128)(2,1)S(1)}, bf16[160,256]{1,0:T(8,128)(2,1)S(1)}, u32[]{:S(2)}, u32[]{:S(2)}) collective-permute-start(bf16[160,256]{1,0:T(8,128)(2,1)S(1)} %get-tuple-element.15.refs_0_), channel_id=1, source_target_pairs={{4,0},{6,2},{0,4},{2,6},{12,8},{14,10},{8,12},{10,14},{5,1},{7,3},... | collective-permute-start | bytes 245768 | tf_op jit(solution)/shard_map/ppermute | solution.py:348
  9.7 9.2 %collective-permute-start.2 = (bf16[160,256]{1,0:T(8,128)(2,1)S(1)}, bf16[160,256]{1,0:T(8,128)(2,1)S(1)}, u32[]{:S(2)}, u32[]{:S(2)}) collective-permute-start(bf16[160,256]{1,0:T(8,128)(2,1)S(1)} %get-tuple-element.15.refs_0_), channel_id=1, source_target_pairs={{8,0},{10,2},{12,4},{14,6},{0,8},{2,10},{4,12},{6,14},{9,1},{11,3}... | collective-permute-start | bytes 245768 | tf_op jit(solution)/shard_map/ppermute | solution.py:348
  12.3 6.6 %collective-permute-start.3 = (bf16[160,256]{1,0:T(8,128)(2,1)S(1)}, bf16[160,256]{1,0:T(8,128)(2,1)S(1)}, u32[]{:S(2)}, u32[]{:S(2)}) collective-permute-start(bf16[160,256]{1,0:T(8,128)(2,1)S(1)} %get-tuple-element.15.refs_0_), channel_id=1, source_target_pairs={{12,0},{14,2},{8,4},{10,6},{4,8},{6,10},{0,12},{2,14},{13,1},{15,3... | collective-permute-start | bytes 245768 | tf_op jit(solution)/shard_map/ppermute | solution.py:348
  19.7 6.4 %collective-permute-start.4 = (bf16[512,256]{1,0:T(8,128)(2,1)S(1)}, bf16[512,256]{1,0:T(8,128)(2,1)S(1)}, u32[]{:S(2)}, u32[]{:S(2)}) collective-permute-start(bf16[512,256]{1,0:T(8,128)(2,1)S(1)} %get-tuple-element.18), channel_id=1, source_target_pairs={{0,2},{2,0},{4,6},{6,4},{8,10},{10,8},{12,14},{14,12},{1,3},{3,1},... | collective-permute-start | bytes 786440 | tf_op jit(solution)/shard_map/ppermute | solution.py:361
  21.7 8.1 %collective-permute-start.6 = (f32[8,16,256]{2,1,0:T(8,128)S(1)}, f32[8,16,256]{2,1,0:T(8,128)S(1)}, u32[]{:S(2)}, u32[]{:S(2)}) collective-permute-start(f32[8,16,256]{2,1,0:T(8,128)S(1)} %get-tuple-element.22), channel_id=1, source_target_pairs={{0,12},{2,14},{4,8},{6,10},{8,4},{10,6},{12,0},{14,2},{1,13},{3,15... | collective-permute-start | bytes 393224 | tf_op jit(solution)/shard_map/ppermute | solution.py:387
  24.2 10.9 %collective-permute-start.7 = (f32[8,16,256]{2,1,0:T(8,128)S(1)}, f32[8,16,256]{2,1,0:T(8,128)S(1)}, u32[]{:S(2)}, u32[]{:S(2)}) collective-permute-start(f32[8,16,256]{2,1,0:T(8,128)S(1)} %get-tuple-element.23), channel_id=1, source_target_pairs={{0,8},{2,10},{4,12},{6,14},{8,0},{10,2},{12,4},{14,6},{1,9},{3,11}... | collective-permute-start | bytes 393224 | tf_op jit(solution)/shard_map/ppermute | solution.py:387
  27.3 8.2 %collective-permute-start.8 = (f32[8,16,256]{2,1,0:T(8,128)S(1)}, f32[8,16,256]{2,1,0:T(8,128)S(1)}, u32[]{:S(2)}, u32[]{:S(2)}) collective-permute-start(f32[8,16,256]{2,1,0:T(8,128)S(1)} %get-tuple-element.24), channel_id=1, source_target_pairs={{0,4},{2,6},{4,0},{6,2},{8,12},{10,14},{12,8},{14,10},{1,5},{3,7},... | collective-permute-start | bytes 393224 | tf_op jit(solution)/shard_map/ppermute | solution.py:387

commit v3 on v2

--- a/solution.py
+++ b/solution.py
@@ -53,12 +53,12 @@
         return (slab > 0, slab < self.n_slab - 1)
 
 
-def call(kernel, outs, *args, scratch=(), flops=0, specs=None):
+def call(kernel, outs, *args, scratch=(), flops=0):
     size = lambda xs: sum(x.size * x.dtype.itemsize for x in xs)
     return pl.pallas_call(
         kernel,
         out_shape=outs,
-        in_specs=specs or [VMEM] * len(args),
+        in_specs=[VMEM] * len(args),
         out_specs=[VMEM] * len(outs),
         scratch_shapes=list(scratch),
         compiler_params=pltpu.CompilerParams(vmem_limit_bytes=24 * 1024 * 1024),
@@ -68,36 +68,22 @@
     )(*args)
 
 
-def pack_kernel(p, counts_ref, activity_ref, back_ref, edges_ref, tiles_ref, active_ref, backs_ref, sems):
-    slab = lax.axis_index("slab")
-    last, tile = p.slices - 1, min(8, p.slices)
-    copies = [
-        pltpu.make_async_copy(activity_ref, active_ref, sems.at[0]),
-        pltpu.make_async_copy(back_ref, backs_ref, sems.at[1]),
-    ]
+def valid_kernel(p, valid_ref):
+    for high, valid in enumerate(p.valid()):
+        valid_ref[high] = jnp.where(valid, jnp.ones((8, 128), F32), 0.0)
+
+
+def pack_kernel(p, valid_ref, counts_ref, activity_ref, back_ref, edges_ref):
+    lowest = valid_ref[0, 0:1, 0:1] == 0.0
+    last = p.slices - 1
+    activity = activity_ref[...].astype(F32)
+    back = back_ref[...].astype(F32)
     for slot in range(p.n_edges):
-        first = (slot == 0) if p.n_edges == 2 else (slab == 0)
-        low = jnp.where(first, p.slices - tile, 0)
-        copies.append(
-            pltpu.make_async_copy(
-                counts_ref.at[:, :, :, pl.ds(pl.multiple_of(low, tile), tile), :],
-                tiles_ref.at[slot],
-                sems.at[2 + slot],
-            )
-        )
-    for copy in copies:
-        copy.start()
-    copies[0].wait()
-    copies[1].wait()
-    activity = active_ref[...].astype(F32)
-    back = backs_ref[...].astype(F32)
-    for slot in range(p.n_edges):
-        copies[2 + slot].wait()
 
         def edge(high, low):
             if p.n_edges == 2:
                 return high if slot == 0 else low
-            return jnp.where(slab == 0, high, low)
+            return jnp.where(lowest, high, low)
 
         for j in range(2):
             edges_ref[slot, j * p.each : (j + 1) * p.each] = edge(
@@ -107,7 +93,7 @@
             for r in range(p.n_view):
                 at = p.edge_counts + (v * p.n_view + r) * p.each
                 edges_ref[slot, at : at + p.each] = edge(
-                    tiles_ref[slot, v, r, :, tile - 1, :], tiles_ref[slot, v, r, :, 0, :]
+                    counts_ref[v, r, :, last, :], counts_ref[v, r, :, 0, :]
                 ).astype(F32)
             edges_ref[slot, p.edge_back + v : p.edge_back + v + 1] = edge(
                 back[v, last : last + 1], back[v, 0:1]
@@ -121,16 +107,15 @@
     at = lax.axis_index("view")
     at_line, side = at // p.pairs, at % p.pairs
     payload_ref[: p.block] = activity_ref[...].reshape(p.block, p.width)
-    for high, valid in enumerate(p.valid()):
-        edge = edges_ref[min(high, p.n_edges - 1), : 2 * p.each]
-        low = p.block + high * 2 * p.each
-        payload_ref[low : low + 2 * p.each] = jnp.where(valid, edge, 0.0).astype(BF16)
-    if p.pairs == 1:
-        return
-    (out,) = outs
+    for e in range(p.n_edges):
+        low = p.block + e * 2 * p.each
+        payload_ref[low : low + 2 * p.each] = edges_ref[e, : 2 * p.each].astype(BF16)
+    out = outs[0]
+    for ks, later in zip(p.halves[1:], outs[1:]):
+        copy_counts(p, ks, counts_ref, later, 0)
     out[: p.bands] = values_ref[...].reshape(p.bands, p.width)
     out[p.bands : p.starts] = back_ref[...].reshape(p.views * p.slices, p.width)
-    starts = starts_ref[...]
+    starts = jnp.concatenate([starts_ref[t] for t in range(p.taps)], axis=0)
     pieces = [lax.shift_right_logical(starts, 7), starts & 127]
     tail = p.param_rows - p.starts - 2 * p.views * p.taps
     if tail:
@@ -178,42 +163,7 @@
     return moved.astype(BF16)
 
 
-def own_kernel(p, values_ref, starts_ref, counts_ref, *refs):
-    blocks, outs, lifted_ref = refs[: p.line], refs[p.line : -1], refs[-1]
-    matrix_ref, sources = outs[0], outs[1 : 1 + len(p.halves)]
-    if p.pairs == 2:
-        for ks, out in zip(p.halves[1:], outs[1 + len(p.halves) :]):
-            copy_counts(p, ks, counts_ref, out, 0)
-    for v in range(p.views):
-        for t in range(p.taps):
-            at = v * p.taps + t
-            matrix_ref[v, t] = place_bands(
-                values_ref[v, t].astype(F32), starts_ref[at : at + 1]
-            )
-    for ks, source_ref in zip(p.halves, sources):
-        rows = len(ks) * p.each
-        for i, k in enumerate(ks):
-            low = i * p.each
-            lifted_ref[low : low + p.each, 8 : 8 + p.slices, :] = (
-                blocks[k][: p.block].astype(F32).reshape(p.each, p.slices, p.width)
-            )
-            edges = blocks[k][p.block :].astype(F32)
-            for high in range(2):
-                for j in range(2):
-                    lifted_ref[low : low + p.each, (8 + p.slices if high else 6) + j, :] = edges[
-                        (2 * high + j) * p.each : (2 * high + j + 1) * p.each
-                    ]
-        main = rows * p.slices
-        for t in range(p.taps):
-            source_ref[t, :main] = (
-                lifted_ref[:rows, 7 + t : 7 + t + p.slices, :].astype(BF16).reshape(main, p.width)
-            )
-            source_ref[t, main:] = jnp.concatenate(
-                [lifted_ref[:rows, 6 + t, :], lifted_ref[:rows, 7 + p.slices + t, :]], axis=0
-            ).astype(BF16)
-
-
-def their_kernel(p, params_ref, matrix_ref):
+def matrix_kernel(p, params_ref, matrix_ref):
     starts = params_ref[p.starts : p.param_rows].astype(F32).astype(I32)
     n = p.views * p.taps
     starts = starts[:n] * 128 + starts[n : 2 * n]
@@ -221,15 +171,43 @@
         for t in range(p.taps):
             at = v * p.taps + t
             values = params_ref[at * p.band : (at + 1) * p.band].astype(F32)
+            at = t * p.views + v
             matrix_ref[v, t] = place_bands(values, starts[at : at + 1])
 
 
-def rows_kernel(p, half, source_ref, counts_ref, edges_ref, back_ref, matrix_ref, *refs):
+def place_source(p, blocks, lifted_ref, source_ref):
+    rows = len(blocks) * p.each
+    for i, block_ref in enumerate(blocks):
+        low = i * p.each
+        lifted_ref[low : low + p.each, 8 : 8 + p.slices, :] = (
+            block_ref[: p.block].astype(F32).reshape(p.each, p.slices, p.width)
+        )
+        edges = block_ref[p.block :].astype(F32)
+        for high, valid in enumerate(p.valid()):
+            for j in range(2):
+                at = (2 * min(high, p.n_edges - 1) + j) * p.each
+                lifted_ref[low : low + p.each, (8 + p.slices if high else 6) + j, :] = jnp.where(
+                    valid, edges[at : at + p.each], 0.0
+                )
+    main = rows * p.slices
+    for t in range(p.taps):
+        source_ref[t, :main] = (
+            lifted_ref[:, 7 + t : 7 + t + p.slices, :].astype(BF16).reshape(main, p.width)
+        )
+        source_ref[t, main:] = jnp.concatenate(
+            [lifted_ref[:, 6 + t, :], lifted_ref[:, 7 + p.slices + t, :]], axis=0
+        ).astype(BF16)
+
+
+def rows_kernel(p, half, counts_ref, edges_ref, back_ref, matrix_ref, *refs):
     ks = p.halves[half]
+    blocks, refs = refs[: len(ks)], refs[len(ks) :]
+    refs = refs[half:]
     if p.pairs == 2:
         (their_ref, first_ref, their_matrix_ref), refs = refs[:3], refs[3:]
         base = p.first_counts if half == 0 else 0
-    outs, (ratio_ref, up_ref, down_ref) = refs[: len(ks)], refs[len(ks) :]
+    outs, (lifted_ref, source_ref, ratio_ref, up_ref, down_ref) = refs[: len(ks)], refs[len(ks) :]
+    place_source(p, blocks, lifted_ref, source_ref)
     at = lax.axis_index("view")
     at_line, side = at // p.pairs, at % p.pairs
     rows = len(ks) * p.each
@@ -307,7 +285,15 @@
     total = project(1, main).reshape(rows, p.slices, p.width)
     total = total + up_ref[:, 1 : 1 + p.slices, :] + down_ref[:, 7 : 7 + p.slices, :]
     for i, out in enumerate(outs):
-        out[...] = total[i * p.each : (i + 1) * p.each]
+        part = total[i * p.each : (i + 1) * p.each]
+        out[...] = part
+
+
+def sum_kernel(p, *refs):
+    total = None
+    for ref in refs[:-1]:
+        total = ref[...] if total is None else total + ref[...]
+    refs[-1][...] = total
 
 
 def per_device(activity, histo_counts, background, blur_values, band_start):
@@ -315,66 +301,55 @@
     shape = jax.ShapeDtypeStruct
     part = lambda kernel, *static: functools.partial(kernel, p, *static)
     width = p.width
+    other = [(i, i ^ 1) for i in range(p.n_view)]
+
     counts = histo_counts.reshape(p.views, p.n_view, p.each, p.slices, width)
     values = jnp.swapaxes(blur_values, 2, 3)
-    starts = band_start.reshape(p.views * p.taps, width)
-    other = [(i, i ^ 1) for i in range(p.n_view)]
-
-    edges = call(
+    starts = jnp.swapaxes(band_start, 0, 1)
+    (valid,) = call(part(valid_kernel), [shape((2, 8, 128), F32)], flops=2 * 10**9)
+    (edges,) = call(
         part(pack_kernel),
         [shape((p.n_edges, p.edge_rows, width), F32)],
-        counts, activity, background,
-        specs=[pl.BlockSpec(memory_space=pl.ANY)] * 3,
-        scratch=[
-            pltpu.VMEM((p.n_edges, p.views, p.n_view, p.each, min(8, p.slices), width), I32),
-            pltpu.VMEM(activity.shape, BF16),
-            pltpu.VMEM(background.shape, BF16),
-            pltpu.SemaphoreType.DMA((2 + p.n_edges,)),
-        ],
-    )[0]
+        valid, counts, activity, background,
+    )
     if p.n_slab == 2:
         edges = lax.ppermute(edges, "slab", [(0, 1), (1, 0)])
     elif p.n_slab > 2:
         up = [(i, i + 1) for i in range(p.n_slab - 1)]
         down = [(j, i) for i, j in up]
         edges = jnp.stack([lax.ppermute(edges[0], "slab", up), lax.ppermute(edges[1], "slab", down)])
-    outs = [shape((p.block + 4 * p.each, width), BF16)]
-    if p.pairs == 2:
-        outs.append(shape((p.first_rows, width), BF16))
+    outs = [shape((p.block + 2 * p.n_edges * p.each, width), BF16), shape((p.first_rows, width), BF16)]
+    outs += [shape((p.views * len(h) * p.block, width), BF16) for h in p.halves[1:]]
     payload, *sent = call(
         part(send_kernel), outs, edges, counts, activity, background, values, starts
     )
-    theirs = [lax.ppermute(x, "view", other) for x in sent]
-    blocks = [payload] + [lax.ppermute(payload, "view", p.across(k, False)) for k in range(1, p.line)]
+    theirs = [lax.ppermute(x, "view", other) for x in sent] if p.pairs == 2 else []
+    far_first = range(p.line - 1, 0, -1)
+    blocks = {k: lax.ppermute(payload, "view", p.across(k, False)) for k in far_first}
+    blocks = [payload] + [blocks[k] for k in range(1, p.line)]
 
     matrices = shape((p.views, p.taps, width, width), BF16)
-    most = max(len(h) for h in p.halves) * p.each
-    outs = [matrices]
-    outs += [shape((p.taps, len(h) * p.each * (p.slices + 2), width), BF16) for h in p.halves]
+    (matrix,) = call(part(matrix_kernel), [matrices], sent[0])
     if p.pairs == 2:
-        outs += [shape((p.views * len(h) * p.block, width), BF16) for h in p.halves[1:]]
-    matrix, *outs = call(
-        part(own_kernel), outs, values, starts, counts, *blocks,
-        scratch=[pltpu.VMEM((most, p.slices + 16, width), F32)],
-    )
-    sources, later = outs[: len(p.halves)], outs[len(p.halves) :]
-    theirs += [lax.ppermute(x, "view", other) for x in later]
-    if p.pairs == 2:
-        (their_matrix,) = call(part(their_kernel), [matrices], theirs[0])
+        (their_matrix,) = call(part(matrix_kernel), [matrices], theirs[0])
 
     terms = {}
     for half, ks in enumerate(p.halves):
-        args = [sources[half], counts, edges, background, matrix]
+        args = [counts, edges, background, matrix] + [blocks[k] for k in ks]
+        args += list(terms.values())[:half]
         if p.pairs == 2:
             args += [theirs[half], theirs[0], their_matrix]
         rows = len(ks) * p.each
         full = rows * (p.slices + 2)
         n_views = p.views * p.pairs
+        plain = shape((p.each, p.slices, width), F32)
         outs = call(
             part(rows_kernel, half),
-            [shape((p.each, p.slices, width), F32)] * len(ks),
+            [plain] * len(ks),
             *args,
             scratch=[
+                pltpu.VMEM((rows, p.slices + 16, width), F32),
+                pltpu.VMEM((p.taps, full, width), BF16),
                 pltpu.VMEM((n_views, full, width), BF16),
                 pltpu.VMEM((rows, p.slices + 8, width), F32),
                 pltpu.VMEM((rows, p.slices + 8, width), F32),
@@ -382,10 +357,14 @@
             flops=4 * n_views * p.taps * full * width * width,
         )
         terms.update(zip(ks, outs))
-    total = terms[0]
-    for k in reversed(range(1, p.line)):
-        total = total + lax.ppermute(terms[k], "view", p.across(k, True))
-    return total
+    total = [terms[0]]
+    for ks in p.halves:
+        came = [lax.ppermute(terms[k], "view", p.across(k, True)) for k in ks if k]
+        if came or ks[0] == 0:
+            plain_terms = total if ks[0] == 0 else []
+            done = call(part(sum_kernel), [plain], *came, *plain_terms)
+            total = list(done) if ks[0] == 0 else total + list(done)
+    return total[0]
 
 
 def solution(mesh):

time: 36.4 us -> 32.3 us (0.89)
  local copies, waits for them, and re-layouts: 3.18 us -> 1.58 us
  waiting for transfers between devices: 14.6 us -> 13 us
  other arithmetic: 0.7 us -> 0 us
    ppermute x3, waiting for transfers between devices: 6.4 us -> 0.01 us  [per_device(): lax.ppermute(payload, 'view', p.across(k, False))]
    ppermute x5, waiting for transfers between devices: 7.14 us -> 11.9 us  [the longest x3 6.35 us: per_device(): came = [lax.ppermute(terms[k], 'view', p.across(k, True)) for k in ks if k]]
    unnamed x17 -> x10, local copies, waits for them, and re-layouts: 3.17 us -> 1.58 us
    add x1 -> x0, other arithmetic: 0.7 us -> none  [per_device(): total = total + lax.ppermute(terms[k], 'view', p.across(k, True))]
    ppermute x5, starting transfers between devices: 9.01 us -> 8.49 us  [the longest x3 5.47 us: per_device(): came = [lax.ppermute(terms[k], 'view', p.across(k, True)) for k in ks if k]]
    pallas_call x6 -> x9, Pallas kernels: 3.73 us -> 3.87 us  [call(): pl.pallas_call(kernel, out_shape=outs, in_specs=[VMEM] * len(args), out_s...]
  transfers between devices with their start and end apart: 9 -> 9, of which waited for: 6 -> 4; matrix products, arithmetic and copies ran while one was open for 0% -> 0% of each run, Pallas kernels for 9% -> 9%
where the time goes in v3:
time: 32.3 us; the launch traced here: 32.2 us
  starting transfers between devices  13.7 us (42%)
  waiting for transfers between devices  13 us (40%)
  Pallas kernels  3.87 us (12%)
  local copies, waits for them, and re-layouts  1.58 us (5%)
    ppermute x3, waiting for transfers between devices, per_device(): came = [lax.ppermute(terms[k], 'view', p.across(k, True)) for k in ks if k]  6.35 us
    ppermute x2, waiting for transfers between devices, per_device(): lax.ppermute(x, 'view', other)  5.57 us
    ppermute x3, starting transfers between devices, per_device(): came = [lax.ppermute(terms[k], 'view', p.across(k, True)) for k in ks if k]  5.47 us
    ppermute x3, starting transfers between devices, per_device(): lax.ppermute(payload, 'view', p.across(k, False))  4.66 us
    pallas_call x9, Pallas kernels, call(): pl.pallas_call(kernel, out_shape=outs, in_specs=[VMEM] * len(args), out_s...  3.87 us
    ppermute x2, starting transfers between devices, per_device(): lax.ppermute(x, 'view', other)  3.02 us
    unnamed x10, local copies, waits for them, and re-layouts  1.58 us
    ppermute x1, waiting for transfers between devices, per_device(): edges = lax.ppermute(edges, 'slab', [(0, 1), (1, 0)])  1.03 us
  transfers between devices with their start and end apart: 9, of which 4 were waited for; matrix products, arithmetic and copies ran while one was open for 0% of the time, Pallas kernels for 9%

profile of v3, /device:TPU:0, one launch (start us, length us, event | category | flops | bytes accessed | tf_op | source)
XLA Modules:
  0.0 32.2 jit_solution(605229148311333663)
XLA Ops:
  0.0 0.0 copy-start.3
  0.0 0.0 copy-start.4
  0.0 1.6 %copy-done = s32[2,64,16,256]{3,2,1,0:T(8,128)S(1)} copy-done((s32[2,64,16,256]{3,2,1,0:T(8,128)S(1)}, s32[2,64,16,256]{3,2,1,0:T(8,128)}, u32[]{:S(2)}) %copy-start) | copy-done | bytes 2097176
  1.6 0.0 copy-done.2
  1.6 0.0 copy-done.1
  1.6 0.1 shard_map.56
  1.7 0.5 %collective-permute-start = (f32[1,160,256]{2,1,0:T(8,128)S(1)}, f32[1,160,256]{2,1,0:T(8,128)S(1)}, u32[]{:S(2)}, u32[]{:S(2)}) collective-permute-start(f32[1,160,256]{2,1,0:T(8,128)S(1)} %shard_map.56), channel_id=1, source_target_pairs={{0,1},{1,0},{2,3},{3,2},{4,5},{5,4},{6,7},{7,6},{8,9},{9,8},{10,11... | collective-permute-start | bytes 491528 | tf_op jit(solution)/shard_map/ppermute | solution.py:316
  2.2 1.0 %collective-permute-done.edges_ref = f32[1,160,256]{2,1,0:T(8,128)S(1)} collective-permute-done((f32[1,160,256]{2,1,0:T(8,128)S(1)}, f32[1,160,256]{2,1,0:T(8,128)S(1)}, u32[]{:S(2)}, u32[]{:S(2)}) %collective-permute-start) | collective-permute-done | bytes 163872 | tf_op jit(solution)/shard_map/ppermute | solution.py:316
  3.3 0.0 copy-done.3
  3.3 0.0 copy-done.4
  3.3 0.1 shard_map.57
  3.4 2.9 %collective-permute-start.4 = (bf16[832,256]{1,0:T(8,128)(2,1)S(1)}, bf16[832,256]{1,0:T(8,128)(2,1)S(1)}, u32[]{:S(2)}, u32[]{:S(2)}) collective-permute-start(bf16[832,256]{1,0:T(8,128)(2,1)S(1)} %get-tuple-element.12.params_ref), channel_id=1, source_target_pairs={{0,2},{2,0},{4,6},{6,4},{8,10},{10,8},{12,14},{14,12},{1,3},{3,1},... | collective-permute-start | bytes 1277960 | tf_op jit(solution)/shard_map/ppermute | solution.py:326
  6.3 0.1 collective-permute-start.5
  6.4 3.0 %collective-permute-start.2 = (bf16[144,256]{1,0:T(8,128)(2,1)S(1)}, bf16[144,256]{1,0:T(8,128)(2,1)S(1)}, u32[]{:S(2)}, u32[]{:S(2)}) collective-permute-start(bf16[144,256]{1,0:T(8,128)(2,1)S(1)} %get-tuple-element.13.refs_0_), channel_id=1, source_target_pairs={{8,0},{10,2},{12,4},{14,6},{0,8},{2,10},{4,12},{6,14},{9,1},{11,3}... | collective-permute-start | bytes 221192 | tf_op jit(solution)/shard_map/ppermute | solution.py:328
  9.4 1.3 %collective-permute-start.3 = (bf16[144,256]{1,0:T(8,128)(2,1)S(1)}, bf16[144,256]{1,0:T(8,128)(2,1)S(1)}, u32[]{:S(2)}, u32[]{:S(2)}) collective-permute-start(bf16[144,256]{1,0:T(8,128)(2,1)S(1)} %get-tuple-element.13.refs_0_), channel_id=1, source_target_pairs={{12,0},{14,2},{8,4},{10,6},{4,8},{6,10},{0,12},{2,14},{13,1},{15,3... | collective-permute-start | bytes 221192 | tf_op jit(solution)/shard_map/ppermute | solution.py:328
  10.8 0.3 shard_map.58.matrix_ref
  11.0 0.3 collective-permute-start.1
  11.3 5.6 %collective-permute-done.4.params_ref.refs_2_.refs_3_.refs_4_ = bf16[832,256]{1,0:T(8,128)(2,1)S(1)} collective-permute-done((bf16[832,256]{1,0:T(8,128)(2,1)S(1)}, bf16[832,256]{1,0:T(8,128)(2,1)S(1)}, u32[]{:S(2)}, u32[]{:S(2)}) %collective-permute-start.4) | collective-permute-done | bytes 426016 | tf_op jit(solution)/shard_map/ppermute | solution.py:326
  16.9 0.3 shard_map.59.refs_4_.refs_5_
  17.2 0.0 collective-permute-done.2.refs_0_
  17.2 0.0 collective-permute-done.3.refs_1_
  17.2 1.2 %shard_map.60 = (f32[8,16,256]{2,1,0:T(8,128)S(1)}, f32[8,16,256]{2,1,0:T(8,128)S(1)}) custom-call(s32[2,8,8,16,256]{4,3,2,1,0:T(8,128)S(1)} %bitcast.5, f32[1,160,256]{2,1,0:T(8,128)S(1)} %collective-permute-done.edges_ref, bf16[2,16,256]{2,1,0:T(8,128)(2,1)S(1)} %copy-done.1, bf16[2,3,256,256]{3,2,1,0:T(8,128)(2,1)S(1)} %shard_map.58.matrix_ref, ...), custom_call_target="tpu_custom_call" | custom-call | flops 905969664 | bytes 5111808 | tf_op jit(solution)/shard_map/pallas_call | solution.py:58
  18.4 3.2 %collective-permute-start.7 = (f32[8,16,256]{2,1,0:T(8,128)S(1)}, f32[8,16,256]{2,1,0:T(8,128)S(1)}, u32[]{:S(2)}, u32[]{:S(2)}) collective-permute-start(f32[8,16,256]{2,1,0:T(8,128)S(1)} %get-tuple-element.14.refs_2_), channel_id=1, source_target_pairs={{0,8},{2,10},{4,12},{6,14},{8,0},{10,2},{12,4},{14,6},{1,9},{3,11}... | collective-permute-start | bytes 393224 | tf_op jit(solution)/shard_map/ppermute | solution.py:362
  21.6 1.3 %collective-permute-start.8 = (f32[8,16,256]{2,1,0:T(8,128)S(1)}, f32[8,16,256]{2,1,0:T(8,128)S(1)}, u32[]{:S(2)}, u32[]{:S(2)}) collective-permute-start(f32[8,16,256]{2,1,0:T(8,128)S(1)} %get-tuple-element.18), channel_id=1, source_target_pairs={{0,12},{2,14},{4,8},{6,10},{8,4},{10,6},{12,0},{14,2},{1,13},{3,15... | collective-permute-start | bytes 393224 | tf_op jit(solution)/shard_map/ppermute | solution.py:362
  23.0 0.0 collective-permute-done.1.refs_1_
  23.0 0.0 collective-permute-done.5.refs_3_
  23.0 1.2 %shard_map.61 = (f32[8,16,256]{2,1,0:T(8,128)S(1)}, f32[8,16,256]{2,1,0:T(8,128)S(1)}) custom-call(s32[2,8,8,16,256]{4,3,2,1,0:T(8,128)S(1)} %bitcast.6, f32[1,160,256]{2,1,0:T(8,128)S(1)} %collective-permute-done.edges_ref, bf16[2,16,256]{2,1,0:T(8,128)(2,1)S(1)} %copy-done.1, bf16[2,3,256,256]{3,2,1,0:T(8,128)(2,1)S(1)} %shard_map.58.matrix_ref, ...), custom_call_target="tpu_custom_call" | custom-call | flops 905969664 | bytes 5079040 | tf_op jit(solution)/shard_map/pallas_call | solution.py:58
  24.2 0.9 %collective-permute-start.6 = (f32[8,16,256]{2,1,0:T(8,128)S(1)}, f32[8,16,256]{2,1,0:T(8,128)S(1)}, u32[]{:S(2)}, u32[]{:S(2)}) collective-permute-start(f32[8,16,256]{2,1,0:T(8,128)S(1)} %get-tuple-element.16), channel_id=1, source_target_pairs={{0,4},{2,6},{4,0},{6,2},{8,12},{10,14},{12,8},{14,10},{1,5},{3,7},... | collective-permute-start | bytes 393224 | tf_op jit(solution)/shard_map/ppermute | solution.py:362
  25.1 5.5 %collective-permute-done.7.refs_0_ = f32[8,16,256]{2,1,0:T(8,128)S(1)} collective-permute-done((f32[8,16,256]{2,1,0:T(8,128)S(1)}, f32[8,16,256]{2,1,0:T(8,128)S(1)}, u32[]{:S(2)}, u32[]{:S(2)}) %collective-permute-start.7) | collective-permute-done | bytes 131104 | tf_op jit(solution)/shard_map/ppermute | solution.py:362
  30.7 0.0 collective-permute-done.8.refs_1_
  30.7 0.8 %collective-permute-done.6.refs_0_ = f32[8,16,256]{2,1,0:T(8,128)S(1)} collective-permute-done((f32[8,16,256]{2,1,0:T(8,128)S(1)}, f32[8,16,256]{2,1,0:T(8,128)S(1)}, u32[]{:S(2)}, u32[]{:S(2)}) %collective-permute-start.6) | collective-permute-done | bytes 131104 | tf_op jit(solution)/shard_map/ppermute | solution.py:362
  31.5 0.7 %shard_map.63 = f32[8,16,256]{2,1,0:T(8,128)} custom-call(f32[8,16,256]{2,1,0:T(8,128)S(1)} %collective-permute-done.6.refs_0_, f32[8,16,256]{2,1,0:T(8,128)S(1)} %get-tuple-element.17.refs_1_, f32[8,16,256]{2,1,0:T(8,128)S(1)} %shard_map.62.refs_2_), custom_call_target="tpu_custom_call" | custom-call | bytes 524288 | tf_op jit(solution)/shard_map/pallas_call | solution.py:58
  (5 shorter events, 0.0 us)
Async XLA Ops:
  0.0 1.6 %copy-start = (s32[2,64,16,256]{3,2,1,0:T(8,128)S(1)}, s32[2,64,16,256]{3,2,1,0:T(8,128)}, u32[]{:S(2)}) copy-start(s32[2,64,16,256]{3,2,1,0:T(8,128)} %param.6) | copy-start | bytes 6291460
  0.0 1.6 %copy-start.2 = (bf16[8,16,256]{2,1,0:T(8,128)(2,1)S(1)}, bf16[8,16,256]{2,1,0:T(8,128)(2,1)}, u32[]{:S(2)}) copy-start(bf16[8,16,256]{2,1,0:T(8,128)(2,1)} %activity_ref.3) | copy-start | bytes 196612
  0.0 1.6 %copy-start.1 = (bf16[2,16,256]{2,1,0:T(8,128)(2,1)S(1)}, bf16[2,16,256]{2,1,0:T(8,128)(2,1)}, u32[]{:S(2)}) copy-start(bf16[2,16,256]{2,1,0:T(8,128)(2,1)} %back_ref.7) | copy-start | bytes 49156
  0.0 3.3 %copy-start.3 = (bf16[2,3,256,32]{2,3,1,0:T(8,128)(2,1)S(1)}, bf16[2,3,256,32]{2,3,1,0:T(8,128)(2,1)}, u32[]{:S(2)}) copy-start(bf16[2,3,256,32]{2,3,1,0:T(8,128)(2,1)} %param.8) | copy-start | bytes 294916
  0.0 3.3 %copy-start.4 = (s32[2,3,256]{2,0,1:T(2,128)S(1)}, s32[2,3,256]{2,0,1:T(2,128)}, u32[]{:S(2)}) copy-start(s32[2,3,256]{2,0,1:T(2,128)} %param.9) | copy-start | bytes 18436
  1.7 1.5 %collective-permute-start = (f32[1,160,256]{2,1,0:T(8,128)S(1)}, f32[1,160,256]{2,1,0:T(8,128)S(1)}, u32[]{:S(2)}, u32[]{:S(2)}) collective-permute-start(f32[1,160,256]{2,1,0:T(8,128)S(1)} %shard_map.56), channel_id=1, source_target_pairs={{0,1},{1,0},{2,3},{3,2},{4,5},{5,4},{6,7},{7,6},{8,9},{9,8},{10,11... | collective-permute-start | bytes 491528 | tf_op jit(solution)/shard_map/ppermute | solution.py:316
  3.4 13.5 %collective-permute-start.4 = (bf16[832,256]{1,0:T(8,128)(2,1)S(1)}, bf16[832,256]{1,0:T(8,128)(2,1)S(1)}, u32[]{:S(2)}, u32[]{:S(2)}) collective-permute-start(bf16[832,256]{1,0:T(8,128)(2,1)S(1)} %get-tuple-element.12.params_ref), channel_id=1, source_target_pairs={{0,2},{2,0},{4,6},{6,4},{8,10},{10,8},{12,14},{14,12},{1,3},{3,1},... | collective-permute-start | bytes 1277960 | tf_op jit(solution)/shard_map/ppermute | solution.py:326
  6.3 16.7 %collective-permute-start.5 = (bf16[512,256]{1,0:T(8,128)(2,1)S(1)}, bf16[512,256]{1,0:T(8,128)(2,1)S(1)}, u32[]{:S(2)}, u32[]{:S(2)}) collective-permute-start(bf16[512,256]{1,0:T(8,128)(2,1)S(1)} %get-tuple-element.15), channel_id=1, source_target_pairs={{0,2},{2,0},{4,6},{6,4},{8,10},{10,8},{12,14},{14,12},{1,3},{3,1},... | collective-permute-start | bytes 786440 | tf_op jit(solution)/shard_map/ppermute | solution.py:326
  6.4 10.8 %collective-permute-start.2 = (bf16[144,256]{1,0:T(8,128)(2,1)S(1)}, bf16[144,256]{1,0:T(8,128)(2,1)S(1)}, u32[]{:S(2)}, u32[]{:S(2)}) collective-permute-start(bf16[144,256]{1,0:T(8,128)(2,1)S(1)} %get-tuple-element.13.refs_0_), channel_id=1, source_target_pairs={{8,0},{10,2},{12,4},{14,6},{0,8},{2,10},{4,12},{6,14},{9,1},{11,3}... | collective-permute-start | bytes 221192 | tf_op jit(solution)/shard_map/ppermute | solution.py:328
  9.4 7.8 %collective-permute-start.3 = (bf16[144,256]{1,0:T(8,128)(2,1)S(1)}, bf16[144,256]{1,0:T(8,128)(2,1)S(1)}, u32[]{:S(2)}, u32[]{:S(2)}) collective-permute-start(bf16[144,256]{1,0:T(8,128)(2,1)S(1)} %get-tuple-element.13.refs_0_), channel_id=1, source_target_pairs={{12,0},{14,2},{8,4},{10,6},{4,8},{6,10},{0,12},{2,14},{13,1},{15,3... | collective-permute-start | bytes 221192 | tf_op jit(solution)/shard_map/ppermute | solution.py:328
  11.0 11.9 %collective-permute-start.1 = (bf16[144,256]{1,0:T(8,128)(2,1)S(1)}, bf16[144,256]{1,0:T(8,128)(2,1)S(1)}, u32[]{:S(2)}, u32[]{:S(2)}) collective-permute-start(bf16[144,256]{1,0:T(8,128)(2,1)S(1)} %get-tuple-element.13.refs_0_), channel_id=1, source_target_pairs={{4,0},{6,2},{0,4},{2,6},{12,8},{14,10},{8,12},{10,14},{5,1},{7,3},... | collective-permute-start | bytes 221192 | tf_op jit(solution)/shard_map/ppermute | solution.py:328
  18.4 12.2 %collective-permute-start.7 = (f32[8,16,256]{2,1,0:T(8,128)S(1)}, f32[8,16,256]{2,1,0:T(8,128)S(1)}, u32[]{:S(2)}, u32[]{:S(2)}) collective-permute-start(f32[8,16,256]{2,1,0:T(8,128)S(1)} %get-tuple-element.14.refs_2_), channel_id=1, source_target_pairs={{0,8},{2,10},{4,12},{6,14},{8,0},{10,2},{12,4},{14,6},{1,9},{3,11}... | collective-permute-start | bytes 393224 | tf_op jit(solution)/shard_map/ppermute | solution.py:362
  21.6 9.0 %collective-permute-start.8 = (f32[8,16,256]{2,1,0:T(8,128)S(1)}, f32[8,16,256]{2,1,0:T(8,128)S(1)}, u32[]{:S(2)}, u32[]{:S(2)}) collective-permute-start(f32[8,16,256]{2,1,0:T(8,128)S(1)} %get-tuple-element.18), channel_id=1, source_target_pairs={{0,12},{2,14},{4,8},{6,10},{8,4},{10,6},{12,0},{14,2},{1,13},{3,15... | collective-permute-start | bytes 393224 | tf_op jit(solution)/shard_map/ppermute | solution.py:362
  24.2 7.3 %collective-permute-start.6 = (f32[8,16,256]{2,1,0:T(8,128)S(1)}, f32[8,16,256]{2,1,0:T(8,128)S(1)}, u32[]{:S(2)}, u32[]{:S(2)}) collective-permute-start(f32[8,16,256]{2,1,0:T(8,128)S(1)} %get-tuple-element.16), channel_id=1, source_target_pairs={{0,4},{2,6},{4,0},{6,2},{8,12},{10,14},{12,8},{14,10},{1,5},{3,7},... | collective-permute-start | bytes 393224 | tf_op jit(solution)/shard_map/ppermute | solution.py:362

commit v4 on v3

--- a/solution.py
+++ b/solution.py
@@ -8,7 +8,8 @@
 from jax.sharding import PartitionSpec as P
 
 VMEM = pl.BlockSpec(memory_space=pltpu.VMEM)
-BF16, F32, I32 = jnp.bfloat16, jnp.float32, jnp.int32
+BF16, F32, I16, I32 = jnp.bfloat16, jnp.float32, jnp.int16, jnp.int32
+FULL, STEPS = 32700.0, 64.0
 
 
 def padded_16(rows):
@@ -286,13 +287,35 @@
     total = total + up_ref[:, 1 : 1 + p.slices, :] + down_ref[:, 7 : 7 + p.slices, :]
     for i, out in enumerate(outs):
         part = total[i * p.each : (i + 1) * p.each]
-        out[...] = part
-
-
-def sum_kernel(p, *refs):
+        if ks[i] == 0:
+            out[...] = part
+        else:
+            encode(p, part, out)
+
+
+def encode(p, x, out_ref):
+    most = jnp.maximum(jnp.max(jnp.abs(x), axis=1), 1e-30)
+    power = jnp.ceil(jnp.log2(most) * STEPS)
+    codes = jnp.round(x * (FULL * jnp.exp2(power * (-1.0 / STEPS)))[:, None, :])
+    out_ref[: p.block] = codes.reshape(p.block, p.width).astype(I32).astype(I16)
+    tail = padded_16(p.each) - p.each
+    if tail:
+        power = jnp.concatenate([power, jnp.zeros((tail, p.width), F32)], axis=0)
+    out_ref[p.block :] = power.astype(I32).astype(I16)
+
+
+def decode(p, in_ref):
+    power = in_ref[p.block :].astype(I32).astype(F32)[: p.each]
+    scale = jnp.exp2(power * (1.0 / STEPS)) * (1.0 / FULL)
+    codes = in_ref[: p.block].astype(I32).astype(F32)
+    return codes.reshape(p.each, p.slices, p.width) * scale[:, None, :]
+
+
+def sum_kernel(p, coded, *refs):
     total = None
-    for ref in refs[:-1]:
-        total = ref[...] if total is None else total + ref[...]
+    for i, ref in enumerate(refs[:-1]):
+        term = decode(p, ref) if i < coded else ref[...]
+        total = term if total is None else total + term
     refs[-1][...] = total
 
 
@@ -342,10 +365,11 @@
         rows = len(ks) * p.each
         full = rows * (p.slices + 2)
         n_views = p.views * p.pairs
+        code = shape((p.block + padded_16(p.each), width), I16)
         plain = shape((p.each, p.slices, width), F32)
         outs = call(
             part(rows_kernel, half),
-            [plain] * len(ks),
+            [code if k else plain for k in ks],
             *args,
             scratch=[
                 pltpu.VMEM((rows, p.slices + 16, width), F32),
@@ -362,7 +386,7 @@
         came = [lax.ppermute(terms[k], "view", p.across(k, True)) for k in ks if k]
         if came or ks[0] == 0:
             plain_terms = total if ks[0] == 0 else []
-            done = call(part(sum_kernel), [plain], *came, *plain_terms)
+            done = call(part(sum_kernel, len(came)), [plain], *came, *plain_terms)
             total = list(done) if ks[0] == 0 else total + list(done)
     return total[0]
 

time: 32.3 us -> 29.7 us (0.920)
  waiting for transfers between devices: 13 us -> 10.3 us
    ppermute x3, waiting for transfers between devices: 6.35 us -> 3.67 us  [per_device(): came = [lax.ppermute(terms[k], 'view', p.across(k, True)) for k in ks if k]]
  transfers between devices with their start and end apart: 9 -> 9, of which waited for: 4 -> 5; matrix products, arithmetic and copies ran while one was open for 0% -> 0% of each run, Pallas kernels for 9% -> 11%
where the time goes in v4:
time: 29.7 us; the launch traced here: 29.6 us
  starting transfers between devices  13.6 us (46%)
  waiting for transfers between devices  10.3 us (35%)
  Pallas kernels  4.01 us (14%)
  local copies, waits for them, and re-layouts  1.58 us (5%)
    ppermute x2, waiting for transfers between devices, per_device(): lax.ppermute(x, 'view', other)  5.57 us
    ppermute x3, starting transfers between devices, per_device(): came = [lax.ppermute(terms[k], 'view', p.across(k, True)) for k in ks if k]  5.41 us
    ppermute x3, starting transfers between devices, per_device(): lax.ppermute(payload, 'view', p.across(k, False))  4.66 us
    pallas_call x9, Pallas kernels, call(): pl.pallas_call(kernel, out_shape=outs, in_specs=[VMEM] * len(args), out_s...  4.01 us
    ppermute x3, waiting for transfers between devices, per_device(): came = [lax.ppermute(terms[k], 'view', p.across(k, True)) for k in ks if k]  3.67 us
    ppermute x2, starting transfers between devices, per_device(): lax.ppermute(x, 'view', other)  3.02 us
    unnamed x10, local copies, waits for them, and re-layouts  1.58 us
    ppermute x1, waiting for transfers between devices, per_device(): edges = lax.ppermute(edges, 'slab', [(0, 1), (1, 0)])  1.03 us
  transfers between devices with their start and end apart: 9, of which 5 were waited for; matrix products, arithmetic and copies ran while one was open for 0% of the time, Pallas kernels for 11%

profile of v4, /device:TPU:0, one launch (start us, length us, event | category | flops | bytes accessed | tf_op | source)
XLA Modules:
  0.0 29.6 jit_solution(4715027055367395958)
XLA Ops:
  0.0 0.0 copy-start.3
  0.0 0.0 copy-start.4
  0.0 1.6 %copy-done = s32[2,64,16,256]{3,2,1,0:T(8,128)S(1)} copy-done((s32[2,64,16,256]{3,2,1,0:T(8,128)S(1)}, s32[2,64,16,256]{3,2,1,0:T(8,128)}, u32[]{:S(2)}) %copy-start) | copy-done | bytes 2097176
  1.6 0.0 copy-done.2
  1.6 0.0 copy-done.1
  1.6 0.1 shard_map.56
  1.7 0.5 %collective-permute-start = (f32[1,160,256]{2,1,0:T(8,128)S(1)}, f32[1,160,256]{2,1,0:T(8,128)S(1)}, u32[]{:S(2)}, u32[]{:S(2)}) collective-permute-start(f32[1,160,256]{2,1,0:T(8,128)S(1)} %shard_map.56), channel_id=1, source_target_pairs={{0,1},{1,0},{2,3},{3,2},{4,5},{5,4},{6,7},{7,6},{8,9},{9,8},{10,11... | collective-permute-start | bytes 491528 | tf_op jit(solution)/shard_map/ppermute | solution.py:339
  2.2 1.0 %collective-permute-done.edges_ref = f32[1,160,256]{2,1,0:T(8,128)S(1)} collective-permute-done((f32[1,160,256]{2,1,0:T(8,128)S(1)}, f32[1,160,256]{2,1,0:T(8,128)S(1)}, u32[]{:S(2)}, u32[]{:S(2)}) %collective-permute-start) | collective-permute-done | bytes 163872 | tf_op jit(solution)/shard_map/ppermute | solution.py:339
  3.3 0.0 copy-done.3
  3.3 0.0 copy-done.4
  3.3 0.1 shard_map.57
  3.4 2.9 %collective-permute-start.4 = (bf16[832,256]{1,0:T(8,128)(2,1)S(1)}, bf16[832,256]{1,0:T(8,128)(2,1)S(1)}, u32[]{:S(2)}, u32[]{:S(2)}) collective-permute-start(bf16[832,256]{1,0:T(8,128)(2,1)S(1)} %get-tuple-element.12.params_ref), channel_id=1, source_target_pairs={{0,2},{2,0},{4,6},{6,4},{8,10},{10,8},{12,14},{14,12},{1,3},{3,1},... | collective-permute-start | bytes 1277960 | tf_op jit(solution)/shard_map/ppermute | solution.py:349
  6.3 0.1 collective-permute-start.5
  6.4 3.0 %collective-permute-start.2 = (bf16[144,256]{1,0:T(8,128)(2,1)S(1)}, bf16[144,256]{1,0:T(8,128)(2,1)S(1)}, u32[]{:S(2)}, u32[]{:S(2)}) collective-permute-start(bf16[144,256]{1,0:T(8,128)(2,1)S(1)} %get-tuple-element.13.refs_0_), channel_id=1, source_target_pairs={{8,0},{10,2},{12,4},{14,6},{0,8},{2,10},{4,12},{6,14},{9,1},{11,3}... | collective-permute-start | bytes 221192 | tf_op jit(solution)/shard_map/ppermute | solution.py:351
  9.4 1.3 %collective-permute-start.3 = (bf16[144,256]{1,0:T(8,128)(2,1)S(1)}, bf16[144,256]{1,0:T(8,128)(2,1)S(1)}, u32[]{:S(2)}, u32[]{:S(2)}) collective-permute-start(bf16[144,256]{1,0:T(8,128)(2,1)S(1)} %get-tuple-element.13.refs_0_), channel_id=1, source_target_pairs={{12,0},{14,2},{8,4},{10,6},{4,8},{6,10},{0,12},{2,14},{13,1},{15,3... | collective-permute-start | bytes 221192 | tf_op jit(solution)/shard_map/ppermute | solution.py:351
  10.8 0.3 shard_map.58.matrix_ref
  11.0 0.3 %collective-permute-start.1 = (bf16[144,256]{1,0:T(8,128)(2,1)S(1)}, bf16[144,256]{1,0:T(8,128)(2,1)S(1)}, u32[]{:S(2)}, u32[]{:S(2)}) collective-permute-start(bf16[144,256]{1,0:T(8,128)(2,1)S(1)} %get-tuple-element.13.refs_0_), channel_id=1, source_target_pairs={{4,0},{6,2},{0,4},{2,6},{12,8},{14,10},{8,12},{10,14},{5,1},{7,3},... | collective-permute-start | bytes 221192 | tf_op jit(solution)/shard_map/ppermute | solution.py:351
  11.3 5.6 %collective-permute-done.4.params_ref.refs_2_.refs_3_.refs_4_ = bf16[832,256]{1,0:T(8,128)(2,1)S(1)} collective-permute-done((bf16[832,256]{1,0:T(8,128)(2,1)S(1)}, bf16[832,256]{1,0:T(8,128)(2,1)S(1)}, u32[]{:S(2)}, u32[]{:S(2)}) %collective-permute-start.4) | collective-permute-done | bytes 426016 | tf_op jit(solution)/shard_map/ppermute | solution.py:349
  16.9 0.3 shard_map.59.refs_4_.refs_5_
  17.2 0.0 collective-permute-done.2.refs_0_
  17.2 0.0 collective-permute-done.3.refs_1_
  17.2 1.3 %shard_map.60 = (s16[144,256]{1,0:T(8,128)(2,1)S(1)}, s16[144,256]{1,0:T(8,128)(2,1)S(1)}) custom-call(s32[2,8,8,16,256]{4,3,2,1,0:T(8,128)S(1)} %bitcast.5, f32[1,160,256]{2,1,0:T(8,128)S(1)} %collective-permute-done.edges_ref, bf16[2,16,256]{2,1,0:T(8,128)(2,1)S(1)} %copy-done.1, bf16[2,3,256,256]{3,2,1,0:T(8,128)(2,1)S(1)} %shard_map.58.matrix_ref, ...), custom_call_target="tpu_custom_call" | custom-call | flops 905969664 | bytes 4997120 | tf_op jit(solution)/shard_map/pallas_call | solution.py:59
  18.5 3.2 %collective-permute-start.7 = (s16[144,256]{1,0:T(8,128)(2,1)S(1)}, s16[144,256]{1,0:T(8,128)(2,1)S(1)}, u32[]{:S(2)}, u32[]{:S(2)}) collective-permute-start(s16[144,256]{1,0:T(8,128)(2,1)S(1)} %get-tuple-element.14.refs_2_), channel_id=1, source_target_pairs={{0,8},{2,10},{4,12},{6,14},{8,0},{10,2},{12,4},{14,6},{1,9},{3,11}... | collective-permute-start | bytes 221192 | tf_op jit(solution)/shard_map/ppermute | solution.py:386
  21.7 1.3 %collective-permute-start.8 = (s16[144,256]{1,0:T(8,128)(2,1)S(1)}, s16[144,256]{1,0:T(8,128)(2,1)S(1)}, u32[]{:S(2)}, u32[]{:S(2)}) collective-permute-start(s16[144,256]{1,0:T(8,128)(2,1)S(1)} %get-tuple-element.18), channel_id=1, source_target_pairs={{0,12},{2,14},{4,8},{6,10},{8,4},{10,6},{12,0},{14,2},{1,13},{3,15... | collective-permute-start | bytes 221192 | tf_op jit(solution)/shard_map/ppermute | solution.py:386
  23.0 0.0 collective-permute-done.1.refs_1_
  23.0 0.0 collective-permute-done.5.refs_3_
  23.0 1.2 %shard_map.61 = (f32[8,16,256]{2,1,0:T(8,128)S(1)}, s16[144,256]{1,0:T(8,128)(2,1)S(1)}) custom-call(s32[2,8,8,16,256]{4,3,2,1,0:T(8,128)S(1)} %bitcast.6, f32[1,160,256]{2,1,0:T(8,128)S(1)} %collective-permute-done.edges_ref, bf16[2,16,256]{2,1,0:T(8,128)(2,1)S(1)} %copy-done.1, bf16[2,3,256,256]{3,2,1,0:T(8,128)(2,1)S(1)} %shard_map.58.matrix_ref, ...), custom_call_target="tpu_custom_call" | custom-call | flops 905969664 | bytes 4964352 | tf_op jit(solution)/shard_map/pallas_call | solution.py:59
  24.3 0.9 %collective-permute-start.6 = (s16[144,256]{1,0:T(8,128)(2,1)S(1)}, s16[144,256]{1,0:T(8,128)(2,1)S(1)}, u32[]{:S(2)}, u32[]{:S(2)}) collective-permute-start(s16[144,256]{1,0:T(8,128)(2,1)S(1)} %get-tuple-element.16), channel_id=1, source_target_pairs={{0,4},{2,6},{4,0},{6,2},{8,12},{10,14},{12,8},{14,10},{1,5},{3,7},... | collective-permute-start | bytes 221192 | tf_op jit(solution)/shard_map/ppermute | solution.py:386
  25.1 0.9 %collective-permute-done.7.refs_0_ = s16[144,256]{1,0:T(8,128)(2,1)S(1)} collective-permute-done((s16[144,256]{1,0:T(8,128)(2,1)S(1)}, s16[144,256]{1,0:T(8,128)(2,1)S(1)}, u32[]{:S(2)}, u32[]{:S(2)}) %collective-permute-start.7) | collective-permute-done | bytes 73760 | tf_op jit(solution)/shard_map/ppermute | solution.py:386
  26.1 2.2 %collective-permute-done.8.refs_1_ = s16[144,256]{1,0:T(8,128)(2,1)S(1)} collective-permute-done((s16[144,256]{1,0:T(8,128)(2,1)S(1)}, s16[144,256]{1,0:T(8,128)(2,1)S(1)}, u32[]{:S(2)}, u32[]{:S(2)}) %collective-permute-start.8) | collective-permute-done | bytes 73760 | tf_op jit(solution)/shard_map/ppermute | solution.py:386
  28.3 0.6 %collective-permute-done.6.refs_0_ = s16[144,256]{1,0:T(8,128)(2,1)S(1)} collective-permute-done((s16[144,256]{1,0:T(8,128)(2,1)S(1)}, s16[144,256]{1,0:T(8,128)(2,1)S(1)}, u32[]{:S(2)}, u32[]{:S(2)}) %collective-permute-start.6) | collective-permute-done | bytes 73760 | tf_op jit(solution)/shard_map/ppermute | solution.py:386
  28.9 0.7 %shard_map.63 = f32[8,16,256]{2,1,0:T(8,128)} custom-call(s16[144,256]{1,0:T(8,128)(2,1)S(1)} %collective-permute-done.6.refs_0_, f32[8,16,256]{2,1,0:T(8,128)S(1)} %get-tuple-element.17.refs_1_, f32[8,16,256]{2,1,0:T(8,128)S(1)} %shard_map.62.refs_2_), custom_call_target="tpu_custom_call" | custom-call | bytes 466944 | tf_op jit(solution)/shard_map/pallas_call | solution.py:59
  (5 shorter events, 0.1 us)
Async XLA Ops:
  0.0 1.6 %copy-start = (s32[2,64,16,256]{3,2,1,0:T(8,128)S(1)}, s32[2,64,16,256]{3,2,1,0:T(8,128)}, u32[]{:S(2)}) copy-start(s32[2,64,16,256]{3,2,1,0:T(8,128)} %param.6) | copy-start | bytes 6291460
  0.0 1.6 %copy-start.2 = (bf16[8,16,256]{2,1,0:T(8,128)(2,1)S(1)}, bf16[8,16,256]{2,1,0:T(8,128)(2,1)}, u32[]{:S(2)}) copy-start(bf16[8,16,256]{2,1,0:T(8,128)(2,1)} %activity_ref.3) | copy-start | bytes 196612
  0.0 1.6 %copy-start.1 = (bf16[2,16,256]{2,1,0:T(8,128)(2,1)S(1)}, bf16[2,16,256]{2,1,0:T(8,128)(2,1)}, u32[]{:S(2)}) copy-start(bf16[2,16,256]{2,1,0:T(8,128)(2,1)} %back_ref.7) | copy-start | bytes 49156
  0.0 3.3 %copy-start.3 = (bf16[2,3,256,32]{2,3,1,0:T(8,128)(2,1)S(1)}, bf16[2,3,256,32]{2,3,1,0:T(8,128)(2,1)}, u32[]{:S(2)}) copy-start(bf16[2,3,256,32]{2,3,1,0:T(8,128)(2,1)} %param.8) | copy-start | bytes 294916
  0.0 3.3 %copy-start.4 = (s32[2,3,256]{2,0,1:T(2,128)S(1)}, s32[2,3,256]{2,0,1:T(2,128)}, u32[]{:S(2)}) copy-start(s32[2,3,256]{2,0,1:T(2,128)} %param.9) | copy-start | bytes 18436
  1.7 1.5 %collective-permute-start = (f32[1,160,256]{2,1,0:T(8,128)S(1)}, f32[1,160,256]{2,1,0:T(8,128)S(1)}, u32[]{:S(2)}, u32[]{:S(2)}) collective-permute-start(f32[1,160,256]{2,1,0:T(8,128)S(1)} %shard_map.56), channel_id=1, source_target_pairs={{0,1},{1,0},{2,3},{3,2},{4,5},{5,4},{6,7},{7,6},{8,9},{9,8},{10,11... | collective-permute-start | bytes 491528 | tf_op jit(solution)/shard_map/ppermute | solution.py:339
  3.4 13.5 %collective-permute-start.4 = (bf16[832,256]{1,0:T(8,128)(2,1)S(1)}, bf16[832,256]{1,0:T(8,128)(2,1)S(1)}, u32[]{:S(2)}, u32[]{:S(2)}) collective-permute-start(bf16[832,256]{1,0:T(8,128)(2,1)S(1)} %get-tuple-element.12.params_ref), channel_id=1, source_target_pairs={{0,2},{2,0},{4,6},{6,4},{8,10},{10,8},{12,14},{14,12},{1,3},{3,1},... | collective-permute-start | bytes 1277960 | tf_op jit(solution)/shard_map/ppermute | solution.py:349
  6.3 16.7 %collective-permute-start.5 = (bf16[512,256]{1,0:T(8,128)(2,1)S(1)}, bf16[512,256]{1,0:T(8,128)(2,1)S(1)}, u32[]{:S(2)}, u32[]{:S(2)}) collective-permute-start(bf16[512,256]{1,0:T(8,128)(2,1)S(1)} %get-tuple-element.15), channel_id=1, source_target_pairs={{0,2},{2,0},{4,6},{6,4},{8,10},{10,8},{12,14},{14,12},{1,3},{3,1},... | collective-permute-start | bytes 786440 | tf_op jit(solution)/shard_map/ppermute | solution.py:349
  6.4 10.8 %collective-permute-start.2 = (bf16[144,256]{1,0:T(8,128)(2,1)S(1)}, bf16[144,256]{1,0:T(8,128)(2,1)S(1)}, u32[]{:S(2)}, u32[]{:S(2)}) collective-permute-start(bf16[144,256]{1,0:T(8,128)(2,1)S(1)} %get-tuple-element.13.refs_0_), channel_id=1, source_target_pairs={{8,0},{10,2},{12,4},{14,6},{0,8},{2,10},{4,12},{6,14},{9,1},{11,3}... | collective-permute-start | bytes 221192 | tf_op jit(solution)/shard_map/ppermute | solution.py:351
  9.4 7.8 %collective-permute-start.3 = (bf16[144,256]{1,0:T(8,128)(2,1)S(1)}, bf16[144,256]{1,0:T(8,128)(2,1)S(1)}, u32[]{:S(2)}, u32[]{:S(2)}) collective-permute-start(bf16[144,256]{1,0:T(8,128)(2,1)S(1)} %get-tuple-element.13.refs_0_), channel_id=1, source_target_pairs={{12,0},{14,2},{8,4},{10,6},{4,8},{6,10},{0,12},{2,14},{13,1},{15,3... | collective-permute-start | bytes 221192 | tf_op jit(solution)/shard_map/ppermute | solution.py:351
  11.0 12.0 %collective-permute-start.1 = (bf16[144,256]{1,0:T(8,128)(2,1)S(1)}, bf16[144,256]{1,0:T(8,128)(2,1)S(1)}, u32[]{:S(2)}, u32[]{:S(2)}) collective-permute-start(bf16[144,256]{1,0:T(8,128)(2,1)S(1)} %get-tuple-element.13.refs_0_), channel_id=1, source_target_pairs={{4,0},{6,2},{0,4},{2,6},{12,8},{14,10},{8,12},{10,14},{5,1},{7,3},... | collective-permute-start | bytes 221192 | tf_op jit(solution)/shard_map/ppermute | solution.py:351
  18.5 7.6 %collective-permute-start.7 = (s16[144,256]{1,0:T(8,128)(2,1)S(1)}, s16[144,256]{1,0:T(8,128)(2,1)S(1)}, u32[]{:S(2)}, u32[]{:S(2)}) collective-permute-start(s16[144,256]{1,0:T(8,128)(2,1)S(1)} %get-tuple-element.14.refs_2_), channel_id=1, source_target_pairs={{0,8},{2,10},{4,12},{6,14},{8,0},{10,2},{12,4},{14,6},{1,9},{3,11}... | collective-permute-start | bytes 221192 | tf_op jit(solution)/shard_map/ppermute | solution.py:386
  21.7 6.6 %collective-permute-start.8 = (s16[144,256]{1,0:T(8,128)(2,1)S(1)}, s16[144,256]{1,0:T(8,128)(2,1)S(1)}, u32[]{:S(2)}, u32[]{:S(2)}) collective-permute-start(s16[144,256]{1,0:T(8,128)(2,1)S(1)} %get-tuple-element.18), channel_id=1, source_target_pairs={{0,12},{2,14},{4,8},{6,10},{8,4},{10,6},{12,0},{14,2},{1,13},{3,15... | collective-permute-start | bytes 221192 | tf_op jit(solution)/shard_map/ppermute | solution.py:386
  24.3 4.6 %collective-permute-start.6 = (s16[144,256]{1,0:T(8,128)(2,1)S(1)}, s16[144,256]{1,0:T(8,128)(2,1)S(1)}, u32[]{:S(2)}, u32[]{:S(2)}) collective-permute-start(s16[144,256]{1,0:T(8,128)(2,1)S(1)} %get-tuple-element.16), channel_id=1, source_target_pairs={{0,4},{2,6},{4,0},{6,2},{8,12},{10,14},{12,8},{14,10},{1,5},{3,7},... | collective-permute-start | bytes 221192 | tf_op jit(solution)/shard_map/ppermute | solution.py:386

commit v5 on v4

v5 whole, which is shorter than its diff:
```python
import functools

import jax
import jax.numpy as jnp
from jax import lax
from jax.experimental import pallas as pl
from jax.experimental.pallas import tpu as pltpu
from jax.sharding import PartitionSpec as P

VMEM = pl.BlockSpec(memory_space=pltpu.VMEM)
BF16, F32, I16, I32 = jnp.bfloat16, jnp.float32, jnp.int16, jnp.int32
FULL, STEPS = 32700.0, 64.0


def padded_16(rows):
    return -(-rows // 16) * 16


class Plan:
    def __init__(self, activity, histo_counts, blur_values):
        self.each, self.slices, self.width = activity.shape
        self.views, self.taps, _, self.band = blur_values.shape
        self.n_slab = lax.axis_size("slab")
        self.n_view = lax.axis_size("view")
        self.pairs = 2 if self.n_view % 2 == 0 else 1
        self.line = self.n_view // self.pairs
        self.block = self.each * self.slices
        self.n_edges = 2 if self.n_slab > 2 else 1
        half = self.line // 2
        stages = [s for s in (range(half, self.line), range(1, half), range(1)) if len(s)]
        self.stages = [list(s) for s in stages] if half else [[0]]
        self.messages = [[0], list(range(1, len(self.stages)))][: len(self.stages)]
        self.edge_counts = 2 * self.each
        self.edge_back = self.edge_counts + self.views * self.n_view * self.each
        self.edge_rows = self.edge_back + padded_16(self.views)
        self.bands = self.views * self.taps * self.band
        self.starts = self.bands + self.views * self.slices
        self.edge_backs = self.starts + 2 * self.views * self.taps
        need = self.edge_backs + self.n_edges * self.views
        self.param_rows = self.starts + padded_16(need - self.starts)

    def message_peers(self, m):
        return [k for s in self.messages[m] for k in self.stages[s]]

    def base(self, m):
        return 0 if m else self.param_rows

    def message_edges(self, m):
        return self.base(m) + self.views * len(self.message_peers(m)) * self.block

    def edges_each(self, m):
        return padded_16(self.views * len(self.message_peers(m)) * self.each)

    def message_rows(self, m):
        return self.message_edges(m) + self.n_edges * self.edges_each(m)

    def peer(self, at, k):
        xor = self.line & (self.line - 1) == 0
        return at ^ k if xor else (at + k) % self.line

    def across(self, k, towards):
        g = self.pairs
        moves = [(i, self.peer(i // g, k) * g + i % g) for i in range(self.n_view)]
        return moves if towards else [(j, i) for i, j in moves]

    def valid(self):
        slab = lax.axis_index("slab")
        return (slab > 0, slab < self.n_slab - 1)


def call(kernel, outs, *args, scratch=(), flops=0):
    size = lambda xs: sum(x.size * x.dtype.itemsize for x in xs)
    return pl.pallas_call(
        kernel,
        out_shape=outs,
        in_specs=[VMEM] * len(args),
        out_specs=[VMEM] * len(outs),
        scratch_shapes=list(scratch),
        compiler_params=pltpu.CompilerParams(vmem_limit_bytes=24 * 1024 * 1024),
        cost_estimate=pl.CostEstimate(
            flops=flops, bytes_accessed=size(args) + size(outs), transcendentals=0
        ),
    )(*args)


def valid_kernel(p, valid_ref):
    for high, valid in enumerate(p.valid()):
        valid_ref[high] = jnp.where(valid, jnp.ones((8, 128), F32), 0.0)


def pack_kernel(p, valid_ref, counts_ref, activity_ref, back_ref, edges_ref):
    lowest = valid_ref[0, 0:1, 0:1] == 0.0
    last = p.slices - 1
    activity = activity_ref[...].astype(F32)
    back = back_ref[...].astype(F32)
    for slot in range(p.n_edges):

        def edge(high, low):
            if p.n_edges == 2:
                return high if slot == 0 else low
            return jnp.where(lowest, high, low)

        for j in range(2):
            edges_ref[slot, j * p.each : (j + 1) * p.each] = edge(
                activity[:, last - 1 + j, :], activity[:, j, :]
            )
        for v in range(p.views):
            for r in range(p.n_view):
                at = p.edge_counts + (v * p.n_view + r) * p.each
                edges_ref[slot, at : at + p.each] = edge(
                    counts_ref[v, r, :, last, :], counts_ref[v, r, :, 0, :]
                ).astype(F32)
            edges_ref[slot, p.edge_back + v : p.edge_back + v + 1] = edge(
                back[v, last : last + 1], back[v, 0:1]
            )
        tail = p.edge_rows - p.edge_back - p.views
        if tail:
            edges_ref[slot, p.edge_back + p.views :] = jnp.zeros((tail, p.width), F32)


def send_kernel(p, edges_ref, counts_ref, activity_ref, back_ref, values_ref, starts_ref, payload_ref, *outs):
    payload_ref[: p.block] = activity_ref[...].reshape(p.block, p.width)
    for e in range(p.n_edges):
        low = p.block + e * 2 * p.each
        payload_ref[low : low + 2 * p.each] = edges_ref[e, : 2 * p.each].astype(BF16)
    out = outs[0]
    out[: p.bands] = values_ref[...].reshape(p.bands, p.width)
    out[p.bands : p.starts] = back_ref[...].reshape(p.views * p.slices, p.width)
    starts = jnp.concatenate([starts_ref[t] for t in range(p.taps)], axis=0)
    pieces = [lax.shift_right_logical(starts, 7).astype(F32), (starts & 127).astype(F32)]
    pieces += [edges_ref[e, p.edge_back : p.edge_back + p.views] for e in range(p.n_edges)]
    tail = p.param_rows - p.edge_backs - p.n_edges * p.views
    if tail:
        pieces.append(jnp.zeros((tail, p.width), F32))
    out[p.starts : p.param_rows] = jnp.concatenate(pieces, axis=0).astype(BF16)
    for m, out in enumerate(outs):
        put_counts(p, m, edges_ref, counts_ref, out)


def put_counts(p, m, edges_ref, counts_ref, out):
    at = lax.axis_index("view")
    ks = p.message_peers(m)
    rows = [p.peer(at // p.pairs, k) * p.pairs + p.pairs - 1 - at % p.pairs for k in ks]
    for v in range(p.views):
        for i, row in enumerate(rows):
            low = p.base(m) + (v * len(ks) + i) * p.block
            counts = counts_ref[v, row].astype(F32).astype(BF16)
            out[low : low + p.block] = counts.reshape(p.block, p.width)
    for e in range(p.n_edges):
        pieces = []
        for v in range(p.views):
            for row in rows:
                start = p.edge_counts + (v * p.n_view + row) * p.each
                pieces.append(edges_ref[e, pl.ds(pl.multiple_of(start, p.each), p.each), :])
        tail = p.edges_each(m) - len(pieces) * p.each
        if tail:
            pieces.append(jnp.zeros((tail, p.width), F32))
        low = p.message_edges(m) + e * p.edges_each(m)
        out[low : low + p.edges_each(m)] = jnp.concatenate(pieces, axis=0).astype(BF16)


def place_bands(values, start):
    width = values.shape[1]
    moved = jnp.concatenate([values, jnp.zeros((8, width), F32)], axis=0)
    for step in (1, 2, 4):
        moved = jnp.where((start & step) != 0, pltpu.roll(moved, step, 0), moved)
    step = 8
    while step < width:
        longer = min(moved.shape[0] + step, width)
        zeros = jnp.zeros((step, width), F32)
        down = jnp.concatenate([zeros, moved], axis=0)[:longer]
        stay = jnp.concatenate([moved, zeros], axis=0)[:longer]
        moved = jnp.where((start & step) != 0, down, stay)
        step *= 2
    return moved.astype(BF16)


def matrix_kernel(p, params_ref, *refs):
    matrix_ref = refs[-1]
    starts = params_ref[p.starts : p.param_rows].astype(F32).astype(I32)
    n = p.views * p.taps
    starts = starts[:n] * 128 + starts[n : 2 * n]
    for v in range(p.views):
        for t in range(p.taps):
            at = v * p.taps + t
            values = params_ref[at * p.band : (at + 1) * p.band].astype(F32)
            at = t * p.views + v
            matrix_ref[v, t] = place_bands(values, starts[at : at + 1])


def place_source(p, blocks, lifted_ref, source_ref):
    rows = len(blocks) * p.each
    for i, block_ref in enumerate(blocks):
        low = i * p.each
        lifted_ref[low : low + p.each, 8 : 8 + p.slices, :] = (
            block_ref[: p.block].astype(F32).reshape(p.each, p.slices, p.width)
        )
        edges = block_ref[p.block :].astype(F32)
        for high, valid in enumerate(p.valid()):
            for j in range(2):
                at = (2 * min(high, p.n_edges - 1) + j) * p.each
                lifted_ref[low : low + p.each, (8 + p.slices if high else 6) + j, :] = jnp.where(
                    valid, edges[at : at + p.each], 0.0
                )
    main = rows * p.slices
    for t in range(p.taps):
        source_ref[t, :main] = (
            lifted_ref[:, 7 + t : 7 + t + p.slices, :].astype(BF16).reshape(main, p.width)
        )
        source_ref[t, main:] = jnp.concatenate(
            [lifted_ref[:, 6 + t, :], lifted_ref[:, 7 + p.slices + t, :]], axis=0
        ).astype(BF16)


class Rows:
    def __init__(self, p, stage, source_ref, ratio_ref, up_ref, down_ref):
        self.p, self.source_ref, self.ratio_ref, self.views = p, source_ref, ratio_ref, []
        self.up_ref, self.down_ref = up_ref, down_ref
        self.rows = len(p.stages[stage]) * p.each
        self.main, self.full = self.rows * p.slices, self.rows * (p.slices + 2)

    def view(self, matrix_ref, v, counts, back, edges, edge_backs):
        p, rows, main = self.p, self.rows, self.main
        expected = None
        for t in range(p.taps):
            term = jnp.dot(self.source_ref[t], matrix_ref[v, t], preferred_element_type=F32)
            expected = term if expected is None else expected + term
        inner = expected[:main].reshape(rows, p.slices, p.width) + back[None]
        ratio = counts.astype(F32).reshape(rows, p.slices, p.width) / inner - 1.0
        n = len(self.views)
        self.ratio_ref[n, :main] = ratio.astype(BF16).reshape(main, p.width)
        outer = []
        for high, valid in enumerate(p.valid()):
            low = main + high * rows
            e = min(high, p.n_edges - 1)
            ratio = edges[e] / (expected[low : low + rows] + edge_backs[e]) - 1.0
            outer.append(jnp.where(valid, ratio, 0.0))
        self.ratio_ref[n, main:] = jnp.concatenate(outer, axis=0).astype(BF16)
        self.views.append((matrix_ref, v))

    def project(self, tap, stop):
        total = None
        for n, (matrix_ref, v) in enumerate(self.views):
            term = lax.dot_general(
                self.ratio_ref[n, :stop],
                matrix_ref[v, tap],
                (((1,), (1,)), ((), ())),
                preferred_element_type=F32,
            )
            total = term if total is None else total + term
        return total

    def gradient(self):
        p, rows, main, full = self.p, self.rows, self.main, self.full
        shape = (rows, p.slices, p.width)
        part = self.project(0, full)
        self.up_ref[:, : p.slices, :] = part[:main].reshape(shape)
        self.up_ref[:, p.slices, :] = part[main + rows :]
        part = self.project(2, full)
        self.down_ref[:, 8 : 8 + p.slices, :] = part[:main].reshape(shape)
        self.down_ref[:, 7, :] = part[main : main + rows]
        total = self.project(1, main).reshape(shape)
        return total + self.up_ref[:, 1 : 1 + p.slices, :] + self.down_ref[:, 7 : 7 + p.slices, :]


def own_kernel(p, stage, counts_ref, edges_ref, back_ref, matrix_ref, *refs):
    ks = p.stages[stage]
    blocks, refs = refs[: len(ks)], refs[len(ks) :]
    refs = refs[min(stage, 1) :]
    source_ref, total_ref, lifted_ref, *scratch = refs
    place_source(p, blocks, lifted_ref, source_ref)
    work = Rows(p, stage, source_ref, *scratch)
    at = lax.axis_index("view")
    places = [p.peer(at // p.pairs, k) * p.pairs + at % p.pairs for k in ks]
    for v in range(p.views):
        edges, edge_backs = [], []
        for e in range(p.n_edges):
            pieces = []
            for row in places:
                start = p.edge_counts + (v * p.n_view + row) * p.each
                pieces.append(edges_ref[e, pl.ds(pl.multiple_of(start, p.each), p.each), :])
            edges.append(jnp.concatenate(pieces, axis=0))
            edge_backs.append(edges_ref[e, p.edge_back + v : p.edge_back + v + 1])
        counts = jnp.concatenate([counts_ref[v, row] for row in places], axis=0)
        work.view(matrix_ref, v, counts, back_ref[v].astype(F32), edges, edge_backs)
    total_ref[...] = work.gradient()


def their_kernel(p, stage, after, source_ref, total_ref, *refs):
    ks = p.stages[stage]
    refs = refs[after:]
    total = total_ref[...]
    if p.pairs == 2:
        (message_ref, first_ref, matrix_ref), refs = refs[:3], refs[3:]
    outs, scratch = refs[: len(ks)], refs[len(ks) :]
    if p.pairs == 2:
        work = Rows(p, stage, source_ref, *scratch)
        (m,) = [m for m, stages in enumerate(p.messages) if stage in stages]
        peers = p.message_peers(m)
        skip = peers.index(ks[0])
        last = first_ref[p.starts : p.param_rows].astype(F32)
        came = []
        for e in range(p.n_edges):
            low = p.message_edges(m) + e * p.edges_each(m)
            came.append(message_ref[low : low + p.edges_each(m)].astype(F32))
        for v in range(p.views):
            low = (v * len(peers) + skip) * p.each
            edges = [x[low : low + work.rows] for x in came]
            low = p.edge_backs - p.starts + v
            edge_backs = [
                last[low + e * p.views : low + e * p.views + 1] for e in range(p.n_edges)
            ]
            low = p.base(m) + (v * len(peers) + skip) * p.block
            back = first_ref[p.bands + v * p.slices : p.bands + (v + 1) * p.slices].astype(F32)
            counts = message_ref[low : low + work.main]
            work.view(matrix_ref, v, counts, back, edges, edge_backs)
        total = total + work.gradient()
    for i, out in enumerate(outs):
        part = total[i * p.each : (i + 1) * p.each]
        if ks[i] == 0:
            out[...] = part
        else:
            encode(p, part, out)


def encode(p, x, out_ref):
    most = jnp.maximum(jnp.max(jnp.abs(x), axis=1), 1e-30)
    power = jnp.ceil(jnp.log2(most) * STEPS)
    codes = jnp.round(x * (FULL * jnp.exp2(power * (-1.0 / STEPS)))[:, None, :])
    out_ref[: p.block] = codes.reshape(p.block, p.width).astype(I32).astype(I16)
    tail = padded_16(p.each) - p.each
    if tail:
        power = jnp.concatenate([power, jnp.zeros((tail, p.width), F32)], axis=0)
    out_ref[p.block :] = power.astype(I32).astype(I16)


def decode(p, in_ref):
    power = in_ref[p.block :].astype(I32).astype(F32)[: p.each]
    scale = jnp.exp2(power * (1.0 / STEPS)) * (1.0 / FULL)
    codes = in_ref[: p.block].astype(I32).astype(F32)
    return codes.reshape(p.each, p.slices, p.width) * scale[:, None, :]


def sum_kernel(p, coded, *refs):
    total = None
    for i, ref in enumerate(refs[:-1]):
        term = decode(p, ref) if i < coded else ref[...]
        total = term if total is None else total + term
    refs[-1][...] = total


def per_device(activity, histo_counts, background, blur_values, band_start):
    p = Plan(activity, histo_counts, blur_values)
    shape = jax.ShapeDtypeStruct
    part = lambda kernel, *static: functools.partial(kernel, p, *static)
    width = p.width
    other = [(i, i ^ 1) for i in range(p.n_view)]

    counts = histo_counts.reshape(p.views, p.n_view, p.each, p.slices, width)
    values = jnp.swapaxes(blur_values, 2, 3)
    starts = jnp.swapaxes(band_start, 0, 1)
    (valid,) = call(part(valid_kernel), [shape((2, 8, 128), F32)], flops=2 * 10**9)
    (edges,) = call(
        part(pack_kernel),
        [shape((p.n_edges, p.edge_rows, width), F32)],
        valid, counts, activity, background,
    )
    if p.n_slab == 2:
        edges = lax.ppermute(edges, "slab", [(0, 1), (1, 0)])
    elif p.n_slab > 2:
        up = [(i, i + 1) for i in range(p.n_slab - 1)]
        down = [(j, i) for i, j in up]
        edges = jnp.stack([lax.ppermute(edges[0], "slab", up), lax.ppermute(edges[1], "slab", down)])
    outs = [shape((p.block + 2 * p.n_edges * p.each, width), BF16)]
    outs += [shape((p.message_rows(m), width), BF16) for m in range(len(p.messages))]
    payload, *sent = call(
        part(send_kernel), outs, edges, counts, activity, background, values, starts
    )
    theirs = [lax.ppermute(x, "view", other) for x in sent] if p.pairs == 2 else []
    blocks = {0: payload}
    for k in [k for ks in p.stages for k in ks if k]:
        blocks[k] = lax.ppermute(payload, "view", p.across(k, False))

    matrices = shape((p.views, p.taps, width, width), BF16)
    (matrix,) = call(part(matrix_kernel), [matrices], sent[0])
    own = []
    for stage, ks in enumerate(p.stages):
        rows = len(ks) * p.each
        full = rows * (p.slices + 2)
        scratch = [
            pltpu.VMEM((p.views, full, width), BF16),
            pltpu.VMEM((rows, p.slices + 8, width), F32),
            pltpu.VMEM((rows, p.slices + 8, width), F32),
        ]
        own.append(
            call(
                part(own_kernel, stage),
                [
                    shape((p.taps, full, width), BF16),
                    shape((rows, p.slices, width), F32),
                ],
                counts, edges, background, matrix, *[blocks[k] for k in ks],
                *[blocks[p.stages[0][-1]]][: min(stage, 1)],
                scratch=[pltpu.VMEM((rows, p.slices + 16, width), F32)] + scratch,
                flops=4 * p.views * p.taps * full * width * width,
            )
        )
    if p.pairs == 2:
        (their_matrix,) = call(part(matrix_kernel), [matrices], theirs[0])

    code = shape((p.block + padded_16(p.each), width), I16)
    plain = shape((p.each, p.slices, width), F32)
    terms = {}
    for stage, ks in enumerate(p.stages):
        rows = len(ks) * p.each
        full = rows * (p.slices + 2)
        before = list(terms.values())[-1:]
        args = [*own[stage], *before]
        if p.pairs == 2:
            (m,) = [m for m, stages in enumerate(p.messages) if stage in stages]
            args += [theirs[m], theirs[0], their_matrix]
        outs = call(
            part(their_kernel, stage, len(before)),
            [code if k else plain for k in ks],
            *args,
            scratch=[
                pltpu.VMEM((p.views, full, width), BF16),
                pltpu.VMEM((rows, p.slices + 8, width), F32),
                pltpu.VMEM((rows, p.slices + 8, width), F32),
            ],
            flops=4 * p.views * p.taps * full * width * width,
        )
        terms.update(zip(ks, outs))
    total = []
    for m in range(len(p.messages)):
        came = [
            lax.ppermute(terms[k], "view", p.across(k, True)) for k in p.message_peers(m) if k
        ]
        if m == len(p.messages) - 1:
            total = total + [terms[0]]
        total = list(call(part(sum_kernel, len(came)), [plain], *came, *total))
    return total[0]


def solution(mesh):
    placed = (
        P(("parts", "view"), "slab", None),
        P(("parts", "view"), None, "slab", None),
        P(("parts", "view"), "slab", None),
        P("view", None, None, None),
        P("view", None, None),
    )
    return jax.shard_map(
        per_device,
        mesh=mesh,
        in_specs=placed,
        out_specs=P(("parts", "view"), "slab", None),
        check_vma=False,
    )
```

time: 29.7 us -> 28.7 us (0.966)
  waiting for transfers between devices: 10.3 us -> 8.03 us
  Pallas kernels: 4.01 us -> 5.54 us
  starting transfers between devices: 13.6 us -> 13.3 us
    ppermute x2, waiting for transfers between devices: 5.57 us -> 0.01 us  [per_device(): lax.ppermute(x, 'view', other)]
    ppermute x6, waiting for transfers between devices: 3.68 us -> 7 us  [the longest x3 4.82 us: per_device(): blocks[k] = lax.ppermute(payload, 'view', p.across(k, False))]
    pallas_call x9 -> x13, Pallas kernels: 4.01 us -> 5.54 us  [call(): pl.pallas_call(kernel, out_shape=outs, in_specs=[VMEM] * len(args), out_s...]
    ppermute x6, starting transfers between devices: 10.1 us -> 9.74 us  [the longest x3 5.14 us: per_device(): lax.ppermute(terms[k], 'view', p.across(k, True))]
  transfers between devices with their start and end apart: 9 -> 9, of which waited for: 5 -> 6; matrix products, arithmetic and copies ran while one was open for 0% -> 0% of each run, Pallas kernels for 11% -> 16%
where the time goes in v5:
time: 28.7 us; the launch traced here: 28.5 us
  starting transfers between devices  13.3 us (46%)
  waiting for transfers between devices  8.03 us (28%)
  Pallas kernels  5.54 us (19%)
  local copies, waits for them, and re-layouts  1.58 us (6%)
    pallas_call x13, Pallas kernels, call(): pl.pallas_call(kernel, out_shape=outs, in_specs=[VMEM] * len(args), out_s...  5.54 us
    ppermute x3, starting transfers between devices, per_device(): lax.ppermute(terms[k], 'view', p.across(k, True))  5.14 us
    ppermute x3, waiting for transfers between devices, per_device(): blocks[k] = lax.ppermute(payload, 'view', p.across(k, False))  4.82 us
    ppermute x3, starting transfers between devices, per_device(): blocks[k] = lax.ppermute(payload, 'view', p.across(k, False))  4.6 us
    ppermute x2, starting transfers between devices, per_device(): lax.ppermute(x, 'view', other)  3.02 us
    ppermute x3, waiting for transfers between devices, per_device(): lax.ppermute(terms[k], 'view', p.across(k, True))  2.18 us
    unnamed x10, local copies, waits for them, and re-layouts  1.58 us
    ppermute x1, waiting for transfers between devices, per_device(): edges = lax.ppermute(edges, 'slab', [(0, 1), (1, 0)])  1.03 us
  transfers between devices with their start and end apart: 9, of which 6 were waited for; matrix products, arithmetic and copies ran while one was open for 0% of the time, Pallas kernels for 16%

profile of v5, /device:TPU:0, one launch (start us, length us, event | category | flops | bytes accessed | tf_op | source)
XLA Modules:
  0.0 28.5 jit_solution(5083503063288194543)
XLA Ops:
  0.0 0.0 copy-start.3
  0.0 0.0 copy-start.4
  0.0 1.6 %copy-done = s32[2,64,16,256]{3,2,1,0:T(8,128)S(1)} copy-done((s32[2,64,16,256]{3,2,1,0:T(8,128)S(1)}, s32[2,64,16,256]{3,2,1,0:T(8,128)}, u32[]{:S(2)}) %copy-start) | copy-done | bytes 2097176
  1.6 0.1 shard_map.56
  1.7 0.5 %collective-permute-start = (f32[1,160,256]{2,1,0:T(8,128)S(1)}, f32[1,160,256]{2,1,0:T(8,128)S(1)}, u32[]{:S(2)}, u32[]{:S(2)}) collective-permute-start(f32[1,160,256]{2,1,0:T(8,128)S(1)} %shard_map.56), channel_id=1, source_target_pairs={{0,1},{1,0},{2,3},{3,2},{4,5},{5,4},{6,7},{7,6},{8,9},{9,8},{10,11... | collective-permute-start | bytes 491528 | tf_op jit(solution)/shard_map/ppermute | solution.py:369
  2.2 1.0 %collective-permute-done.edges_ref = f32[1,160,256]{2,1,0:T(8,128)S(1)} collective-permute-done((f32[1,160,256]{2,1,0:T(8,128)S(1)}, f32[1,160,256]{2,1,0:T(8,128)S(1)}, u32[]{:S(2)}, u32[]{:S(2)}) %collective-permute-start) | collective-permute-done | bytes 163872 | tf_op jit(solution)/shard_map/ppermute | solution.py:369
  3.3 0.1 shard_map.57
  3.4 2.9 %collective-permute-start.4 = (bf16[784,256]{1,0:T(8,128)(2,1)S(1)}, bf16[784,256]{1,0:T(8,128)(2,1)S(1)}, u32[]{:S(2)}, u32[]{:S(2)}) collective-permute-start(bf16[784,256]{1,0:T(8,128)(2,1)S(1)} %get-tuple-element.16.params_ref), channel_id=1, source_target_pairs={{0,2},{2,0},{4,6},{6,4},{8,10},{10,8},{12,14},{14,12},{1,3},{3,1},... | collective-permute-start | bytes 1204232 | tf_op jit(solution)/shard_map/ppermute | solution.py:379
  6.3 0.1 collective-permute-start.5
  6.4 4.0 %collective-permute-start.2 = (bf16[144,256]{1,0:T(8,128)(2,1)S(1)}, bf16[144,256]{1,0:T(8,128)(2,1)S(1)}, u32[]{:S(2)}, u32[]{:S(2)}) collective-permute-start(bf16[144,256]{1,0:T(8,128)(2,1)S(1)} %get-tuple-element.17.refs_0_), channel_id=1, source_target_pairs={{12,0},{14,2},{8,4},{10,6},{4,8},{6,10},{0,12},{2,14},{13,1},{15,3... | collective-permute-start | bytes 221192 | tf_op jit(solution)/shard_map/ppermute | solution.py:382
  10.4 0.0 collective-permute-start.1
  10.4 0.6 %collective-permute-start.3 = (bf16[144,256]{1,0:T(8,128)(2,1)S(1)}, bf16[144,256]{1,0:T(8,128)(2,1)S(1)}, u32[]{:S(2)}, u32[]{:S(2)}) collective-permute-start(bf16[144,256]{1,0:T(8,128)(2,1)S(1)} %get-tuple-element.17.refs_0_), channel_id=1, source_target_pairs={{8,0},{10,2},{12,4},{14,6},{0,8},{2,10},{4,12},{6,14},{9,1},{11,3}... | collective-permute-start | bytes 221192 | tf_op jit(solution)/shard_map/ppermute | solution.py:382
  11.0 0.3 shard_map.58.matrix_ref
  11.3 2.0 %collective-permute-done.2.refs_1_ = bf16[144,256]{1,0:T(8,128)(2,1)S(1)} collective-permute-done((bf16[144,256]{1,0:T(8,128)(2,1)S(1)}, bf16[144,256]{1,0:T(8,128)(2,1)S(1)}, u32[]{:S(2)}, u32[]{:S(2)}) %collective-permute-start.2) | collective-permute-done | bytes 73760 | tf_op jit(solution)/shard_map/ppermute | solution.py:382
  13.3 2.8 %collective-permute-done.1.refs_0_ = bf16[144,256]{1,0:T(8,128)(2,1)S(1)} collective-permute-done((bf16[144,256]{1,0:T(8,128)(2,1)S(1)}, bf16[144,256]{1,0:T(8,128)(2,1)S(1)}, u32[]{:S(2)}, u32[]{:S(2)}) %collective-permute-start.1) | collective-permute-done | bytes 73760 | tf_op jit(solution)/shard_map/ppermute | solution.py:382
  16.1 0.6 %shard_map.59 = (bf16[3,144,256]{2,1,0:T(8,128)(2,1)S(1)}, f32[8,16,256]{2,1,0:T(8,128)S(1)}) custom-call(s32[2,8,8,16,256]{4,3,2,1,0:T(8,128)S(1)} %bitcast.5, f32[1,160,256]{2,1,0:T(8,128)S(1)} %collective-permute-done.edges_ref, bf16[2,16,256]{2,1,0:T(8,128)(2,1)S(1)} %copy-done.1, bf16[2,3,256,256]{3,2,1,0:T(8,128)(2,1)S(1)} %shard_map.58.matrix_ref, ...), custom_call_target="tpu_custom_call" | custom-call | flops 226492416 | bytes 3563520 | tf_op jit(solution)/shard_map/pallas_call | solution.py:73
  16.7 0.0 collective-permute-done.3.refs_0_
  16.7 0.7 %shard_map.60 = (bf16[3,288,256]{2,1,0:T(8,128)(2,1)S(1)}, f32[16,16,256]{2,1,0:T(8,128)S(1)}) custom-call(s32[2,8,8,16,256]{4,3,2,1,0:T(8,128)S(1)} %bitcast.6, f32[1,160,256]{2,1,0:T(8,128)S(1)} %collective-permute-done.edges_ref, bf16[2,16,256]{2,1,0:T(8,128)(2,1)S(1)} %copy-done.1, bf16[2,3,256,256]{3,2,1,0:T(8,128)(2,1)S(1)} %shard_map.58.matrix_ref, ...), custom_call_target="tpu_custom_call" | custom-call | flops 452984832 | bytes 3915776 | tf_op jit(solution)/shard_map/pallas_call | solution.py:73
  17.5 0.0 collective-permute-done.4.params_ref.refs_0_.refs_1_.refs_2_
  17.5 0.3 %shard_map.61.refs_2_.refs_3_ = bf16[2,3,256,256]{3,2,1,0:T(8,128)(2,1)S(1)} custom-call(bf16[784,256]{1,0:T(8,128)(2,1)S(1)} %collective-permute-done.4.params_ref.refs_0_.refs_1_.refs_2_), custom_call_target="tpu_custom_call" | custom-call | bytes 1187840 | tf_op jit(solution)/shard_map/pallas_call | solution.py:73
  17.8 0.8 %shard_map.62 = (s16[144,256]{1,0:T(8,128)(2,1)S(1)}, s16[144,256]{1,0:T(8,128)(2,1)S(1)}) custom-call(bf16[3,288,256]{2,1,0:T(8,128)(2,1)S(1)} %get-tuple-element.20.source_ref, f32[16,16,256]{2,1,0:T(8,128)S(1)} %get-tuple-element.21.total_ref, bf16[784,256]{1,0:T(8,128)(2,1)S(1)} %collective-permute-done.4.params_ref.refs_0_.refs_1_.refs_2_, ...), custom_call_target="tpu_custom_call" | custom-call | flops 452984832 | bytes 2441216 | tf_op jit(solution)/shard_map/pallas_call | solution.py:73
  18.6 2.1 %collective-permute-start.7 = (s16[144,256]{1,0:T(8,128)(2,1)S(1)}, s16[144,256]{1,0:T(8,128)(2,1)S(1)}, u32[]{:S(2)}, u32[]{:S(2)}) collective-permute-start(s16[144,256]{1,0:T(8,128)(2,1)S(1)} %get-tuple-element.24), channel_id=1, source_target_pairs={{0,8},{2,10},{4,12},{6,14},{8,0},{10,2},{12,4},{14,6},{1,9},{3,11}... | collective-permute-start | bytes 221192 | tf_op jit(solution)/shard_map/ppermute | solution.py:437
  20.7 1.3 %collective-permute-start.8 = (s16[144,256]{1,0:T(8,128)(2,1)S(1)}, s16[144,256]{1,0:T(8,128)(2,1)S(1)}, u32[]{:S(2)}, u32[]{:S(2)}) collective-permute-start(s16[144,256]{1,0:T(8,128)(2,1)S(1)} %get-tuple-element.22.refs_0_), channel_id=1, source_target_pairs={{0,12},{2,14},{4,8},{6,10},{8,4},{10,6},{12,0},{14,2},{1,13},{3,15... | collective-permute-start | bytes 221192 | tf_op jit(solution)/shard_map/ppermute | solution.py:437
  22.0 0.0 collective-permute-done.5.refs_1_
  22.0 0.6 %shard_map.63.refs_0_ = s16[144,256]{1,0:T(8,128)(2,1)S(1)} custom-call(bf16[3,144,256]{2,1,0:T(8,128)(2,1)S(1)} %get-tuple-element.18.source_ref, f32[8,16,256]{2,1,0:T(8,128)S(1)} %get-tuple-element.19.total_ref, s16[144,256]{1,0:T(8,128)(2,1)S(1)} %get-tuple-element.22.refs_0_, bf16[544,256]{1,0:T(8,128)(2,1)S(1)} %collective-permute-done.5.refs_1_, ...), custom_call_target="tpu_custom_call" | custom-call | flops 226492416 | bytes 1966080 | tf_op jit(solution)/shard_map/pallas_call | solution.py:73
  22.7 1.7 %collective-permute-start.6 = (s16[144,256]{1,0:T(8,128)(2,1)S(1)}, s16[144,256]{1,0:T(8,128)(2,1)S(1)}, u32[]{:S(2)}, u32[]{:S(2)}) collective-permute-start(s16[144,256]{1,0:T(8,128)(2,1)S(1)} %shard_map.63.refs_0_), channel_id=1, source_target_pairs={{0,4},{2,6},{4,0},{6,2},{8,12},{10,14},{12,8},{14,10},{1,5},{3,7},... | collective-permute-start | bytes 221192 | tf_op jit(solution)/shard_map/ppermute | solution.py:437
  24.4 0.6 %shard_map.65 = (bf16[3,144,256]{2,1,0:T(8,128)(2,1)S(1)}, f32[8,16,256]{2,1,0:T(8,128)S(1)}) custom-call(s32[2,8,8,16,256]{4,3,2,1,0:T(8,128)S(1)} %bitcast.7, f32[1,160,256]{2,1,0:T(8,128)S(1)} %collective-permute-done.edges_ref, bf16[2,16,256]{2,1,0:T(8,128)(2,1)S(1)} %copy-done.1, bf16[2,3,256,256]{3,2,1,0:T(8,128)(2,1)S(1)} %shard_map.58.matrix_ref, ...), custom_call_target="tpu_custom_call" | custom-call | flops 226492416 | bytes 3563520 | tf_op jit(solution)/shard_map/pallas_call | solution.py:73
  25.0 0.6 %shard_map.66.refs_2_ = f32[8,16,256]{2,1,0:T(8,128)S(1)} custom-call(bf16[3,144,256]{2,1,0:T(8,128)(2,1)S(1)} %get-tuple-element.25.source_ref, f32[8,16,256]{2,1,0:T(8,128)S(1)} %get-tuple-element.26.total_ref, s16[144,256]{1,0:T(8,128)(2,1)S(1)} %shard_map.63.refs_0_, bf16[544,256]{1,0:T(8,128)(2,1)S(1)} %collective-permute-done.5.refs_1_, ...), custom_call_target="tpu_custom_call" | custom-call | flops 226492416 | bytes 2023424 | tf_op jit(solution)/shard_map/pallas_call | solution.py:73
  25.6 0.2 collective-permute-done.7.refs_0_
  25.9 1.1 %collective-permute-done.8.refs_1_ = s16[144,256]{1,0:T(8,128)(2,1)S(1)} collective-permute-done((s16[144,256]{1,0:T(8,128)(2,1)S(1)}, s16[144,256]{1,0:T(8,128)(2,1)S(1)}, u32[]{:S(2)}, u32[]{:S(2)}) %collective-permute-start.8) | collective-permute-done | bytes 73760 | tf_op jit(solution)/shard_map/ppermute | solution.py:437
  27.1 0.8 %collective-permute-done.6.refs_0_ = s16[144,256]{1,0:T(8,128)(2,1)S(1)} collective-permute-done((s16[144,256]{1,0:T(8,128)(2,1)S(1)}, s16[144,256]{1,0:T(8,128)(2,1)S(1)}, u32[]{:S(2)}, u32[]{:S(2)}) %collective-permute-start.6) | collective-permute-done | bytes 73760 | tf_op jit(solution)/shard_map/ppermute | solution.py:437
  27.9 0.7 %shard_map.67 = f32[8,16,256]{2,1,0:T(8,128)} custom-call(s16[144,256]{1,0:T(8,128)(2,1)S(1)} %collective-permute-done.6.refs_0_, f32[8,16,256]{2,1,0:T(8,128)S(1)} %shard_map.64.refs_1_, f32[8,16,256]{2,1,0:T(8,128)S(1)} %shard_map.66.refs_2_), custom_call_target="tpu_custom_call" | custom-call | bytes 466944 | tf_op jit(solution)/shard_map/pallas_call | solution.py:73
  (9 shorter events, 0.1 us)
Async XLA Ops:
  0.0 1.6 %copy-start = (s32[2,64,16,256]{3,2,1,0:T(8,128)S(1)}, s32[2,64,16,256]{3,2,1,0:T(8,128)}, u32[]{:S(2)}) copy-start(s32[2,64,16,256]{3,2,1,0:T(8,128)} %param.6) | copy-start | bytes 6291460
  0.0 1.6 %copy-start.2 = (bf16[8,16,256]{2,1,0:T(8,128)(2,1)S(1)}, bf16[8,16,256]{2,1,0:T(8,128)(2,1)}, u32[]{:S(2)}) copy-start(bf16[8,16,256]{2,1,0:T(8,128)(2,1)} %activity_ref.3) | copy-start | bytes 196612
  0.0 1.6 %copy-start.1 = (bf16[2,16,256]{2,1,0:T(8,128)(2,1)S(1)}, bf16[2,16,256]{2,1,0:T(8,128)(2,1)}, u32[]{:S(2)}) copy-start(bf16[2,16,256]{2,1,0:T(8,128)(2,1)} %back_ref.9) | copy-start | bytes 49156
  0.0 3.3 %copy-start.3 = (bf16[2,3,256,32]{2,3,1,0:T(8,128)(2,1)S(1)}, bf16[2,3,256,32]{2,3,1,0:T(8,128)(2,1)}, u32[]{:S(2)}) copy-start(bf16[2,3,256,32]{2,3,1,0:T(8,128)(2,1)} %param.8) | copy-start | bytes 294916
  0.0 3.3 %copy-start.4 = (s32[2,3,256]{2,0,1:T(2,128)S(1)}, s32[2,3,256]{2,0,1:T(2,128)}, u32[]{:S(2)}) copy-start(s32[2,3,256]{2,0,1:T(2,128)} %param.9) | copy-start | bytes 18436
  1.7 1.5 %collective-permute-start = (f32[1,160,256]{2,1,0:T(8,128)S(1)}, f32[1,160,256]{2,1,0:T(8,128)S(1)}, u32[]{:S(2)}, u32[]{:S(2)}) collective-permute-start(f32[1,160,256]{2,1,0:T(8,128)S(1)} %shard_map.56), channel_id=1, source_target_pairs={{0,1},{1,0},{2,3},{3,2},{4,5},{5,4},{6,7},{7,6},{8,9},{9,8},{10,11... | collective-permute-start | bytes 491528 | tf_op jit(solution)/shard_map/ppermute | solution.py:369
  3.4 14.1 %collective-permute-start.4 = (bf16[784,256]{1,0:T(8,128)(2,1)S(1)}, bf16[784,256]{1,0:T(8,128)(2,1)S(1)}, u32[]{:S(2)}, u32[]{:S(2)}) collective-permute-start(bf16[784,256]{1,0:T(8,128)(2,1)S(1)} %get-tuple-element.16.params_ref), channel_id=1, source_target_pairs={{0,2},{2,0},{4,6},{6,4},{8,10},{10,8},{12,14},{14,12},{1,3},{3,1},... | collective-permute-start | bytes 1204232 | tf_op jit(solution)/shard_map/ppermute | solution.py:379
  6.3 15.7 %collective-permute-start.5 = (bf16[544,256]{1,0:T(8,128)(2,1)S(1)}, bf16[544,256]{1,0:T(8,128)(2,1)S(1)}, u32[]{:S(2)}, u32[]{:S(2)}) collective-permute-start(bf16[544,256]{1,0:T(8,128)(2,1)S(1)} %get-tuple-element.23), channel_id=1, source_target_pairs={{0,2},{2,0},{4,6},{6,4},{8,10},{10,8},{12,14},{14,12},{1,3},{3,1},... | collective-permute-start | bytes 835592 | tf_op jit(solution)/shard_map/ppermute | solution.py:379
  6.4 6.9 %collective-permute-start.2 = (bf16[144,256]{1,0:T(8,128)(2,1)S(1)}, bf16[144,256]{1,0:T(8,128)(2,1)S(1)}, u32[]{:S(2)}, u32[]{:S(2)}) collective-permute-start(bf16[144,256]{1,0:T(8,128)(2,1)S(1)} %get-tuple-element.17.refs_0_), channel_id=1, source_target_pairs={{12,0},{14,2},{8,4},{10,6},{4,8},{6,10},{0,12},{2,14},{13,1},{15,3... | collective-permute-start | bytes 221192 | tf_op jit(solution)/shard_map/ppermute | solution.py:382
  10.4 5.7 %collective-permute-start.1 = (bf16[144,256]{1,0:T(8,128)(2,1)S(1)}, bf16[144,256]{1,0:T(8,128)(2,1)S(1)}, u32[]{:S(2)}, u32[]{:S(2)}) collective-permute-start(bf16[144,256]{1,0:T(8,128)(2,1)S(1)} %get-tuple-element.17.refs_0_), channel_id=1, source_target_pairs={{4,0},{6,2},{0,4},{2,6},{12,8},{14,10},{8,12},{10,14},{5,1},{7,3},... | collective-permute-start | bytes 221192 | tf_op jit(solution)/shard_map/ppermute | solution.py:382
  10.4 6.3 %collective-permute-start.3 = (bf16[144,256]{1,0:T(8,128)(2,1)S(1)}, bf16[144,256]{1,0:T(8,128)(2,1)S(1)}, u32[]{:S(2)}, u32[]{:S(2)}) collective-permute-start(bf16[144,256]{1,0:T(8,128)(2,1)S(1)} %get-tuple-element.17.refs_0_), channel_id=1, source_target_pairs={{8,0},{10,2},{12,4},{14,6},{0,8},{2,10},{4,12},{6,14},{9,1},{11,3}... | collective-permute-start | bytes 221192 | tf_op jit(solution)/shard_map/ppermute | solution.py:382
  18.6 7.3 %collective-permute-start.7 = (s16[144,256]{1,0:T(8,128)(2,1)S(1)}, s16[144,256]{1,0:T(8,128)(2,1)S(1)}, u32[]{:S(2)}, u32[]{:S(2)}) collective-permute-start(s16[144,256]{1,0:T(8,128)(2,1)S(1)} %get-tuple-element.24), channel_id=1, source_target_pairs={{0,8},{2,10},{4,12},{6,14},{8,0},{10,2},{12,4},{14,6},{1,9},{3,11}... | collective-permute-start | bytes 221192 | tf_op jit(solution)/shard_map/ppermute | solution.py:437
  20.7 6.3 %collective-permute-start.8 = (s16[144,256]{1,0:T(8,128)(2,1)S(1)}, s16[144,256]{1,0:T(8,128)(2,1)S(1)}, u32[]{:S(2)}, u32[]{:S(2)}) collective-permute-start(s16[144,256]{1,0:T(8,128)(2,1)S(1)} %get-tuple-element.22.refs_0_), channel_id=1, source_target_pairs={{0,12},{2,14},{4,8},{6,10},{8,4},{10,6},{12,0},{14,2},{1,13},{3,15... | collective-permute-start | bytes 221192 | tf_op jit(solution)/shard_map/ppermute | solution.py:437
  22.7 5.2 %collective-permute-start.6 = (s16[144,256]{1,0:T(8,128)(2,1)S(1)}, s16[144,256]{1,0:T(8,128)(2,1)S(1)}, u32[]{:S(2)}, u32[]{:S(2)}) collective-permute-start(s16[144,256]{1,0:T(8,128)(2,1)S(1)} %shard_map.63.refs_0_), channel_id=1, source_target_pairs={{0,4},{2,6},{4,0},{6,2},{8,12},{10,14},{12,8},{14,10},{1,5},{3,7},... | collective-permute-start | bytes 221192 | tf_op jit(solution)/shard_map/ppermute | solution.py:437

commit v6 on v5

--- a/solution.py
+++ b/solution.py
@@ -9,6 +9,7 @@
 
 VMEM = pl.BlockSpec(memory_space=pltpu.VMEM)
 BF16, F32, I16, I32 = jnp.bfloat16, jnp.float32, jnp.int16, jnp.int32
+LONG = 8 * 10**9
 FULL, STEPS = 32700.0, 64.0
 
 
@@ -35,9 +36,10 @@
         self.edge_rows = self.edge_back + padded_16(self.views)
         self.bands = self.views * self.taps * self.band
         self.starts = self.bands + self.views * self.slices
-        self.edge_backs = self.starts + 2 * self.views * self.taps
-        need = self.edge_backs + self.n_edges * self.views
-        self.param_rows = self.starts + padded_16(need - self.starts)
+        self.param_rows = self.starts + padded_16(2 * self.views * self.taps)
+        self.order = [k for s in self.stages for k in s]
+        self.early_back = self.views * self.line * self.each
+        self.early_rows = padded_16(self.early_back + self.views)
 
     def message_peers(self, m):
         return [k for s in self.messages[m] for k in self.stages[s]]
@@ -45,14 +47,8 @@
     def base(self, m):
         return 0 if m else self.param_rows
 
-    def message_edges(self, m):
+    def message_rows(self, m):
         return self.base(m) + self.views * len(self.message_peers(m)) * self.block
-
-    def edges_each(self, m):
-        return padded_16(self.views * len(self.message_peers(m)) * self.each)
-
-    def message_rows(self, m):
-        return self.message_edges(m) + self.n_edges * self.edges_each(m)
 
     def peer(self, at, k):
         xor = self.line & (self.line - 1) == 0
@@ -86,6 +82,12 @@
 def valid_kernel(p, valid_ref):
     for high, valid in enumerate(p.valid()):
         valid_ref[high] = jnp.where(valid, jnp.ones((8, 128), F32), 0.0)
+
+
+def edge_of(p, valid_ref, slot, high, low):
+    if p.n_edges == 2:
+        return high if slot == 0 else low
+    return jnp.where(valid_ref[0, 0:1, 0:1] == 0.0, high, low)
 
 
 def pack_kernel(p, valid_ref, counts_ref, activity_ref, back_ref, edges_ref):
@@ -118,45 +120,57 @@
             edges_ref[slot, p.edge_back + p.views :] = jnp.zeros((tail, p.width), F32)
 
 
-def send_kernel(p, edges_ref, counts_ref, activity_ref, back_ref, values_ref, starts_ref, payload_ref, *outs):
+def payload_kernel(p, edges_ref, activity_ref, payload_ref):
     payload_ref[: p.block] = activity_ref[...].reshape(p.block, p.width)
     for e in range(p.n_edges):
         low = p.block + e * 2 * p.each
         payload_ref[low : low + 2 * p.each] = edges_ref[e, : 2 * p.each].astype(BF16)
+
+
+def send_kernel(p, valid_ref, counts_ref, back_ref, values_ref, starts_ref, early_ref, *outs):
+    at = lax.axis_index("view")
+    row = lambda k: p.peer(at // p.pairs, k) * p.pairs + p.pairs - 1 - at % p.pairs
+    last = p.slices - 1
+    back = back_ref[...].astype(F32)
+    for slot in range(p.n_edges):
+        edge = functools.partial(edge_of, p, valid_ref, slot)
+        pieces = []
+        for v in range(p.views):
+            for k in p.order:
+                high, low = counts_ref[v, row(k), :, last, :], counts_ref[v, row(k), :, 0, :]
+                pieces.append(edge(high, low).astype(F32))
+        pieces += [edge(back[v, last : last + 1], back[v, 0:1]) for v in range(p.views)]
+        tail = p.early_rows - p.early_back - p.views
+        if tail:
+            pieces.append(jnp.zeros((tail, p.width), F32))
+        early_ref[slot] = jnp.concatenate(pieces, axis=0).astype(BF16)
     out = outs[0]
     out[: p.bands] = values_ref[...].reshape(p.bands, p.width)
     out[p.bands : p.starts] = back_ref[...].reshape(p.views * p.slices, p.width)
     starts = jnp.concatenate([starts_ref[t] for t in range(p.taps)], axis=0)
-    pieces = [lax.shift_right_logical(starts, 7).astype(F32), (starts & 127).astype(F32)]
-    pieces += [edges_ref[e, p.edge_back : p.edge_back + p.views] for e in range(p.n_edges)]
-    tail = p.param_rows - p.edge_backs - p.n_edges * p.views
+    pieces = [lax.shift_right_logical(starts, 7), starts & 127]
+    tail = p.param_rows - p.starts - 2 * p.views * p.taps
     if tail:
-        pieces.append(jnp.zeros((tail, p.width), F32))
-    out[p.starts : p.param_rows] = jnp.concatenate(pieces, axis=0).astype(BF16)
-    for m, out in enumerate(outs):
-        put_counts(p, m, edges_ref, counts_ref, out)
-
-
-def put_counts(p, m, edges_ref, counts_ref, out):
+        pieces.append(jnp.zeros((tail, p.width), I32))
+    out[p.starts : p.param_rows] = jnp.concatenate(pieces, axis=0).astype(F32).astype(BF16)
+    put_counts(p, 0, counts_ref, out)
+
+
+def put_counts(p, m, counts_ref, out):
     at = lax.axis_index("view")
     ks = p.message_peers(m)
-    rows = [p.peer(at // p.pairs, k) * p.pairs + p.pairs - 1 - at % p.pairs for k in ks]
     for v in range(p.views):
-        for i, row in enumerate(rows):
+        for i, k in enumerate(ks):
+            row = p.peer(at // p.pairs, k) * p.pairs + p.pairs - 1 - at % p.pairs
             low = p.base(m) + (v * len(ks) + i) * p.block
             counts = counts_ref[v, row].astype(F32).astype(BF16)
             out[low : low + p.block] = counts.reshape(p.block, p.width)
-    for e in range(p.n_edges):
-        pieces = []
-        for v in range(p.views):
-            for row in rows:
-                start = p.edge_counts + (v * p.n_view + row) * p.each
-                pieces.append(edges_ref[e, pl.ds(pl.multiple_of(start, p.each), p.each), :])
-        tail = p.edges_each(m) - len(pieces) * p.each
-        if tail:
-            pieces.append(jnp.zeros((tail, p.width), F32))
-        low = p.message_edges(m) + e * p.edges_each(m)
-        out[low : low + p.edges_each(m)] = jnp.concatenate(pieces, axis=0).astype(BF16)
+
+
+def later_kernel(p, early_ref, counts_ref, wide_ref, *outs):
+    wide_ref[...] = early_ref[...].astype(F32)
+    for i, out in enumerate(outs):
+        put_counts(p, 1 + i, counts_ref, out)
 
 
 def place_bands(values, start):
@@ -291,25 +305,18 @@
     refs = refs[after:]
     total = total_ref[...]
     if p.pairs == 2:
-        (message_ref, first_ref, matrix_ref), refs = refs[:3], refs[3:]
+        (message_ref, first_ref, early_ref, matrix_ref), refs = refs[:4], refs[4:]
     outs, scratch = refs[: len(ks)], refs[len(ks) :]
     if p.pairs == 2:
         work = Rows(p, stage, source_ref, *scratch)
         (m,) = [m for m, stages in enumerate(p.messages) if stage in stages]
         peers = p.message_peers(m)
         skip = peers.index(ks[0])
-        last = first_ref[p.starts : p.param_rows].astype(F32)
-        came = []
-        for e in range(p.n_edges):
-            low = p.message_edges(m) + e * p.edges_each(m)
-            came.append(message_ref[low : low + p.edges_each(m)].astype(F32))
+        came = [early_ref[e].astype(F32) for e in range(p.n_edges)]
         for v in range(p.views):
-            low = (v * len(peers) + skip) * p.each
+            low = (v * p.line + p.order.index(ks[0])) * p.each
             edges = [x[low : low + work.rows] for x in came]
-            low = p.edge_backs - p.starts + v
-            edge_backs = [
-                last[low + e * p.views : low + e * p.views + 1] for e in range(p.n_edges)
-            ]
+            edge_backs = [x[p.early_back + v : p.early_back + v + 1] for x in came]
             low = p.base(m) + (v * len(peers) + skip) * p.block
             back = first_ref[p.bands + v * p.slices : p.bands + (v + 1) * p.slices].astype(F32)
             counts = message_ref[low : low + work.main]
@@ -365,60 +372,66 @@
         [shape((p.n_edges, p.edge_rows, width), F32)],
         valid, counts, activity, background,
     )
-    if p.n_slab == 2:
-        edges = lax.ppermute(edges, "slab", [(0, 1), (1, 0)])
-    elif p.n_slab > 2:
-        up = [(i, i + 1) for i in range(p.n_slab - 1)]
-        down = [(j, i) for i, j in up]
-        edges = jnp.stack([lax.ppermute(edges[0], "slab", up), lax.ppermute(edges[1], "slab", down)])
-    outs = [shape((p.block + 2 * p.n_edges * p.each, width), BF16)]
-    outs += [shape((p.message_rows(m), width), BF16) for m in range(len(p.messages))]
-    payload, *sent = call(
-        part(send_kernel), outs, edges, counts, activity, background, values, starts
+    def swapped(x, flip):
+        n = p.n_slab
+        pairs = [(i, i ^ flip) for i in range(p.n_view)]
+        up = [(i * n + s, j * n + s + 1) for i, j in pairs for s in range(n - 1)]
+        down = [(i * n + s + 1, j * n + s) for i, j in pairs for s in range(n - 1)]
+        send = lambda part, moves: lax.ppermute(part, ("view", "slab"), moves)
+        if n > 2:
+            return jnp.stack([send(x[0], up), send(x[1], down)])
+        return send(x, up + down) if n == 2 else x
+
+    outs = [shape((p.n_edges, p.early_rows, width), BF16)]
+    outs += [shape((p.message_rows(0), width), BF16)]
+    early, *sent = call(part(send_kernel), outs, valid, counts, background, values, starts)
+    if p.pairs == 2:
+        early = swapped(early, 1)
+        theirs = [lax.ppermute(x, "view", other) for x in sent]
+        outs = [shape(early.shape, F32)]
+        outs += [shape((p.message_rows(m), width), BF16) for m in range(1, len(p.messages))]
+        early, *later = call(part(later_kernel), outs, early, counts, flops=LONG)
+        theirs += [lax.ppermute(x, "view", other) for x in later]
+    edges = swapped(edges, 0)
+    (payload,) = call(
+        part(payload_kernel),
+        [shape((p.block + 2 * p.n_edges * p.each, width), BF16)],
+        edges, activity,
     )
-    theirs = [lax.ppermute(x, "view", other) for x in sent] if p.pairs == 2 else []
     blocks = {0: payload}
     for k in [k for ks in p.stages for k in ks if k]:
         blocks[k] = lax.ppermute(payload, "view", p.across(k, False))
 
     matrices = shape((p.views, p.taps, width, width), BF16)
     (matrix,) = call(part(matrix_kernel), [matrices], sent[0])
-    own = []
+    if p.pairs == 2:
+        (their_matrix,) = call(part(matrix_kernel), [matrices], theirs[0])
+
+    code = shape((p.block + padded_16(p.each), width), I16)
+    plain = shape((p.each, p.slices, width), F32)
+    terms, firsts = {}, []
     for stage, ks in enumerate(p.stages):
         rows = len(ks) * p.each
         full = rows * (p.slices + 2)
+        before = list(terms.values())[-1:] if stage > 1 else firsts[:1]
         scratch = [
             pltpu.VMEM((p.views, full, width), BF16),
             pltpu.VMEM((rows, p.slices + 8, width), F32),
             pltpu.VMEM((rows, p.slices + 8, width), F32),
         ]
-        own.append(
-            call(
-                part(own_kernel, stage),
-                [
-                    shape((p.taps, full, width), BF16),
-                    shape((rows, p.slices, width), F32),
-                ],
-                counts, edges, background, matrix, *[blocks[k] for k in ks],
-                *[blocks[p.stages[0][-1]]][: min(stage, 1)],
-                scratch=[pltpu.VMEM((rows, p.slices + 16, width), F32)] + scratch,
-                flops=4 * p.views * p.taps * full * width * width,
-            )
+        own = call(
+            part(own_kernel, stage),
+            [shape((p.taps, full, width), BF16), shape((rows, p.slices, width), F32)],
+            counts, edges, background, matrix, *[blocks[k] for k in ks], *before,
+            scratch=[pltpu.VMEM((rows, p.slices + 16, width), F32)] + scratch,
+            flops=LONG if stage == 0 else 4 * p.views * p.taps * full * width * width,
         )
-    if p.pairs == 2:
-        (their_matrix,) = call(part(matrix_kernel), [matrices], theirs[0])
-
-    code = shape((p.block + padded_16(p.each), width), I16)
-    plain = shape((p.each, p.slices, width), F32)
-    terms = {}
-    for stage, ks in enumerate(p.stages):
-        rows = len(ks) * p.each
-        full = rows * (p.slices + 2)
+        firsts.append(own[1])
         before = list(terms.values())[-1:]
-        args = [*own[stage], *before]
+        args = [*own, *before]
         if p.pairs == 2:
             (m,) = [m for m, stages in enumerate(p.messages) if stage in stages]
-            args += [theirs[m], theirs[0], their_matrix]
+            args += [theirs[m], theirs[0], early, their_matrix]
         outs = call(
             part(their_kernel, stage, len(before)),
             [code if k else plain for k in ks],

time: 28.7 us -> 28.6 us (level)
  waiting for transfers between devices: 8.03 us -> 6.39 us
  starting transfers between devices: 13.3 us -> 14.7 us
    ppermute x3, waiting for transfers between devices: 4.82 us -> 3.48 us  [per_device(): blocks[k] = lax.ppermute(payload, 'view', p.across(k, False))]
    ppermute x3 -> x4, starting transfers between devices: 3.54 us -> 4.83 us  [the longest x2 3.24 us: swapped(): send = lambda part, moves: lax.ppermute(part, ('view', 'slab'), moves)]
    ppermute x3 -> x4, waiting for transfers between devices: 1.03 us -> 0.3 us  [the longest x1 0.29 us: per_device(): theirs = [lax.ppermute(x, 'view', other) for x in sent]]
    ppermute x3, waiting for transfers between devices: 2.18 us -> 2.61 us  [per_device(): lax.ppermute(terms[k], 'view', p.across(k, True))]
    pallas_call x13 -> x15, Pallas kernels: 5.54 us -> 5.6 us  [call(): pl.pallas_call(kernel, out_shape=outs, in_specs=[VMEM] * len(args), out_s...]
  transfers between devices with their start and end apart: 9 -> 10, of which waited for: 6 -> 6; matrix products, arithmetic and copies ran while one was open for 0% -> 0% of each run, Pallas kernels for 16% -> 17%
where the time goes in v6:
time: 28.6 us; the launch traced here: 28.4 us
  starting transfers between devices  14.7 us (51%)
  waiting for transfers between devices  6.39 us (22%)
  Pallas kernels  5.6 us (20%)
  local copies, waits for them, and re-layouts  1.58 us (6%)
    pallas_call x15, Pallas kernels, call(): pl.pallas_call(kernel, out_shape=outs, in_specs=[VMEM] * len(args), out_s...  5.6 us
    ppermute x3, starting transfers between devices, per_device(): lax.ppermute(terms[k], 'view', p.across(k, True))  5.19 us
    ppermute x3, starting transfers between devices, per_device(): blocks[k] = lax.ppermute(payload, 'view', p.across(k, False))  4.71 us
    ppermute x3, waiting for transfers between devices, per_device(): blocks[k] = lax.ppermute(payload, 'view', p.across(k, False))  3.48 us
    ppermute x2, starting transfers between devices, swapped(): send = lambda part, moves: lax.ppermute(part, ('view', 'slab'), moves)  3.24 us
    ppermute x3, waiting for transfers between devices, per_device(): lax.ppermute(terms[k], 'view', p.across(k, True))  2.61 us
    ppermute x1, starting transfers between devices, per_device(): theirs += [lax.ppermute(x, 'view', other) for x in later]  1.58 us
    unnamed x10, local copies, waits for them, and re-layouts  1.58 us
  transfers between devices with their start and end apart: 10, of which 6 were waited for; matrix products, arithmetic and copies ran while one was open for 0% of the time, Pallas kernels for 17%

profile of v6, /device:TPU:0, one launch (start us, length us, event | category | flops | bytes accessed | tf_op | source)
XLA Modules:
  0.0 28.4 jit_solution(847850632988689273)
XLA Ops:
  0.0 0.0 copy-start.3
  0.0 0.0 copy-start.4
  0.0 1.6 %copy-done = s32[2,64,16,256]{3,2,1,0:T(8,128)S(1)} copy-done((s32[2,64,16,256]{3,2,1,0:T(8,128)S(1)}, s32[2,64,16,256]{3,2,1,0:T(8,128)}, u32[]{:S(2)}) %copy-start) | copy-done | bytes 2097176
  1.6 0.1 shard_map.56
  1.7 0.5 %collective-permute-start = (f32[1,160,256]{2,1,0:T(8,128)S(1)}, f32[1,160,256]{2,1,0:T(8,128)S(1)}, u32[]{:S(2)}, u32[]{:S(2)}) collective-permute-start(f32[1,160,256]{2,1,0:T(8,128)S(1)} %shard_map.56), channel_id=1, source_target_pairs={{0,1},{2,3},{4,5},{6,7},{8,9},{10,11},{12,13},{14,15},{1,0},{3,2},... | collective-permute-start | bytes 491528 | tf_op jit(solution)/shard_map/ppermute | solution.py:380
  2.3 0.1 shard_map.57
  2.4 2.7 %collective-permute-start.5 = (bf16[1,80,256]{2,1,0:T(8,128)(2,1)S(1)}, bf16[1,80,256]{2,1,0:T(8,128)(2,1)S(1)}, u32[]{:S(2)}, u32[]{:S(2)}) collective-permute-start(bf16[1,80,256]{2,1,0:T(8,128)(2,1)S(1)} %get-tuple-element.22), channel_id=1, source_target_pairs={{0,3},{2,1},{4,7},{6,5},{8,11},{10,9},{12,15},{14,13},{1,2},{3,0},... | collective-permute-start | bytes 122888 | tf_op jit(solution)/shard_map/ppermute | solution.py:380
  5.1 0.0 collective-permute-start.4
  5.1 0.3 %shard_map.58.matrix_ref = bf16[2,3,256,256]{3,2,1,0:T(8,128)(2,1)S(1)} custom-call(bf16[752,256]{1,0:T(8,128)(2,1)S(1)} %get-tuple-element.17.params_ref), custom_call_target="tpu_custom_call" | custom-call | bytes 1171456 | tf_op jit(solution)/shard_map/pallas_call | solution.py:69
  5.4 0.0 collective-permute-done.edges_ref
  5.4 3.1 %collective-permute-start.2 = (bf16[144,256]{1,0:T(8,128)(2,1)S(1)}, bf16[144,256]{1,0:T(8,128)(2,1)S(1)}, u32[]{:S(2)}, u32[]{:S(2)}) collective-permute-start(bf16[144,256]{1,0:T(8,128)(2,1)S(1)} %shard_map.59.refs_0_), channel_id=1, source_target_pairs={{8,0},{10,2},{12,4},{14,6},{0,8},{2,10},{4,12},{6,14},{9,1},{11,3}... | collective-permute-start | bytes 221192 | tf_op jit(solution)/shard_map/ppermute | solution.py:403
  8.5 1.3 %collective-permute-start.3 = (bf16[144,256]{1,0:T(8,128)(2,1)S(1)}, bf16[144,256]{1,0:T(8,128)(2,1)S(1)}, u32[]{:S(2)}, u32[]{:S(2)}) collective-permute-start(bf16[144,256]{1,0:T(8,128)(2,1)S(1)} %shard_map.59.refs_0_), channel_id=1, source_target_pairs={{12,0},{14,2},{8,4},{10,6},{4,8},{6,10},{0,12},{2,14},{13,1},{15,3... | collective-permute-start | bytes 221192 | tf_op jit(solution)/shard_map/ppermute | solution.py:403
  9.9 0.0 collective-permute-done.5.early_ref
  9.9 1.6 %collective-permute-start.6 = (bf16[512,256]{1,0:T(8,128)(2,1)S(1)}, bf16[512,256]{1,0:T(8,128)(2,1)S(1)}, u32[]{:S(2)}, u32[]{:S(2)}) collective-permute-start(bf16[512,256]{1,0:T(8,128)(2,1)S(1)} %get-tuple-element.25), channel_id=1, source_target_pairs={{0,2},{2,0},{4,6},{6,4},{8,10},{10,8},{12,14},{14,12},{1,3},{3,1},... | collective-permute-start | bytes 786440 | tf_op jit(solution)/shard_map/ppermute | solution.py:394
  11.5 0.2 collective-permute-start.1
  11.8 1.7 %collective-permute-done.2.refs_0_ = bf16[144,256]{1,0:T(8,128)(2,1)S(1)} collective-permute-done((bf16[144,256]{1,0:T(8,128)(2,1)S(1)}, bf16[144,256]{1,0:T(8,128)(2,1)S(1)}, u32[]{:S(2)}, u32[]{:S(2)}) %collective-permute-start.2) | collective-permute-done | bytes 73760 | tf_op jit(solution)/shard_map/ppermute | solution.py:403
  13.4 1.8 %collective-permute-done.3.refs_1_ = bf16[144,256]{1,0:T(8,128)(2,1)S(1)} collective-permute-done((bf16[144,256]{1,0:T(8,128)(2,1)S(1)}, bf16[144,256]{1,0:T(8,128)(2,1)S(1)}, u32[]{:S(2)}, u32[]{:S(2)}) %collective-permute-start.3) | collective-permute-done | bytes 73760 | tf_op jit(solution)/shard_map/ppermute | solution.py:403
  15.2 0.7 %shard_map.60 = (bf16[3,288,256]{2,1,0:T(8,128)(2,1)S(1)}, f32[16,16,256]{2,1,0:T(8,128)S(1)}) custom-call(s32[2,8,8,16,256]{4,3,2,1,0:T(8,128)S(1)} %bitcast.6, f32[1,160,256]{2,1,0:T(8,128)S(1)} %collective-permute-done.edges_ref, bf16[2,16,256]{2,1,0:T(8,128)(2,1)S(1)} %copy-done.1, bf16[2,3,256,256]{3,2,1,0:T(8,128)(2,1)S(1)} %shard_map.58.matrix_ref, ...), custom_call_target="tpu_custom_call" | custom-call | flops 8000000000 | bytes 3915776 | tf_op jit(solution)/shard_map/pallas_call | solution.py:69
  16.0 0.6 %shard_map.61 = (bf16[3,144,256]{2,1,0:T(8,128)(2,1)S(1)}, f32[8,16,256]{2,1,0:T(8,128)S(1)}) custom-call(s32[2,8,8,16,256]{4,3,2,1,0:T(8,128)S(1)} %bitcast.7, f32[1,160,256]{2,1,0:T(8,128)S(1)} %collective-permute-done.edges_ref, bf16[2,16,256]{2,1,0:T(8,128)(2,1)S(1)} %copy-done.1, bf16[2,3,256,256]{3,2,1,0:T(8,128)(2,1)S(1)} %shard_map.58.matrix_ref, ...), custom_call_target="tpu_custom_call" | custom-call | flops 226492416 | bytes 3751936 | tf_op jit(solution)/shard_map/pallas_call | solution.py:69
  16.6 0.3 %collective-permute-done.4.params_ref.refs_0_.refs_1_.refs_2_ = bf16[752,256]{1,0:T(8,128)(2,1)S(1)} collective-permute-done((bf16[752,256]{1,0:T(8,128)(2,1)S(1)}, bf16[752,256]{1,0:T(8,128)(2,1)S(1)}, u32[]{:S(2)}, u32[]{:S(2)}) %collective-permute-start.4) | collective-permute-done | bytes 385056 | tf_op jit(solution)/shard_map/ppermute | solution.py:390
  16.9 0.3 %shard_map.63.refs_3_.refs_4_ = bf16[2,3,256,256]{3,2,1,0:T(8,128)(2,1)S(1)} custom-call(bf16[752,256]{1,0:T(8,128)(2,1)S(1)} %collective-permute-done.4.params_ref.refs_0_.refs_1_.refs_2_), custom_call_target="tpu_custom_call" | custom-call | bytes 1171456 | tf_op jit(solution)/shard_map/pallas_call | solution.py:69
  17.2 0.8 %shard_map.64 = (s16[144,256]{1,0:T(8,128)(2,1)S(1)}, s16[144,256]{1,0:T(8,128)(2,1)S(1)}) custom-call(bf16[3,288,256]{2,1,0:T(8,128)(2,1)S(1)} %get-tuple-element.21.source_ref, f32[16,16,256]{2,1,0:T(8,128)S(1)} %get-tuple-element.18.refs_1_.total_ref, bf16[752,256]{1,0:T(8,128)(2,1)S(1)} %collective-permute-done.4.params_ref.refs_0_.refs_1_.refs_2_, ...), custom_call_target="tpu_custom_call" | custom-call | flops 452984832 | bytes 2490368 | tf_op jit(solution)/shard_map/pallas_call | solution.py:69
  18.0 2.7 %collective-permute-start.8 = (s16[144,256]{1,0:T(8,128)(2,1)S(1)}, s16[144,256]{1,0:T(8,128)(2,1)S(1)}, u32[]{:S(2)}, u32[]{:S(2)}) collective-permute-start(s16[144,256]{1,0:T(8,128)(2,1)S(1)} %get-tuple-element.26), channel_id=1, source_target_pairs={{0,8},{2,10},{4,12},{6,14},{8,0},{10,2},{12,4},{14,6},{1,9},{3,11}... | collective-permute-start | bytes 221192 | tf_op jit(solution)/shard_map/ppermute | solution.py:450
  20.7 1.3 %collective-permute-start.9 = (s16[144,256]{1,0:T(8,128)(2,1)S(1)}, s16[144,256]{1,0:T(8,128)(2,1)S(1)}, u32[]{:S(2)}, u32[]{:S(2)}) collective-permute-start(s16[144,256]{1,0:T(8,128)(2,1)S(1)} %get-tuple-element.24.refs_0_), channel_id=1, source_target_pairs={{0,12},{2,14},{4,8},{6,10},{8,4},{10,6},{12,0},{14,2},{1,13},{3,15... | collective-permute-start | bytes 221192 | tf_op jit(solution)/shard_map/ppermute | solution.py:450
  22.0 0.6 %shard_map.65.refs_1_.refs_0_ = s16[144,256]{1,0:T(8,128)(2,1)S(1)} custom-call(bf16[3,144,256]{2,1,0:T(8,128)(2,1)S(1)} %get-tuple-element.19.source_ref, f32[8,16,256]{2,1,0:T(8,128)S(1)} %get-tuple-element.20.total_ref, s16[144,256]{1,0:T(8,128)(2,1)S(1)} %get-tuple-element.24.refs_0_, bf16[512,256]{1,0:T(8,128)(2,1)S(1)} %collective-permute-done.6.refs_1_, ...), custom_call_target="tpu_custom_call" | custom-call | flops 226492416 | bytes 2015232 | tf_op jit(solution)/shard_map/pallas_call | solution.py:69
  22.6 1.2 %collective-permute-start.7 = (s16[144,256]{1,0:T(8,128)(2,1)S(1)}, s16[144,256]{1,0:T(8,128)(2,1)S(1)}, u32[]{:S(2)}, u32[]{:S(2)}) collective-permute-start(s16[144,256]{1,0:T(8,128)(2,1)S(1)} %shard_map.65.refs_1_.refs_0_), channel_id=1, source_target_pairs={{0,4},{2,6},{4,0},{6,2},{8,12},{10,14},{12,8},{14,10},{1,5},{3,7},... | collective-permute-start | bytes 221192 | tf_op jit(solution)/shard_map/ppermute | solution.py:450
  23.8 0.6 %shard_map.67 = (bf16[3,144,256]{2,1,0:T(8,128)(2,1)S(1)}, f32[8,16,256]{2,1,0:T(8,128)S(1)}) custom-call(s32[2,8,8,16,256]{4,3,2,1,0:T(8,128)S(1)} %bitcast.8, f32[1,160,256]{2,1,0:T(8,128)S(1)} %collective-permute-done.edges_ref, bf16[2,16,256]{2,1,0:T(8,128)(2,1)S(1)} %copy-done.1, bf16[2,3,256,256]{3,2,1,0:T(8,128)(2,1)S(1)} %shard_map.58.matrix_ref, ...), custom_call_target="tpu_custom_call" | custom-call | flops 226492416 | bytes 3563520 | tf_op jit(solution)/shard_map/pallas_call | solution.py:69
  24.5 0.6 %shard_map.68.refs_2_ = f32[8,16,256]{2,1,0:T(8,128)S(1)} custom-call(bf16[3,144,256]{2,1,0:T(8,128)(2,1)S(1)} %get-tuple-element.27.source_ref, f32[8,16,256]{2,1,0:T(8,128)S(1)} %get-tuple-element.28.total_ref, s16[144,256]{1,0:T(8,128)(2,1)S(1)} %shard_map.65.refs_1_.refs_0_, bf16[512,256]{1,0:T(8,128)(2,1)S(1)} %collective-permute-done.6.refs_1_, ...), custom_call_target="tpu_custom_call" | custom-call | flops 226492416 | bytes 2072576 | tf_op jit(solution)/shard_map/pallas_call | solution.py:69
  25.1 0.6 %collective-permute-done.8.refs_0_ = s16[144,256]{1,0:T(8,128)(2,1)S(1)} collective-permute-done((s16[144,256]{1,0:T(8,128)(2,1)S(1)}, s16[144,256]{1,0:T(8,128)(2,1)S(1)}, u32[]{:S(2)}, u32[]{:S(2)}) %collective-permute-start.8) | collective-permute-done | bytes 73760 | tf_op jit(solution)/shard_map/ppermute | solution.py:450
  25.7 1.9 %collective-permute-done.9.refs_1_ = s16[144,256]{1,0:T(8,128)(2,1)S(1)} collective-permute-done((s16[144,256]{1,0:T(8,128)(2,1)S(1)}, s16[144,256]{1,0:T(8,128)(2,1)S(1)}, u32[]{:S(2)}, u32[]{:S(2)}) %collective-permute-start.9) | collective-permute-done | bytes 73760 | tf_op jit(solution)/shard_map/ppermute | solution.py:450
  27.7 0.1 collective-permute-done.7.refs_0_
  27.7 0.7 %shard_map.69 = f32[8,16,256]{2,1,0:T(8,128)} custom-call(s16[144,256]{1,0:T(8,128)(2,1)S(1)} %collective-permute-done.7.refs_0_, f32[8,16,256]{2,1,0:T(8,128)S(1)} %shard_map.66.refs_1_, f32[8,16,256]{2,1,0:T(8,128)S(1)} %shard_map.68.refs_2_), custom_call_target="tpu_custom_call" | custom-call | bytes 466944 | tf_op jit(solution)/shard_map/pallas_call | solution.py:69
  (13 shorter events, 0.1 us)
Async XLA Ops:
  0.0 1.6 %copy-start = (s32[2,64,16,256]{3,2,1,0:T(8,128)S(1)}, s32[2,64,16,256]{3,2,1,0:T(8,128)}, u32[]{:S(2)}) copy-start(s32[2,64,16,256]{3,2,1,0:T(8,128)} %param.6) | copy-start | bytes 6291460
  0.0 1.6 %copy-start.2 = (bf16[8,16,256]{2,1,0:T(8,128)(2,1)S(1)}, bf16[8,16,256]{2,1,0:T(8,128)(2,1)}, u32[]{:S(2)}) copy-start(bf16[8,16,256]{2,1,0:T(8,128)(2,1)} %activity_ref.3) | copy-start | bytes 196612
  0.0 1.6 %copy-start.1 = (bf16[2,16,256]{2,1,0:T(8,128)(2,1)S(1)}, bf16[2,16,256]{2,1,0:T(8,128)(2,1)}, u32[]{:S(2)}) copy-start(bf16[2,16,256]{2,1,0:T(8,128)(2,1)} %back_ref.9) | copy-start | bytes 49156
  0.0 2.2 %copy-start.3 = (bf16[2,3,256,32]{2,3,1,0:T(8,128)(2,1)S(1)}, bf16[2,3,256,32]{2,3,1,0:T(8,128)(2,1)}, u32[]{:S(2)}) copy-start(bf16[2,3,256,32]{2,3,1,0:T(8,128)(2,1)} %param.8) | copy-start | bytes 294916
  0.0 2.2 %copy-start.4 = (s32[2,3,256]{2,0,1:T(2,128)S(1)}, s32[2,3,256]{2,0,1:T(2,128)}, u32[]{:S(2)}) copy-start(s32[2,3,256]{2,0,1:T(2,128)} %param.9) | copy-start | bytes 18436
  1.7 3.7 %collective-permute-start = (f32[1,160,256]{2,1,0:T(8,128)S(1)}, f32[1,160,256]{2,1,0:T(8,128)S(1)}, u32[]{:S(2)}, u32[]{:S(2)}) collective-permute-start(f32[1,160,256]{2,1,0:T(8,128)S(1)} %shard_map.56), channel_id=1, source_target_pairs={{0,1},{2,3},{4,5},{6,7},{8,9},{10,11},{12,13},{14,15},{1,0},{3,2},... | collective-permute-start | bytes 491528 | tf_op jit(solution)/shard_map/ppermute | solution.py:380
  2.4 7.5 %collective-permute-start.5 = (bf16[1,80,256]{2,1,0:T(8,128)(2,1)S(1)}, bf16[1,80,256]{2,1,0:T(8,128)(2,1)S(1)}, u32[]{:S(2)}, u32[]{:S(2)}) collective-permute-start(bf16[1,80,256]{2,1,0:T(8,128)(2,1)S(1)} %get-tuple-element.22), channel_id=1, source_target_pairs={{0,3},{2,1},{4,7},{6,5},{8,11},{10,9},{12,15},{14,13},{1,2},{3,0},... | collective-permute-start | bytes 122888 | tf_op jit(solution)/shard_map/ppermute | solution.py:380
  5.1 11.8 %collective-permute-start.4 = (bf16[752,256]{1,0:T(8,128)(2,1)S(1)}, bf16[752,256]{1,0:T(8,128)(2,1)S(1)}, u32[]{:S(2)}, u32[]{:S(2)}) collective-permute-start(bf16[752,256]{1,0:T(8,128)(2,1)S(1)} %get-tuple-element.17.params_ref), channel_id=1, source_target_pairs={{0,2},{2,0},{4,6},{6,4},{8,10},{10,8},{12,14},{14,12},{1,3},{3,1},... | collective-permute-start | bytes 1155080 | tf_op jit(solution)/shard_map/ppermute | solution.py:390
  5.4 8.0 %collective-permute-start.2 = (bf16[144,256]{1,0:T(8,128)(2,1)S(1)}, bf16[144,256]{1,0:T(8,128)(2,1)S(1)}, u32[]{:S(2)}, u32[]{:S(2)}) collective-permute-start(bf16[144,256]{1,0:T(8,128)(2,1)S(1)} %shard_map.59.refs_0_), channel_id=1, source_target_pairs={{8,0},{10,2},{12,4},{14,6},{0,8},{2,10},{4,12},{6,14},{9,1},{11,3}... | collective-permute-start | bytes 221192 | tf_op jit(solution)/shard_map/ppermute | solution.py:403
  8.5 6.7 %collective-permute-start.3 = (bf16[144,256]{1,0:T(8,128)(2,1)S(1)}, bf16[144,256]{1,0:T(8,128)(2,1)S(1)}, u32[]{:S(2)}, u32[]{:S(2)}) collective-permute-start(bf16[144,256]{1,0:T(8,128)(2,1)S(1)} %shard_map.59.refs_0_), channel_id=1, source_target_pairs={{12,0},{14,2},{8,4},{10,6},{4,8},{6,10},{0,12},{2,14},{13,1},{15,3... | collective-permute-start | bytes 221192 | tf_op jit(solution)/shard_map/ppermute | solution.py:403
  9.9 12.0 %collective-permute-start.6 = (bf16[512,256]{1,0:T(8,128)(2,1)S(1)}, bf16[512,256]{1,0:T(8,128)(2,1)S(1)}, u32[]{:S(2)}, u32[]{:S(2)}) collective-permute-start(bf16[512,256]{1,0:T(8,128)(2,1)S(1)} %get-tuple-element.25), channel_id=1, source_target_pairs={{0,2},{2,0},{4,6},{6,4},{8,10},{10,8},{12,14},{14,12},{1,3},{3,1},... | collective-permute-start | bytes 786440 | tf_op jit(solution)/shard_map/ppermute | solution.py:394
  11.5 4.5 %collective-permute-start.1 = (bf16[144,256]{1,0:T(8,128)(2,1)S(1)}, bf16[144,256]{1,0:T(8,128)(2,1)S(1)}, u32[]{:S(2)}, u32[]{:S(2)}) collective-permute-start(bf16[144,256]{1,0:T(8,128)(2,1)S(1)} %shard_map.59.refs_0_), channel_id=1, source_target_pairs={{4,0},{6,2},{0,4},{2,6},{12,8},{14,10},{8,12},{10,14},{5,1},{7,3},... | collective-permute-start | bytes 221192 | tf_op jit(solution)/shard_map/ppermute | solution.py:403
  18.0 7.7 %collective-permute-start.8 = (s16[144,256]{1,0:T(8,128)(2,1)S(1)}, s16[144,256]{1,0:T(8,128)(2,1)S(1)}, u32[]{:S(2)}, u32[]{:S(2)}) collective-permute-start(s16[144,256]{1,0:T(8,128)(2,1)S(1)} %get-tuple-element.26), channel_id=1, source_target_pairs={{0,8},{2,10},{4,12},{6,14},{8,0},{10,2},{12,4},{14,6},{1,9},{3,11}... | collective-permute-start | bytes 221192 | tf_op jit(solution)/shard_map/ppermute | solution.py:450
  20.7 6.9 %collective-permute-start.9 = (s16[144,256]{1,0:T(8,128)(2,1)S(1)}, s16[144,256]{1,0:T(8,128)(2,1)S(1)}, u32[]{:S(2)}, u32[]{:S(2)}) collective-permute-start(s16[144,256]{1,0:T(8,128)(2,1)S(1)} %get-tuple-element.24.refs_0_), channel_id=1, source_target_pairs={{0,12},{2,14},{4,8},{6,10},{8,4},{10,6},{12,0},{14,2},{1,13},{3,15... | collective-permute-start | bytes 221192 | tf_op jit(solution)/shard_map/ppermute | solution.py:450
  22.6 5.1 %collective-permute-start.7 = (s16[144,256]{1,0:T(8,128)(2,1)S(1)}, s16[144,256]{1,0:T(8,128)(2,1)S(1)}, u32[]{:S(2)}, u32[]{:S(2)}) collective-permute-start(s16[144,256]{1,0:T(8,128)(2,1)S(1)} %shard_map.65.refs_1_.refs_0_), channel_id=1, source_target_pairs={{0,4},{2,6},{4,0},{6,2},{8,12},{10,14},{12,8},{14,10},{1,5},{3,7},... | collective-permute-start | bytes 221192 | tf_op jit(solution)/shard_map/ppermute | solution.py:450

commit v7 on v6

--- a/solution.py
+++ b/solution.py
@@ -34,12 +34,18 @@
         self.edge_counts = 2 * self.each
         self.edge_back = self.edge_counts + self.views * self.n_view * self.each
         self.edge_rows = self.edge_back + padded_16(self.views)
-        self.bands = self.views * self.taps * self.band
+        self.all_bands = self.views * self.taps * self.band
+        self.start_rows = padded_16(2 * self.views * self.taps)
+        self.split = self.n_slab == 2 and self.all_bands % 32 == 0
+        self.bands = 0 if self.split else self.all_bands
         self.starts = self.bands + self.views * self.slices
-        self.param_rows = self.starts + padded_16(2 * self.views * self.taps)
+        self.param_rows = self.starts + (0 if self.split else self.start_rows)
         self.order = [k for s in self.stages for k in s]
         self.early_back = self.views * self.line * self.each
-        self.early_rows = padded_16(self.early_back + self.views)
+        self.early_starts = padded_16(self.early_back + self.views)
+        self.early_bands = self.early_starts + self.start_rows
+        self.half = self.all_bands // 2
+        self.early_rows = self.early_bands + self.half if self.split else self.early_starts
 
     def message_peers(self, m):
         return [k for s in self.messages[m] for k in self.stages[s]]
@@ -140,19 +146,27 @@
                 high, low = counts_ref[v, row(k), :, last, :], counts_ref[v, row(k), :, 0, :]
                 pieces.append(edge(high, low).astype(F32))
         pieces += [edge(back[v, last : last + 1], back[v, 0:1]) for v in range(p.views)]
-        tail = p.early_rows - p.early_back - p.views
+        tail = p.early_starts - p.early_back - p.views
         if tail:
             pieces.append(jnp.zeros((tail, p.width), F32))
-        early_ref[slot] = jnp.concatenate(pieces, axis=0).astype(BF16)
+        early_ref[slot, : p.early_starts] = jnp.concatenate(pieces, axis=0).astype(BF16)
     out = outs[0]
-    out[: p.bands] = values_ref[...].reshape(p.bands, p.width)
+    values = values_ref[...].reshape(p.all_bands, p.width)
     out[p.bands : p.starts] = back_ref[...].reshape(p.views * p.slices, p.width)
     starts = jnp.concatenate([starts_ref[t] for t in range(p.taps)], axis=0)
     pieces = [lax.shift_right_logical(starts, 7), starts & 127]
-    tail = p.param_rows - p.starts - 2 * p.views * p.taps
+    tail = p.start_rows - 2 * p.views * p.taps
     if tail:
         pieces.append(jnp.zeros((tail, p.width), I32))
-    out[p.starts : p.param_rows] = jnp.concatenate(pieces, axis=0).astype(F32).astype(BF16)
+    starts = jnp.concatenate(pieces, axis=0).astype(F32).astype(BF16)
+    if p.split:
+        lowest = valid_ref[0, 0:1, 0:1] == 0.0
+        values = values.astype(F32)
+        early_ref[0, p.early_starts : p.early_bands] = starts
+        early_ref[0, p.early_bands :] = jnp.where(lowest, values[: p.half], values[p.half :]).astype(BF16)
+    else:
+        out[: p.bands] = values
+        out[p.starts : p.param_rows] = starts
     put_counts(p, 0, counts_ref, out)
 
 
@@ -167,8 +181,10 @@
             out[low : low + p.block] = counts.reshape(p.block, p.width)
 
 
-def later_kernel(p, early_ref, counts_ref, wide_ref, *outs):
+def later_kernel(p, early_ref, counts_ref, block_ref, wide_ref, half_ref, *outs):
     wide_ref[...] = early_ref[...].astype(F32)
+    if p.split:
+        half_ref[...] = early_ref[0, p.early_bands :]
     for i, out in enumerate(outs):
         put_counts(p, 1 + i, counts_ref, out)
 
@@ -189,17 +205,29 @@
     return moved.astype(BF16)
 
 
-def matrix_kernel(p, params_ref, *refs):
+def own_matrix_kernel(p, values_ref, starts_ref, matrix_ref):
+    for v in range(p.views):
+        for t in range(p.taps):
+            matrix_ref[v, t] = place_bands(values_ref[v, t].astype(F32), starts_ref[t, v : v + 1])
+
+
+def their_matrix_kernel(p, valid_ref, params_ref, *refs):
     matrix_ref = refs[-1]
-    starts = params_ref[p.starts : p.param_rows].astype(F32).astype(I32)
+    if p.split:
+        lowest = valid_ref[0, 0:1, 0:1] == 0.0
+        here, rest = params_ref[0, p.early_bands :], refs[0][...].astype(F32)
+        values = [jnp.where(lowest, rest, here), jnp.where(lowest, here, rest)]
+        values = jnp.concatenate(values, axis=0)
+        starts = params_ref[0, p.early_starts : p.early_bands].astype(I32)
+    else:
+        values = params_ref[: p.bands].astype(F32)
+        starts = params_ref[p.starts : p.param_rows].astype(F32).astype(I32)
     n = p.views * p.taps
     starts = starts[:n] * 128 + starts[n : 2 * n]
     for v in range(p.views):
         for t in range(p.taps):
-            at = v * p.taps + t
-            values = params_ref[at * p.band : (at + 1) * p.band].astype(F32)
-            at = t * p.views + v
-            matrix_ref[v, t] = place_bands(values, starts[at : at + 1])
+            low, at = (v * p.taps + t) * p.band, t * p.views + v
+            matrix_ref[v, t] = place_bands(values[low : low + p.band], starts[at : at + 1])
 
 
 def place_source(p, blocks, lifted_ref, source_ref):
@@ -388,10 +416,6 @@
     if p.pairs == 2:
         early = swapped(early, 1)
         theirs = [lax.ppermute(x, "view", other) for x in sent]
-        outs = [shape(early.shape, F32)]
-        outs += [shape((p.message_rows(m), width), BF16) for m in range(1, len(p.messages))]
-        early, *later = call(part(later_kernel), outs, early, counts, flops=LONG)
-        theirs += [lax.ppermute(x, "view", other) for x in later]
     edges = swapped(edges, 0)
     (payload,) = call(
         part(payload_kernel),
@@ -402,18 +426,26 @@
     for k in [k for ks in p.stages for k in ks if k]:
         blocks[k] = lax.ppermute(payload, "view", p.across(k, False))
 
+    if p.pairs == 2:
+        outs = [shape(early.shape, F32), shape((p.half, width), BF16)]
+        outs += [shape((p.message_rows(m), width), BF16) for m in range(1, len(p.messages))]
+        early, rest, *later = call(part(later_kernel), outs, early, counts, blocks[p.stages[0][0]], flops=LONG)
+        theirs += [lax.ppermute(x, "view", other) for x in later]
+        if p.split:
+            rest = swapped(rest, 0)
     matrices = shape((p.views, p.taps, width, width), BF16)
-    (matrix,) = call(part(matrix_kernel), [matrices], sent[0])
+    (matrix,) = call(part(own_matrix_kernel), [matrices], values, starts)
     if p.pairs == 2:
-        (their_matrix,) = call(part(matrix_kernel), [matrices], theirs[0])
+        made_of = [early, rest] if p.split else theirs[:1]
+        (their_matrix,) = call(part(their_matrix_kernel), [matrices], valid, *made_of, flops=0)
 
     code = shape((p.block + padded_16(p.each), width), I16)
     plain = shape((p.each, p.slices, width), F32)
-    terms, firsts = {}, []
+    terms = {}
     for stage, ks in enumerate(p.stages):
         rows = len(ks) * p.each
         full = rows * (p.slices + 2)
-        before = list(terms.values())[-1:] if stage > 1 else firsts[:1]
+        before = list(terms.values())[-1:]
         scratch = [
             pltpu.VMEM((p.views, full, width), BF16),
             pltpu.VMEM((rows, p.slices + 8, width), F32),
@@ -426,7 +458,6 @@
             scratch=[pltpu.VMEM((rows, p.slices + 16, width), F32)] + scratch,
             flops=LONG if stage == 0 else 4 * p.views * p.taps * full * width * width,
         )
-        firsts.append(own[1])
         before = list(terms.values())[-1:]
         args = [*own, *before]
         if p.pairs == 2:
@@ -444,13 +475,11 @@
             flops=4 * p.views * p.taps * full * width * width,
         )
         terms.update(zip(ks, outs))
-    total = []
+    total = [terms[0]]
     for m in range(len(p.messages)):
         came = [
             lax.ppermute(terms[k], "view", p.across(k, True)) for k in p.message_peers(m) if k
         ]
-        if m == len(p.messages) - 1:
-            total = total + [terms[0]]
         total = list(call(part(sum_kernel, len(came)), [plain], *came, *total))
     return total[0]
 

time: 28.6 us -> 28.3 us (0.990)
  waiting for transfers between devices: 6.39 us -> 5.73 us
    ppermute x1, starting transfers between devices: 0.01 us -> 1.08 us  [per_device(): theirs = [lax.ppermute(x, 'view', other) for x in sent]]
    ppermute x3, waiting for transfers between devices: 2.61 us -> 2.1 us  [per_device(): lax.ppermute(terms[k], 'view', p.across(k, True))]
    ppermute x1, starting transfers between devices: 1.58 us -> 1.15 us  [per_device(): theirs += [lax.ppermute(x, 'view', other) for x in later]]
    ppermute x3, starting transfers between devices: 4.71 us -> 4.37 us  [per_device(): blocks[k] = lax.ppermute(payload, 'view', p.across(k, False))]
    ppermute x2 -> x3, starting transfers between devices: 3.24 us -> 3.28 us  [swapped(): send = lambda part, moves: lax.ppermute(part, ('view', 'slab'), moves)]
  transfers between devices with their start and end apart: 10 -> 11, of which waited for: 6 -> 5; matrix products, arithmetic and copies ran while one was open for 0% -> 0% of each run, Pallas kernels for 17% -> 17%
where the time goes in v7:
time: 28.3 us; the launch traced here: 28.1 us
  starting transfers between devices  14.9 us (53%)
  waiting for transfers between devices  5.73 us (20%)
  Pallas kernels  5.65 us (20%)
  local copies, waits for them, and re-layouts  1.63 us (6%)
    pallas_call x15, Pallas kernels, call(): pl.pallas_call(kernel, out_shape=outs, in_specs=[VMEM] * len(args), out_s...  5.65 us
    ppermute x3, starting transfers between devices, per_device(): lax.ppermute(terms[k], 'view', p.across(k, True))  5.04 us
    ppermute x3, starting transfers between devices, per_device(): blocks[k] = lax.ppermute(payload, 'view', p.across(k, False))  4.37 us
    ppermute x3, waiting for transfers between devices, per_device(): blocks[k] = lax.ppermute(payload, 'view', p.across(k, False))  3.48 us
    ppermute x3, starting transfers between devices, swapped(): send = lambda part, moves: lax.ppermute(part, ('view', 'slab'), moves)  3.28 us
    ppermute x3, waiting for transfers between devices, per_device(): lax.ppermute(terms[k], 'view', p.across(k, True))  2.1 us
    unnamed x10, local copies, waits for them, and re-layouts  1.63 us
    ppermute x1, starting transfers between devices, per_device(): theirs += [lax.ppermute(x, 'view', other) for x in later]  1.15 us
  transfers between devices with their start and end apart: 11, of which 5 were waited for; matrix products, arithmetic and copies ran while one was open for 0% of the time, Pallas kernels for 17%

profile of v7, /device:TPU:0, one launch (start us, length us, event | category | flops | bytes accessed | tf_op | source)
XLA Modules:
  0.0 28.1 jit_solution(1075579290358360951)
XLA Ops:
  0.0 0.0 copy-start.1
  0.0 0.7 %copy-done.2 = bf16[2,16,256]{2,1,0:T(8,128)(2,1)S(1)} copy-done((bf16[2,16,256]{2,1,0:T(8,128)(2,1)S(1)}, bf16[2,16,256]{2,1,0:T(8,128)(2,1)}, u32[]{:S(2)}) %copy-start.2) | copy-done | bytes 16408
  0.7 0.1 copy-done.3
  0.9 0.8 %copy-done = s32[2,64,16,256]{3,2,1,0:T(8,128)S(1)} copy-done((s32[2,64,16,256]{3,2,1,0:T(8,128)S(1)}, s32[2,64,16,256]{3,2,1,0:T(8,128)}, u32[]{:S(2)}) %copy-start) | copy-done | bytes 2097176
  1.6 0.1 shard_map.56
  1.8 0.5 %collective-permute-start = (f32[1,160,256]{2,1,0:T(8,128)S(1)}, f32[1,160,256]{2,1,0:T(8,128)S(1)}, u32[]{:S(2)}, u32[]{:S(2)}) collective-permute-start(f32[1,160,256]{2,1,0:T(8,128)S(1)} %shard_map.56), channel_id=1, source_target_pairs={{0,1},{2,3},{4,5},{6,7},{8,9},{10,11},{12,13},{14,15},{1,0},{3,2},... | collective-permute-start | bytes 491528 | tf_op jit(solution)/shard_map/ppermute | solution.py:408
  2.3 0.1 shard_map.60
  2.4 2.7 %collective-permute-start.5 = (bf16[1,192,256]{2,1,0:T(8,128)(2,1)S(1)}, bf16[1,192,256]{2,1,0:T(8,128)(2,1)S(1)}, u32[]{:S(2)}, u32[]{:S(2)}) collective-permute-start(bf16[1,192,256]{2,1,0:T(8,128)(2,1)S(1)} %get-tuple-element.21), channel_id=1, source_target_pairs={{0,3},{2,1},{4,7},{6,5},{8,11},{10,9},{12,15},{14,13},{1,2},{3,0},... | collective-permute-start | bytes 294920 | tf_op jit(solution)/shard_map/ppermute | solution.py:408
  5.1 2.7 %collective-permute-start.2 = (bf16[144,256]{1,0:T(8,128)(2,1)S(1)}, bf16[144,256]{1,0:T(8,128)(2,1)S(1)}, u32[]{:S(2)}, u32[]{:S(2)}) collective-permute-start(bf16[144,256]{1,0:T(8,128)(2,1)S(1)} %shard_map.58.refs_0_), channel_id=1, source_target_pairs={{8,0},{10,2},{12,4},{14,6},{0,8},{2,10},{4,12},{6,14},{9,1},{11,3}... | collective-permute-start | bytes 221192 | tf_op jit(solution)/shard_map/ppermute | solution.py:427
  7.8 1.1 %collective-permute-start.4 = (bf16[544,256]{1,0:T(8,128)(2,1)S(1)}, bf16[544,256]{1,0:T(8,128)(2,1)S(1)}, u32[]{:S(2)}, u32[]{:S(2)}) collective-permute-start(bf16[544,256]{1,0:T(8,128)(2,1)S(1)} %get-tuple-element.20), channel_id=1, source_target_pairs={{0,2},{2,0},{4,6},{6,4},{8,10},{10,8},{12,14},{14,12},{1,3},{3,1},... | collective-permute-start | bytes 835592 | tf_op jit(solution)/shard_map/ppermute | solution.py:418
  8.9 0.3 %shard_map.57.matrix_ref = bf16[2,3,256,256]{3,2,1,0:T(8,128)(2,1)S(1)} custom-call(bf16[2,3,32,256]{3,2,1,0:T(8,128)(2,1)S(1)} %bitcast.10, s32[3,2,256]{2,1,0:T(2,128)S(1)} %bitcast.12), custom_call_target="tpu_custom_call" | custom-call | bytes 890880 | tf_op jit(solution)/shard_map/pallas_call | solution.py:75
  9.2 1.4 %collective-permute-start.3 = (bf16[144,256]{1,0:T(8,128)(2,1)S(1)}, bf16[144,256]{1,0:T(8,128)(2,1)S(1)}, u32[]{:S(2)}, u32[]{:S(2)}) collective-permute-start(bf16[144,256]{1,0:T(8,128)(2,1)S(1)} %shard_map.58.refs_0_), channel_id=1, source_target_pairs={{12,0},{14,2},{8,4},{10,6},{4,8},{6,10},{0,12},{2,14},{13,1},{15,3... | collective-permute-start | bytes 221192 | tf_op jit(solution)/shard_map/ppermute | solution.py:427
  10.6 0.3 %collective-permute-start.1 = (bf16[144,256]{1,0:T(8,128)(2,1)S(1)}, bf16[144,256]{1,0:T(8,128)(2,1)S(1)}, u32[]{:S(2)}, u32[]{:S(2)}) collective-permute-start(bf16[144,256]{1,0:T(8,128)(2,1)S(1)} %shard_map.58.refs_0_), channel_id=1, source_target_pairs={{4,0},{6,2},{0,4},{2,6},{12,8},{14,10},{8,12},{10,14},{5,1},{7,3},... | collective-permute-start | bytes 221192 | tf_op jit(solution)/shard_map/ppermute | solution.py:427
  10.9 1.1 %collective-permute-done.2.refs_0_.block_ref = bf16[144,256]{1,0:T(8,128)(2,1)S(1)} collective-permute-done((bf16[144,256]{1,0:T(8,128)(2,1)S(1)}, bf16[144,256]{1,0:T(8,128)(2,1)S(1)}, u32[]{:S(2)}, u32[]{:S(2)}) %collective-permute-start.2) | collective-permute-done | bytes 73760 | tf_op jit(solution)/shard_map/ppermute | solution.py:427
  12.1 0.1 collective-permute-start.6
  12.2 1.1 %collective-permute-start.7 = (bf16[512,256]{1,0:T(8,128)(2,1)S(1)}, bf16[512,256]{1,0:T(8,128)(2,1)S(1)}, u32[]{:S(2)}, u32[]{:S(2)}) collective-permute-start(bf16[512,256]{1,0:T(8,128)(2,1)S(1)} %get-tuple-element.27), channel_id=1, source_target_pairs={{0,2},{2,0},{4,6},{6,4},{8,10},{10,8},{12,14},{14,12},{1,3},{3,1},... | collective-permute-start | bytes 786440 | tf_op jit(solution)/shard_map/ppermute | solution.py:433
  13.3 2.3 %collective-permute-done.3.refs_1_ = bf16[144,256]{1,0:T(8,128)(2,1)S(1)} collective-permute-done((bf16[144,256]{1,0:T(8,128)(2,1)S(1)}, bf16[144,256]{1,0:T(8,128)(2,1)S(1)}, u32[]{:S(2)}, u32[]{:S(2)}) %collective-permute-start.3) | collective-permute-done | bytes 73760 | tf_op jit(solution)/shard_map/ppermute | solution.py:427
  15.6 0.7 %shard_map.59 = (bf16[3,288,256]{2,1,0:T(8,128)(2,1)S(1)}, f32[16,16,256]{2,1,0:T(8,128)S(1)}) custom-call(s32[2,8,8,16,256]{4,3,2,1,0:T(8,128)S(1)} %bitcast.6, f32[1,160,256]{2,1,0:T(8,128)S(1)} %collective-permute-done.edges_ref, bf16[2,16,256]{2,1,0:T(8,128)(2,1)S(1)} %copy-done.2, bf16[2,3,256,256]{3,2,1,0:T(8,128)(2,1)S(1)} %shard_map.57.matrix_ref, ...), custom_call_target="tpu_custom_call" | custom-call | flops 8000000000 | bytes 3915776 | tf_op jit(solution)/shard_map/pallas_call | solution.py:75
  16.4 0.3 %shard_map.62.refs_3_.refs_4_ = bf16[2,3,256,256]{3,2,1,0:T(8,128)(2,1)S(1)} custom-call(f32[2,8,128]{2,1,0:T(8,128)S(1)} %shard_map.55.valid_ref, f32[1,192,256]{2,1,0:T(8,128)S(1)} %get-tuple-element.22.params_ref.refs_2_.refs_3_, bf16[96,256]{1,0:T(8,128)(2,1)S(1)} %collective-permute-done.6.refs_0_), custom_call_target="tpu_custom_call" | custom-call | bytes 1040384 | tf_op jit(solution)/shard_map/pallas_call | solution.py:75
  16.7 0.1 collective-permute-done.4.refs_0_.refs_1_.refs_2_
  16.9 0.8 %shard_map.63 = (s16[144,256]{1,0:T(8,128)(2,1)S(1)}, s16[144,256]{1,0:T(8,128)(2,1)S(1)}) custom-call(bf16[3,288,256]{2,1,0:T(8,128)(2,1)S(1)} %get-tuple-element.18.source_ref, f32[16,16,256]{2,1,0:T(8,128)S(1)} %get-tuple-element.19.total_ref, bf16[544,256]{1,0:T(8,128)(2,1)S(1)} %collective-permute-done.4.refs_0_.refs_1_.refs_2_, ...), custom_call_target="tpu_custom_call" | custom-call | flops 452984832 | bytes 2392064 | tf_op jit(solution)/shard_map/pallas_call | solution.py:75
  17.7 1.9 %collective-permute-start.9 = (s16[144,256]{1,0:T(8,128)(2,1)S(1)}, s16[144,256]{1,0:T(8,128)(2,1)S(1)}, u32[]{:S(2)}, u32[]{:S(2)}) collective-permute-start(s16[144,256]{1,0:T(8,128)(2,1)S(1)} %get-tuple-element.28), channel_id=1, source_target_pairs={{0,8},{2,10},{4,12},{6,14},{8,0},{10,2},{12,4},{14,6},{1,9},{3,11}... | collective-permute-start | bytes 221192 | tf_op jit(solution)/shard_map/ppermute | solution.py:481
  19.6 2.1 %collective-permute-start.10 = (s16[144,256]{1,0:T(8,128)(2,1)S(1)}, s16[144,256]{1,0:T(8,128)(2,1)S(1)}, u32[]{:S(2)}, u32[]{:S(2)}) collective-permute-start(s16[144,256]{1,0:T(8,128)(2,1)S(1)} %get-tuple-element.24.refs_1_.refs_0_), channel_id=1, source_target_pairs={{0,12},{2,14},{4,8},{6,10},{8,4},{10,6},{12,0},{14,2},{1,13},{3,15... | collective-permute-start | bytes 221192 | tf_op jit(solution)/shard_map/ppermute | solution.py:481
  21.7 0.6 %shard_map.64 = (bf16[3,144,256]{2,1,0:T(8,128)(2,1)S(1)}, f32[8,16,256]{2,1,0:T(8,128)S(1)}) custom-call(s32[2,8,8,16,256]{4,3,2,1,0:T(8,128)S(1)} %bitcast.7, f32[1,160,256]{2,1,0:T(8,128)S(1)} %collective-permute-done.edges_ref, bf16[2,16,256]{2,1,0:T(8,128)(2,1)S(1)} %copy-done.2, bf16[2,3,256,256]{3,2,1,0:T(8,128)(2,1)S(1)} %shard_map.57.matrix_ref, ...), custom_call_target="tpu_custom_call" | custom-call | flops 226492416 | bytes 3563520 | tf_op jit(solution)/shard_map/pallas_call | solution.py:75
  22.3 0.6 %shard_map.65.refs_1_.refs_0_ = s16[144,256]{1,0:T(8,128)(2,1)S(1)} custom-call(bf16[3,144,256]{2,1,0:T(8,128)(2,1)S(1)} %get-tuple-element.25.source_ref, f32[8,16,256]{2,1,0:T(8,128)S(1)} %get-tuple-element.26.total_ref, s16[144,256]{1,0:T(8,128)(2,1)S(1)} %get-tuple-element.24.refs_1_.refs_0_, bf16[512,256]{1,0:T(8,128)(2,1)S(1)} %collective-permute-done.7.refs_1_, ...), custom_call_target="tpu_custom_call" | custom-call | flops 226492416 | bytes 2023424 | tf_op jit(solution)/shard_map/pallas_call | solution.py:75
  23.0 1.0 %collective-permute-start.8 = (s16[144,256]{1,0:T(8,128)(2,1)S(1)}, s16[144,256]{1,0:T(8,128)(2,1)S(1)}, u32[]{:S(2)}, u32[]{:S(2)}) collective-permute-start(s16[144,256]{1,0:T(8,128)(2,1)S(1)} %shard_map.65.refs_1_.refs_0_), channel_id=1, source_target_pairs={{0,4},{2,6},{4,0},{6,2},{8,12},{10,14},{12,8},{14,10},{1,5},{3,7},... | collective-permute-start | bytes 221192 | tf_op jit(solution)/shard_map/ppermute | solution.py:481
  24.0 0.6 %shard_map.66 = (bf16[3,144,256]{2,1,0:T(8,128)(2,1)S(1)}, f32[8,16,256]{2,1,0:T(8,128)S(1)}) custom-call(s32[2,8,8,16,256]{4,3,2,1,0:T(8,128)S(1)} %bitcast.8, f32[1,160,256]{2,1,0:T(8,128)S(1)} %collective-permute-done.edges_ref, bf16[2,16,256]{2,1,0:T(8,128)(2,1)S(1)} %copy-done.2, bf16[2,3,256,256]{3,2,1,0:T(8,128)(2,1)S(1)} %shard_map.57.matrix_ref, ...), custom_call_target="tpu_custom_call" | custom-call | flops 226492416 | bytes 3563520 | tf_op jit(solution)/shard_map/pallas_call | solution.py:75
  24.6 0.6 %shard_map.67.refs_2_ = f32[8,16,256]{2,1,0:T(8,128)S(1)} custom-call(bf16[3,144,256]{2,1,0:T(8,128)(2,1)S(1)} %get-tuple-element.29.source_ref, f32[8,16,256]{2,1,0:T(8,128)S(1)} %get-tuple-element.30.total_ref, s16[144,256]{1,0:T(8,128)(2,1)S(1)} %shard_map.65.refs_1_.refs_0_, bf16[512,256]{1,0:T(8,128)(2,1)S(1)} %collective-permute-done.7.refs_1_, ...), custom_call_target="tpu_custom_call" | custom-call | flops 226492416 | bytes 2080768 | tf_op jit(solution)/shard_map/pallas_call | solution.py:75
  25.3 0.6 %collective-permute-done.10.refs_1_ = s16[144,256]{1,0:T(8,128)(2,1)S(1)} collective-permute-done((s16[144,256]{1,0:T(8,128)(2,1)S(1)}, s16[144,256]{1,0:T(8,128)(2,1)S(1)}, u32[]{:S(2)}, u32[]{:S(2)}) %collective-permute-start.10) | collective-permute-done | bytes 73760 | tf_op jit(solution)/shard_map/ppermute | solution.py:481
  25.9 0.1 shard_map.68.refs_1_
  25.9 1.5 %collective-permute-done.8.refs_0_ = s16[144,256]{1,0:T(8,128)(2,1)S(1)} collective-permute-done((s16[144,256]{1,0:T(8,128)(2,1)S(1)}, s16[144,256]{1,0:T(8,128)(2,1)S(1)}, u32[]{:S(2)}, u32[]{:S(2)}) %collective-permute-start.8) | collective-permute-done | bytes 73760 | tf_op jit(solution)/shard_map/ppermute | solution.py:481
  27.4 0.7 %shard_map.69 = f32[8,16,256]{2,1,0:T(8,128)} custom-call(s16[144,256]{1,0:T(8,128)(2,1)S(1)} %collective-permute-done.8.refs_0_, f32[8,16,256]{2,1,0:T(8,128)S(1)} %shard_map.68.refs_1_), custom_call_target="tpu_custom_call" | custom-call | bytes 335872 | tf_op jit(solution)/shard_map/pallas_call | solution.py:75
  (15 shorter events, 0.1 us)
Async XLA Ops:
  0.0 0.7 %copy-start.2 = (bf16[2,16,256]{2,1,0:T(8,128)(2,1)S(1)}, bf16[2,16,256]{2,1,0:T(8,128)(2,1)}, u32[]{:S(2)}) copy-start(bf16[2,16,256]{2,1,0:T(8,128)(2,1)} %back_ref.9) | copy-start | bytes 49156
  0.0 0.9 %copy-start.3 = (bf16[8,16,256]{2,1,0:T(8,128)(2,1)S(1)}, bf16[8,16,256]{2,1,0:T(8,128)(2,1)}, u32[]{:S(2)}) copy-start(bf16[8,16,256]{2,1,0:T(8,128)(2,1)} %activity_ref.3) | copy-start | bytes 196612
  0.0 1.6 %copy-start = (s32[2,64,16,256]{3,2,1,0:T(8,128)S(1)}, s32[2,64,16,256]{3,2,1,0:T(8,128)}, u32[]{:S(2)}) copy-start(s32[2,64,16,256]{3,2,1,0:T(8,128)} %param.6) | copy-start | bytes 6291460
  0.0 2.3 %copy-start.1 = (bf16[2,3,256,32]{2,3,1,0:T(8,128)(2,1)S(1)}, bf16[2,3,256,32]{2,3,1,0:T(8,128)(2,1)}, u32[]{:S(2)}) copy-start(bf16[2,3,256,32]{2,3,1,0:T(8,128)(2,1)} %param.8) | copy-start | bytes 294916
  0.0 2.3 %copy-start.4 = (s32[2,3,256]{2,0,1:T(2,128)S(1)}, s32[2,3,256]{2,0,1:T(2,128)}, u32[]{:S(2)}) copy-start(s32[2,3,256]{2,0,1:T(2,128)} %param.9) | copy-start | bytes 18436
  1.8 3.3 %collective-permute-start = (f32[1,160,256]{2,1,0:T(8,128)S(1)}, f32[1,160,256]{2,1,0:T(8,128)S(1)}, u32[]{:S(2)}, u32[]{:S(2)}) collective-permute-start(f32[1,160,256]{2,1,0:T(8,128)S(1)} %shard_map.56), channel_id=1, source_target_pairs={{0,1},{2,3},{4,5},{6,7},{8,9},{10,11},{12,13},{14,15},{1,0},{3,2},... | collective-permute-start | bytes 491528 | tf_op jit(solution)/shard_map/ppermute | solution.py:408
  2.4 8.5 %collective-permute-start.5 = (bf16[1,192,256]{2,1,0:T(8,128)(2,1)S(1)}, bf16[1,192,256]{2,1,0:T(8,128)(2,1)S(1)}, u32[]{:S(2)}, u32[]{:S(2)}) collective-permute-start(bf16[1,192,256]{2,1,0:T(8,128)(2,1)S(1)} %get-tuple-element.21), channel_id=1, source_target_pairs={{0,3},{2,1},{4,7},{6,5},{8,11},{10,9},{12,15},{14,13},{1,2},{3,0},... | collective-permute-start | bytes 294920 | tf_op jit(solution)/shard_map/ppermute | solution.py:408
  5.1 6.9 %collective-permute-start.2 = (bf16[144,256]{1,0:T(8,128)(2,1)S(1)}, bf16[144,256]{1,0:T(8,128)(2,1)S(1)}, u32[]{:S(2)}, u32[]{:S(2)}) collective-permute-start(bf16[144,256]{1,0:T(8,128)(2,1)S(1)} %shard_map.58.refs_0_), channel_id=1, source_target_pairs={{8,0},{10,2},{12,4},{14,6},{0,8},{2,10},{4,12},{6,14},{9,1},{11,3}... | collective-permute-start | bytes 221192 | tf_op jit(solution)/shard_map/ppermute | solution.py:427
  7.8 9.1 %collective-permute-start.4 = (bf16[544,256]{1,0:T(8,128)(2,1)S(1)}, bf16[544,256]{1,0:T(8,128)(2,1)S(1)}, u32[]{:S(2)}, u32[]{:S(2)}) collective-permute-start(bf16[544,256]{1,0:T(8,128)(2,1)S(1)} %get-tuple-element.20), channel_id=1, source_target_pairs={{0,2},{2,0},{4,6},{6,4},{8,10},{10,8},{12,14},{14,12},{1,3},{3,1},... | collective-permute-start | bytes 835592 | tf_op jit(solution)/shard_map/ppermute | solution.py:418
  9.2 6.5 %collective-permute-start.3 = (bf16[144,256]{1,0:T(8,128)(2,1)S(1)}, bf16[144,256]{1,0:T(8,128)(2,1)S(1)}, u32[]{:S(2)}, u32[]{:S(2)}) collective-permute-start(bf16[144,256]{1,0:T(8,128)(2,1)S(1)} %shard_map.58.refs_0_), channel_id=1, source_target_pairs={{12,0},{14,2},{8,4},{10,6},{4,8},{6,10},{0,12},{2,14},{13,1},{15,3... | collective-permute-start | bytes 221192 | tf_op jit(solution)/shard_map/ppermute | solution.py:427
  10.6 11.1 %collective-permute-start.1 = (bf16[144,256]{1,0:T(8,128)(2,1)S(1)}, bf16[144,256]{1,0:T(8,128)(2,1)S(1)}, u32[]{:S(2)}, u32[]{:S(2)}) collective-permute-start(bf16[144,256]{1,0:T(8,128)(2,1)S(1)} %shard_map.58.refs_0_), channel_id=1, source_target_pairs={{4,0},{6,2},{0,4},{2,6},{12,8},{14,10},{8,12},{10,14},{5,1},{7,3},... | collective-permute-start | bytes 221192 | tf_op jit(solution)/shard_map/ppermute | solution.py:427
  12.1 4.3 %collective-permute-start.6 = (bf16[96,256]{1,0:T(8,128)(2,1)S(1)}, bf16[96,256]{1,0:T(8,128)(2,1)S(1)}, u32[]{:S(2)}, u32[]{:S(2)}) collective-permute-start(bf16[96,256]{1,0:T(8,128)(2,1)S(1)} %get-tuple-element.23), channel_id=1, source_target_pairs={{0,1},{2,3},{4,5},{6,7},{8,9},{10,11},{12,13},{14,15},{1,0},{3,2},... | collective-permute-start | bytes 147464 | tf_op jit(solution)/shard_map/ppermute | solution.py:408
  12.2 10.2 %collective-permute-start.7 = (bf16[512,256]{1,0:T(8,128)(2,1)S(1)}, bf16[512,256]{1,0:T(8,128)(2,1)S(1)}, u32[]{:S(2)}, u32[]{:S(2)}) collective-permute-start(bf16[512,256]{1,0:T(8,128)(2,1)S(1)} %get-tuple-element.27), channel_id=1, source_target_pairs={{0,2},{2,0},{4,6},{6,4},{8,10},{10,8},{12,14},{14,12},{1,3},{3,1},... | collective-permute-start | bytes 786440 | tf_op jit(solution)/shard_map/ppermute | solution.py:433
  17.7 7.6 %collective-permute-start.9 = (s16[144,256]{1,0:T(8,128)(2,1)S(1)}, s16[144,256]{1,0:T(8,128)(2,1)S(1)}, u32[]{:S(2)}, u32[]{:S(2)}) collective-permute-start(s16[144,256]{1,0:T(8,128)(2,1)S(1)} %get-tuple-element.28), channel_id=1, source_target_pairs={{0,8},{2,10},{4,12},{6,14},{8,0},{10,2},{12,4},{14,6},{1,9},{3,11}... | collective-permute-start | bytes 221192 | tf_op jit(solution)/shard_map/ppermute | solution.py:481
  19.6 6.3 %collective-permute-start.10 = (s16[144,256]{1,0:T(8,128)(2,1)S(1)}, s16[144,256]{1,0:T(8,128)(2,1)S(1)}, u32[]{:S(2)}, u32[]{:S(2)}) collective-permute-start(s16[144,256]{1,0:T(8,128)(2,1)S(1)} %get-tuple-element.24.refs_1_.refs_0_), channel_id=1, source_target_pairs={{0,12},{2,14},{4,8},{6,10},{8,4},{10,6},{12,0},{14,2},{1,13},{3,15... | collective-permute-start | bytes 221192 | tf_op jit(solution)/shard_map/ppermute | solution.py:481
  23.0 4.4 %collective-permute-start.8 = (s16[144,256]{1,0:T(8,128)(2,1)S(1)}, s16[144,256]{1,0:T(8,128)(2,1)S(1)}, u32[]{:S(2)}, u32[]{:S(2)}) collective-permute-start(s16[144,256]{1,0:T(8,128)(2,1)S(1)} %shard_map.65.refs_1_.refs_0_), channel_id=1, source_target_pairs={{0,4},{2,6},{4,0},{6,2},{8,12},{10,14},{12,8},{14,10},{1,5},{3,7},... | collective-permute-start | bytes 221192 | tf_op jit(solution)/shard_map/ppermute | solution.py:481

commit v8 on v7

--- a/solution.py
+++ b/solution.py
@@ -478,7 +478,7 @@
     total = [terms[0]]
     for m in range(len(p.messages)):
         came = [
-            lax.ppermute(terms[k], "view", p.across(k, True)) for k in p.message_peers(m) if k
+            lax.ppermute(terms[k], "view", p.across(k, True)) for k in p.message_peers(m)[::-1] if k
         ]
         total = list(call(part(sum_kernel, len(came)), [plain], *came, *total))
     return total[0]

time: 28.3 us -> 28.3 us (level)
  no operation moved by 1% of the time
where the time goes in v8:
time: 28.3 us; the launch traced here: 28.1 us
  starting transfers between devices  14.9 us (53%)
  waiting for transfers between devices  5.73 us (20%)
  Pallas kernels  5.65 us (20%)
  local copies, waits for them, and re-layouts  1.63 us (6%)
    pallas_call x15, Pallas kernels, call(): pl.pallas_call(kernel, out_shape=outs, in_specs=[VMEM] * len(args), out_s...  5.65 us
    ppermute x3, starting transfers between devices, per_device(): lax.ppermute(terms[k], 'view', p.across(k, True))  5.04 us
    ppermute x3, starting transfers between devices, per_device(): blocks[k] = lax.ppermute(payload, 'view', p.across(k, False))  4.37 us
    ppermute x3, waiting for transfers between devices, per_device(): blocks[k] = lax.ppermute(payload, 'view', p.across(k, False))  3.48 us
    ppermute x3, starting transfers between devices, swapped(): send = lambda part, moves: lax.ppermute(part, ('view', 'slab'), moves)  3.28 us
    ppermute x3, waiting for transfers between devices, per_device(): lax.ppermute(terms[k], 'view', p.across(k, True))  2.1 us
    unnamed x10, local copies, waits for them, and re-layouts  1.63 us
    ppermute x1, starting transfers between devices, per_device(): theirs += [lax.ppermute(x, 'view', other) for x in later]  1.15 us
  transfers between devices with their start and end apart: 11, of which 5 were waited for; matrix products, arithmetic and copies ran while one was open for 0% of the time, Pallas kernels for 17%

profile of v8, /device:TPU:0, one launch (start us, length us, event | category | flops | bytes accessed | tf_op | source)
XLA Modules:
  0.0 28.1 jit_solution(18226686772381587342)
XLA Ops:
  0.0 0.0 copy-start.1
  0.0 0.7 %copy-done.2 = bf16[2,16,256]{2,1,0:T(8,128)(2,1)S(1)} copy-done((bf16[2,16,256]{2,1,0:T(8,128)(2,1)S(1)}, bf16[2,16,256]{2,1,0:T(8,128)(2,1)}, u32[]{:S(2)}) %copy-start.2) | copy-done | bytes 16408
  0.7 0.1 copy-done.3
  0.9 0.8 %copy-done = s32[2,64,16,256]{3,2,1,0:T(8,128)S(1)} copy-done((s32[2,64,16,256]{3,2,1,0:T(8,128)S(1)}, s32[2,64,16,256]{3,2,1,0:T(8,128)}, u32[]{:S(2)}) %copy-start) | copy-done | bytes 2097176
  1.6 0.1 shard_map.56
  1.8 0.5 %collective-permute-start = (f32[1,160,256]{2,1,0:T(8,128)S(1)}, f32[1,160,256]{2,1,0:T(8,128)S(1)}, u32[]{:S(2)}, u32[]{:S(2)}) collective-permute-start(f32[1,160,256]{2,1,0:T(8,128)S(1)} %shard_map.56), channel_id=1, source_target_pairs={{0,1},{2,3},{4,5},{6,7},{8,9},{10,11},{12,13},{14,15},{1,0},{3,2},... | collective-permute-start | bytes 491528 | tf_op jit(solution)/shard_map/ppermute | solution.py:408
  2.3 0.1 shard_map.60
  2.4 2.7 %collective-permute-start.5 = (bf16[1,192,256]{2,1,0:T(8,128)(2,1)S(1)}, bf16[1,192,256]{2,1,0:T(8,128)(2,1)S(1)}, u32[]{:S(2)}, u32[]{:S(2)}) collective-permute-start(bf16[1,192,256]{2,1,0:T(8,128)(2,1)S(1)} %get-tuple-element.21), channel_id=1, source_target_pairs={{0,3},{2,1},{4,7},{6,5},{8,11},{10,9},{12,15},{14,13},{1,2},{3,0},... | collective-permute-start | bytes 294920 | tf_op jit(solution)/shard_map/ppermute | solution.py:408
  5.1 2.7 %collective-permute-start.2 = (bf16[144,256]{1,0:T(8,128)(2,1)S(1)}, bf16[144,256]{1,0:T(8,128)(2,1)S(1)}, u32[]{:S(2)}, u32[]{:S(2)}) collective-permute-start(bf16[144,256]{1,0:T(8,128)(2,1)S(1)} %shard_map.58.refs_0_), channel_id=1, source_target_pairs={{8,0},{10,2},{12,4},{14,6},{0,8},{2,10},{4,12},{6,14},{9,1},{11,3}... | collective-permute-start | bytes 221192 | tf_op jit(solution)/shard_map/ppermute | solution.py:427
  7.8 1.1 %collective-permute-start.4 = (bf16[544,256]{1,0:T(8,128)(2,1)S(1)}, bf16[544,256]{1,0:T(8,128)(2,1)S(1)}, u32[]{:S(2)}, u32[]{:S(2)}) collective-permute-start(bf16[544,256]{1,0:T(8,128)(2,1)S(1)} %get-tuple-element.20), channel_id=1, source_target_pairs={{0,2},{2,0},{4,6},{6,4},{8,10},{10,8},{12,14},{14,12},{1,3},{3,1},... | collective-permute-start | bytes 835592 | tf_op jit(solution)/shard_map/ppermute | solution.py:418
  8.9 0.3 %shard_map.57.matrix_ref = bf16[2,3,256,256]{3,2,1,0:T(8,128)(2,1)S(1)} custom-call(bf16[2,3,32,256]{3,2,1,0:T(8,128)(2,1)S(1)} %bitcast.10, s32[3,2,256]{2,1,0:T(2,128)S(1)} %bitcast.12), custom_call_target="tpu_custom_call" | custom-call | bytes 890880 | tf_op jit(solution)/shard_map/pallas_call | solution.py:75
  9.2 1.4 %collective-permute-start.3 = (bf16[144,256]{1,0:T(8,128)(2,1)S(1)}, bf16[144,256]{1,0:T(8,128)(2,1)S(1)}, u32[]{:S(2)}, u32[]{:S(2)}) collective-permute-start(bf16[144,256]{1,0:T(8,128)(2,1)S(1)} %shard_map.58.refs_0_), channel_id=1, source_target_pairs={{12,0},{14,2},{8,4},{10,6},{4,8},{6,10},{0,12},{2,14},{13,1},{15,3... | collective-permute-start | bytes 221192 | tf_op jit(solution)/shard_map/ppermute | solution.py:427
  10.6 0.3 %collective-permute-start.1 = (bf16[144,256]{1,0:T(8,128)(2,1)S(1)}, bf16[144,256]{1,0:T(8,128)(2,1)S(1)}, u32[]{:S(2)}, u32[]{:S(2)}) collective-permute-start(bf16[144,256]{1,0:T(8,128)(2,1)S(1)} %shard_map.58.refs_0_), channel_id=1, source_target_pairs={{4,0},{6,2},{0,4},{2,6},{12,8},{14,10},{8,12},{10,14},{5,1},{7,3},... | collective-permute-start | bytes 221192 | tf_op jit(solution)/shard_map/ppermute | solution.py:427
  10.9 1.1 %collective-permute-done.2.refs_0_.block_ref = bf16[144,256]{1,0:T(8,128)(2,1)S(1)} collective-permute-done((bf16[144,256]{1,0:T(8,128)(2,1)S(1)}, bf16[144,256]{1,0:T(8,128)(2,1)S(1)}, u32[]{:S(2)}, u32[]{:S(2)}) %collective-permute-start.2) | collective-permute-done | bytes 73760 | tf_op jit(solution)/shard_map/ppermute | solution.py:427
  12.1 0.1 collective-permute-start.6
  12.2 1.1 %collective-permute-start.7 = (bf16[512,256]{1,0:T(8,128)(2,1)S(1)}, bf16[512,256]{1,0:T(8,128)(2,1)S(1)}, u32[]{:S(2)}, u32[]{:S(2)}) collective-permute-start(bf16[512,256]{1,0:T(8,128)(2,1)S(1)} %get-tuple-element.27), channel_id=1, source_target_pairs={{0,2},{2,0},{4,6},{6,4},{8,10},{10,8},{12,14},{14,12},{1,3},{3,1},... | collective-permute-start | bytes 786440 | tf_op jit(solution)/shard_map/ppermute | solution.py:433
  13.3 2.3 %collective-permute-done.3.refs_1_ = bf16[144,256]{1,0:T(8,128)(2,1)S(1)} collective-permute-done((bf16[144,256]{1,0:T(8,128)(2,1)S(1)}, bf16[144,256]{1,0:T(8,128)(2,1)S(1)}, u32[]{:S(2)}, u32[]{:S(2)}) %collective-permute-start.3) | collective-permute-done | bytes 73760 | tf_op jit(solution)/shard_map/ppermute | solution.py:427
  15.6 0.7 %shard_map.59 = (bf16[3,288,256]{2,1,0:T(8,128)(2,1)S(1)}, f32[16,16,256]{2,1,0:T(8,128)S(1)}) custom-call(s32[2,8,8,16,256]{4,3,2,1,0:T(8,128)S(1)} %bitcast.6, f32[1,160,256]{2,1,0:T(8,128)S(1)} %collective-permute-done.edges_ref, bf16[2,16,256]{2,1,0:T(8,128)(2,1)S(1)} %copy-done.2, bf16[2,3,256,256]{3,2,1,0:T(8,128)(2,1)S(1)} %shard_map.57.matrix_ref, ...), custom_call_target="tpu_custom_call" | custom-call | flops 8000000000 | bytes 3915776 | tf_op jit(solution)/shard_map/pallas_call | solution.py:75
  16.4 0.3 %shard_map.62.refs_3_.refs_4_ = bf16[2,3,256,256]{3,2,1,0:T(8,128)(2,1)S(1)} custom-call(f32[2,8,128]{2,1,0:T(8,128)S(1)} %shard_map.55.valid_ref, f32[1,192,256]{2,1,0:T(8,128)S(1)} %get-tuple-element.22.params_ref.refs_2_.refs_3_, bf16[96,256]{1,0:T(8,128)(2,1)S(1)} %collective-permute-done.6.refs_0_), custom_call_target="tpu_custom_call" | custom-call | bytes 1040384 | tf_op jit(solution)/shard_map/pallas_call | solution.py:75
  16.7 0.1 collective-permute-done.4.refs_0_.refs_1_.refs_2_
  16.9 0.8 %shard_map.63 = (s16[144,256]{1,0:T(8,128)(2,1)S(1)}, s16[144,256]{1,0:T(8,128)(2,1)S(1)}) custom-call(bf16[3,288,256]{2,1,0:T(8,128)(2,1)S(1)} %get-tuple-element.18.source_ref, f32[16,16,256]{2,1,0:T(8,128)S(1)} %get-tuple-element.19.total_ref, bf16[544,256]{1,0:T(8,128)(2,1)S(1)} %collective-permute-done.4.refs_0_.refs_1_.refs_2_, ...), custom_call_target="tpu_custom_call" | custom-call | flops 452984832 | bytes 2392064 | tf_op jit(solution)/shard_map/pallas_call | solution.py:75
  17.7 1.9 %collective-permute-start.10 = (s16[144,256]{1,0:T(8,128)(2,1)S(1)}, s16[144,256]{1,0:T(8,128)(2,1)S(1)}, u32[]{:S(2)}, u32[]{:S(2)}) collective-permute-start(s16[144,256]{1,0:T(8,128)(2,1)S(1)} %get-tuple-element.28), channel_id=1, source_target_pairs={{0,8},{2,10},{4,12},{6,14},{8,0},{10,2},{12,4},{14,6},{1,9},{3,11}... | collective-permute-start | bytes 221192 | tf_op jit(solution)/shard_map/ppermute | solution.py:481
  19.6 2.1 %collective-permute-start.9 = (s16[144,256]{1,0:T(8,128)(2,1)S(1)}, s16[144,256]{1,0:T(8,128)(2,1)S(1)}, u32[]{:S(2)}, u32[]{:S(2)}) collective-permute-start(s16[144,256]{1,0:T(8,128)(2,1)S(1)} %get-tuple-element.24.refs_1_.refs_0_), channel_id=1, source_target_pairs={{0,12},{2,14},{4,8},{6,10},{8,4},{10,6},{12,0},{14,2},{1,13},{3,15... | collective-permute-start | bytes 221192 | tf_op jit(solution)/shard_map/ppermute | solution.py:481
  21.7 0.6 %shard_map.64 = (bf16[3,144,256]{2,1,0:T(8,128)(2,1)S(1)}, f32[8,16,256]{2,1,0:T(8,128)S(1)}) custom-call(s32[2,8,8,16,256]{4,3,2,1,0:T(8,128)S(1)} %bitcast.7, f32[1,160,256]{2,1,0:T(8,128)S(1)} %collective-permute-done.edges_ref, bf16[2,16,256]{2,1,0:T(8,128)(2,1)S(1)} %copy-done.2, bf16[2,3,256,256]{3,2,1,0:T(8,128)(2,1)S(1)} %shard_map.57.matrix_ref, ...), custom_call_target="tpu_custom_call" | custom-call | flops 226492416 | bytes 3563520 | tf_op jit(solution)/shard_map/pallas_call | solution.py:75
  22.3 0.6 %shard_map.65.refs_1_.refs_0_ = s16[144,256]{1,0:T(8,128)(2,1)S(1)} custom-call(bf16[3,144,256]{2,1,0:T(8,128)(2,1)S(1)} %get-tuple-element.25.source_ref, f32[8,16,256]{2,1,0:T(8,128)S(1)} %get-tuple-element.26.total_ref, s16[144,256]{1,0:T(8,128)(2,1)S(1)} %get-tuple-element.24.refs_1_.refs_0_, bf16[512,256]{1,0:T(8,128)(2,1)S(1)} %collective-permute-done.7.refs_1_, ...), custom_call_target="tpu_custom_call" | custom-call | flops 226492416 | bytes 2023424 | tf_op jit(solution)/shard_map/pallas_call | solution.py:75
  23.0 1.0 %collective-permute-start.8 = (s16[144,256]{1,0:T(8,128)(2,1)S(1)}, s16[144,256]{1,0:T(8,128)(2,1)S(1)}, u32[]{:S(2)}, u32[]{:S(2)}) collective-permute-start(s16[144,256]{1,0:T(8,128)(2,1)S(1)} %shard_map.65.refs_1_.refs_0_), channel_id=1, source_target_pairs={{0,4},{2,6},{4,0},{6,2},{8,12},{10,14},{12,8},{14,10},{1,5},{3,7},... | collective-permute-start | bytes 221192 | tf_op jit(solution)/shard_map/ppermute | solution.py:481
  24.0 0.6 %shard_map.66 = (bf16[3,144,256]{2,1,0:T(8,128)(2,1)S(1)}, f32[8,16,256]{2,1,0:T(8,128)S(1)}) custom-call(s32[2,8,8,16,256]{4,3,2,1,0:T(8,128)S(1)} %bitcast.8, f32[1,160,256]{2,1,0:T(8,128)S(1)} %collective-permute-done.edges_ref, bf16[2,16,256]{2,1,0:T(8,128)(2,1)S(1)} %copy-done.2, bf16[2,3,256,256]{3,2,1,0:T(8,128)(2,1)S(1)} %shard_map.57.matrix_ref, ...), custom_call_target="tpu_custom_call" | custom-call | flops 226492416 | bytes 3563520 | tf_op jit(solution)/shard_map/pallas_call | solution.py:75
  24.6 0.6 %shard_map.67.refs_2_ = f32[8,16,256]{2,1,0:T(8,128)S(1)} custom-call(bf16[3,144,256]{2,1,0:T(8,128)(2,1)S(1)} %get-tuple-element.29.source_ref, f32[8,16,256]{2,1,0:T(8,128)S(1)} %get-tuple-element.30.total_ref, s16[144,256]{1,0:T(8,128)(2,1)S(1)} %shard_map.65.refs_1_.refs_0_, bf16[512,256]{1,0:T(8,128)(2,1)S(1)} %collective-permute-done.7.refs_1_, ...), custom_call_target="tpu_custom_call" | custom-call | flops 226492416 | bytes 2080768 | tf_op jit(solution)/shard_map/pallas_call | solution.py:75
  25.3 0.6 %collective-permute-done.9.refs_0_ = s16[144,256]{1,0:T(8,128)(2,1)S(1)} collective-permute-done((s16[144,256]{1,0:T(8,128)(2,1)S(1)}, s16[144,256]{1,0:T(8,128)(2,1)S(1)}, u32[]{:S(2)}, u32[]{:S(2)}) %collective-permute-start.9) | collective-permute-done | bytes 73760 | tf_op jit(solution)/shard_map/ppermute | solution.py:481
  25.9 0.1 shard_map.68.refs_1_
  25.9 1.5 %collective-permute-done.8.refs_0_ = s16[144,256]{1,0:T(8,128)(2,1)S(1)} collective-permute-done((s16[144,256]{1,0:T(8,128)(2,1)S(1)}, s16[144,256]{1,0:T(8,128)(2,1)S(1)}, u32[]{:S(2)}, u32[]{:S(2)}) %collective-permute-start.8) | collective-permute-done | bytes 73760 | tf_op jit(solution)/shard_map/ppermute | solution.py:481
  27.4 0.7 %shard_map.69 = f32[8,16,256]{2,1,0:T(8,128)} custom-call(s16[144,256]{1,0:T(8,128)(2,1)S(1)} %collective-permute-done.8.refs_0_, f32[8,16,256]{2,1,0:T(8,128)S(1)} %shard_map.68.refs_1_), custom_call_target="tpu_custom_call" | custom-call | bytes 335872 | tf_op jit(solution)/shard_map/pallas_call | solution.py:75
  (15 shorter events, 0.1 us)
Async XLA Ops:
  0.0 0.7 %copy-start.2 = (bf16[2,16,256]{2,1,0:T(8,128)(2,1)S(1)}, bf16[2,16,256]{2,1,0:T(8,128)(2,1)}, u32[]{:S(2)}) copy-start(bf16[2,16,256]{2,1,0:T(8,128)(2,1)} %back_ref.9) | copy-start | bytes 49156
  0.0 0.9 %copy-start.3 = (bf16[8,16,256]{2,1,0:T(8,128)(2,1)S(1)}, bf16[8,16,256]{2,1,0:T(8,128)(2,1)}, u32[]{:S(2)}) copy-start(bf16[8,16,256]{2,1,0:T(8,128)(2,1)} %activity_ref.3) | copy-start | bytes 196612
  0.0 1.6 %copy-start = (s32[2,64,16,256]{3,2,1,0:T(8,128)S(1)}, s32[2,64,16,256]{3,2,1,0:T(8,128)}, u32[]{:S(2)}) copy-start(s32[2,64,16,256]{3,2,1,0:T(8,128)} %param.6) | copy-start | bytes 6291460
  0.0 2.3 %copy-start.1 = (bf16[2,3,256,32]{2,3,1,0:T(8,128)(2,1)S(1)}, bf16[2,3,256,32]{2,3,1,0:T(8,128)(2,1)}, u32[]{:S(2)}) copy-start(bf16[2,3,256,32]{2,3,1,0:T(8,128)(2,1)} %param.8) | copy-start | bytes 294916
  0.0 2.3 %copy-start.4 = (s32[2,3,256]{2,0,1:T(2,128)S(1)}, s32[2,3,256]{2,0,1:T(2,128)}, u32[]{:S(2)}) copy-start(s32[2,3,256]{2,0,1:T(2,128)} %param.9) | copy-start | bytes 18436
  1.8 3.3 %collective-permute-start = (f32[1,160,256]{2,1,0:T(8,128)S(1)}, f32[1,160,256]{2,1,0:T(8,128)S(1)}, u32[]{:S(2)}, u32[]{:S(2)}) collective-permute-start(f32[1,160,256]{2,1,0:T(8,128)S(1)} %shard_map.56), channel_id=1, source_target_pairs={{0,1},{2,3},{4,5},{6,7},{8,9},{10,11},{12,13},{14,15},{1,0},{3,2},... | collective-permute-start | bytes 491528 | tf_op jit(solution)/shard_map/ppermute | solution.py:408
  2.4 8.5 %collective-permute-start.5 = (bf16[1,192,256]{2,1,0:T(8,128)(2,1)S(1)}, bf16[1,192,256]{2,1,0:T(8,128)(2,1)S(1)}, u32[]{:S(2)}, u32[]{:S(2)}) collective-permute-start(bf16[1,192,256]{2,1,0:T(8,128)(2,1)S(1)} %get-tuple-element.21), channel_id=1, source_target_pairs={{0,3},{2,1},{4,7},{6,5},{8,11},{10,9},{12,15},{14,13},{1,2},{3,0},... | collective-permute-start | bytes 294920 | tf_op jit(solution)/shard_map/ppermute | solution.py:408
  5.1 6.9 %collective-permute-start.2 = (bf16[144,256]{1,0:T(8,128)(2,1)S(1)}, bf16[144,256]{1,0:T(8,128)(2,1)S(1)}, u32[]{:S(2)}, u32[]{:S(2)}) collective-permute-start(bf16[144,256]{1,0:T(8,128)(2,1)S(1)} %shard_map.58.refs_0_), channel_id=1, source_target_pairs={{8,0},{10,2},{12,4},{14,6},{0,8},{2,10},{4,12},{6,14},{9,1},{11,3}... | collective-permute-start | bytes 221192 | tf_op jit(solution)/shard_map/ppermute | solution.py:427
  7.8 9.1 %collective-permute-start.4 = (bf16[544,256]{1,0:T(8,128)(2,1)S(1)}, bf16[544,256]{1,0:T(8,128)(2,1)S(1)}, u32[]{:S(2)}, u32[]{:S(2)}) collective-permute-start(bf16[544,256]{1,0:T(8,128)(2,1)S(1)} %get-tuple-element.20), channel_id=1, source_target_pairs={{0,2},{2,0},{4,6},{6,4},{8,10},{10,8},{12,14},{14,12},{1,3},{3,1},... | collective-permute-start | bytes 835592 | tf_op jit(solution)/shard_map/ppermute | solution.py:418
  9.2 6.5 %collective-permute-start.3 = (bf16[144,256]{1,0:T(8,128)(2,1)S(1)}, bf16[144,256]{1,0:T(8,128)(2,1)S(1)}, u32[]{:S(2)}, u32[]{:S(2)}) collective-permute-start(bf16[144,256]{1,0:T(8,128)(2,1)S(1)} %shard_map.58.refs_0_), channel_id=1, source_target_pairs={{12,0},{14,2},{8,4},{10,6},{4,8},{6,10},{0,12},{2,14},{13,1},{15,3... | collective-permute-start | bytes 221192 | tf_op jit(solution)/shard_map/ppermute | solution.py:427
  10.6 11.1 %collective-permute-start.1 = (bf16[144,256]{1,0:T(8,128)(2,1)S(1)}, bf16[144,256]{1,0:T(8,128)(2,1)S(1)}, u32[]{:S(2)}, u32[]{:S(2)}) collective-permute-start(bf16[144,256]{1,0:T(8,128)(2,1)S(1)} %shard_map.58.refs_0_), channel_id=1, source_target_pairs={{4,0},{6,2},{0,4},{2,6},{12,8},{14,10},{8,12},{10,14},{5,1},{7,3},... | collective-permute-start | bytes 221192 | tf_op jit(solution)/shard_map/ppermute | solution.py:427
  12.1 4.3 %collective-permute-start.6 = (bf16[96,256]{1,0:T(8,128)(2,1)S(1)}, bf16[96,256]{1,0:T(8,128)(2,1)S(1)}, u32[]{:S(2)}, u32[]{:S(2)}) collective-permute-start(bf16[96,256]{1,0:T(8,128)(2,1)S(1)} %get-tuple-element.23), channel_id=1, source_target_pairs={{0,1},{2,3},{4,5},{6,7},{8,9},{10,11},{12,13},{14,15},{1,0},{3,2},... | collective-permute-start | bytes 147464 | tf_op jit(solution)/shard_map/ppermute | solution.py:408
  12.2 10.2 %collective-permute-start.7 = (bf16[512,256]{1,0:T(8,128)(2,1)S(1)}, bf16[512,256]{1,0:T(8,128)(2,1)S(1)}, u32[]{:S(2)}, u32[]{:S(2)}) collective-permute-start(bf16[512,256]{1,0:T(8,128)(2,1)S(1)} %get-tuple-element.27), channel_id=1, source_target_pairs={{0,2},{2,0},{4,6},{6,4},{8,10},{10,8},{12,14},{14,12},{1,3},{3,1},... | collective-permute-start | bytes 786440 | tf_op jit(solution)/shard_map/ppermute | solution.py:433
  17.7 7.6 %collective-permute-start.10 = (s16[144,256]{1,0:T(8,128)(2,1)S(1)}, s16[144,256]{1,0:T(8,128)(2,1)S(1)}, u32[]{:S(2)}, u32[]{:S(2)}) collective-permute-start(s16[144,256]{1,0:T(8,128)(2,1)S(1)} %get-tuple-element.28), channel_id=1, source_target_pairs={{0,8},{2,10},{4,12},{6,14},{8,0},{10,2},{12,4},{14,6},{1,9},{3,11}... | collective-permute-start | bytes 221192 | tf_op jit(solution)/shard_map/ppermute | solution.py:481
  19.6 6.3 %collective-permute-start.9 = (s16[144,256]{1,0:T(8,128)(2,1)S(1)}, s16[144,256]{1,0:T(8,128)(2,1)S(1)}, u32[]{:S(2)}, u32[]{:S(2)}) collective-permute-start(s16[144,256]{1,0:T(8,128)(2,1)S(1)} %get-tuple-element.24.refs_1_.refs_0_), channel_id=1, source_target_pairs={{0,12},{2,14},{4,8},{6,10},{8,4},{10,6},{12,0},{14,2},{1,13},{3,15... | collective-permute-start | bytes 221192 | tf_op jit(solution)/shard_map/ppermute | solution.py:481
  23.0 4.4 %collective-permute-start.8 = (s16[144,256]{1,0:T(8,128)(2,1)S(1)}, s16[144,256]{1,0:T(8,128)(2,1)S(1)}, u32[]{:S(2)}, u32[]{:S(2)}) collective-permute-start(s16[144,256]{1,0:T(8,128)(2,1)S(1)} %shard_map.65.refs_1_.refs_0_), channel_id=1, source_target_pairs={{0,4},{2,6},{4,0},{6,2},{8,12},{10,14},{12,8},{14,10},{1,5},{3,7},... | collective-permute-start | bytes 221192 | tf_op jit(solution)/shard_map/ppermute | solution.py:481

commit v9 on v8

--- a/solution.py
+++ b/solution.py
@@ -298,7 +298,7 @@
         part = self.project(0, full)
         self.up_ref[:, : p.slices, :] = part[:main].reshape(shape)
         self.up_ref[:, p.slices, :] = part[main + rows :]
-        part = self.project(2, full)
+        part = self.project(2, main + padded_16(rows))
         self.down_ref[:, 8 : 8 + p.slices, :] = part[:main].reshape(shape)
         self.down_ref[:, 7, :] = part[main : main + rows]
         total = self.project(1, main).reshape(shape)

time: 28.3 us -> 28.3 us (level)
  no operation moved by 1% of the time
where the time goes in v9:
time: 28.3 us; the launch traced here: 28.1 us
  starting transfers between devices  14.9 us (53%)
  waiting for transfers between devices  5.72 us (20%)
  Pallas kernels  5.65 us (20%)
  local copies, waits for them, and re-layouts  1.63 us (6%)
    pallas_call x15, Pallas kernels, call(): pl.pallas_call(kernel, out_shape=outs, in_specs=[VMEM] * len(args), out_s...  5.65 us
    ppermute x3, starting transfers between devices, per_device(): lax.ppermute(terms[k], 'view', p.across(k, True))  5.05 us
    ppermute x3, starting transfers between devices, per_device(): blocks[k] = lax.ppermute(payload, 'view', p.across(k, False))  4.37 us
    ppermute x3, waiting for transfers between devices, per_device(): blocks[k] = lax.ppermute(payload, 'view', p.across(k, False))  3.48 us
    ppermute x3, starting transfers between devices, swapped(): send = lambda part, moves: lax.ppermute(part, ('view', 'slab'), moves)  3.28 us
    ppermute x3, waiting for transfers between devices, per_device(): lax.ppermute(terms[k], 'view', p.across(k, True))  2.08 us
    unnamed x10, local copies, waits for them, and re-layouts  1.63 us
    ppermute x1, starting transfers between devices, per_device(): theirs += [lax.ppermute(x, 'view', other) for x in later]  1.15 us
  transfers between devices with their start and end apart: 11, of which 5 were waited for; matrix products, arithmetic and copies ran while one was open for 0% of the time, Pallas kernels for 17%

profile of v9, /device:TPU:0, one launch (start us, length us, event | category | flops | bytes accessed | tf_op | source)
XLA Modules:
  0.0 28.1 jit_solution(4389012882077917606)
XLA Ops:
  0.0 0.0 copy-start.1
  0.0 0.7 %copy-done.2 = bf16[2,16,256]{2,1,0:T(8,128)(2,1)S(1)} copy-done((bf16[2,16,256]{2,1,0:T(8,128)(2,1)S(1)}, bf16[2,16,256]{2,1,0:T(8,128)(2,1)}, u32[]{:S(2)}) %copy-start.2) | copy-done | bytes 16408
  0.7 0.1 copy-done.3
  0.9 0.8 %copy-done = s32[2,64,16,256]{3,2,1,0:T(8,128)S(1)} copy-done((s32[2,64,16,256]{3,2,1,0:T(8,128)S(1)}, s32[2,64,16,256]{3,2,1,0:T(8,128)}, u32[]{:S(2)}) %copy-start) | copy-done | bytes 2097176
  1.6 0.1 shard_map.56
  1.8 0.5 %collective-permute-start = (f32[1,160,256]{2,1,0:T(8,128)S(1)}, f32[1,160,256]{2,1,0:T(8,128)S(1)}, u32[]{:S(2)}, u32[]{:S(2)}) collective-permute-start(f32[1,160,256]{2,1,0:T(8,128)S(1)} %shard_map.56), channel_id=1, source_target_pairs={{0,1},{2,3},{4,5},{6,7},{8,9},{10,11},{12,13},{14,15},{1,0},{3,2},... | collective-permute-start | bytes 491528 | tf_op jit(solution)/shard_map/ppermute | solution.py:408
  2.3 0.1 shard_map.60
  2.4 2.7 %collective-permute-start.5 = (bf16[1,192,256]{2,1,0:T(8,128)(2,1)S(1)}, bf16[1,192,256]{2,1,0:T(8,128)(2,1)S(1)}, u32[]{:S(2)}, u32[]{:S(2)}) collective-permute-start(bf16[1,192,256]{2,1,0:T(8,128)(2,1)S(1)} %get-tuple-element.21), channel_id=1, source_target_pairs={{0,3},{2,1},{4,7},{6,5},{8,11},{10,9},{12,15},{14,13},{1,2},{3,0},... | collective-permute-start | bytes 294920 | tf_op jit(solution)/shard_map/ppermute | solution.py:408
  5.1 2.7 %collective-permute-start.2 = (bf16[144,256]{1,0:T(8,128)(2,1)S(1)}, bf16[144,256]{1,0:T(8,128)(2,1)S(1)}, u32[]{:S(2)}, u32[]{:S(2)}) collective-permute-start(bf16[144,256]{1,0:T(8,128)(2,1)S(1)} %shard_map.58.refs_0_), channel_id=1, source_target_pairs={{8,0},{10,2},{12,4},{14,6},{0,8},{2,10},{4,12},{6,14},{9,1},{11,3}... | collective-permute-start | bytes 221192 | tf_op jit(solution)/shard_map/ppermute | solution.py:427
  7.8 1.1 %collective-permute-start.4 = (bf16[544,256]{1,0:T(8,128)(2,1)S(1)}, bf16[544,256]{1,0:T(8,128)(2,1)S(1)}, u32[]{:S(2)}, u32[]{:S(2)}) collective-permute-start(bf16[544,256]{1,0:T(8,128)(2,1)S(1)} %get-tuple-element.20), channel_id=1, source_target_pairs={{0,2},{2,0},{4,6},{6,4},{8,10},{10,8},{12,14},{14,12},{1,3},{3,1},... | collective-permute-start | bytes 835592 | tf_op jit(solution)/shard_map/ppermute | solution.py:418
  8.9 0.3 %shard_map.57.matrix_ref = bf16[2,3,256,256]{3,2,1,0:T(8,128)(2,1)S(1)} custom-call(bf16[2,3,32,256]{3,2,1,0:T(8,128)(2,1)S(1)} %bitcast.10, s32[3,2,256]{2,1,0:T(2,128)S(1)} %bitcast.12), custom_call_target="tpu_custom_call" | custom-call | bytes 890880 | tf_op jit(solution)/shard_map/pallas_call | solution.py:75
  9.2 1.4 %collective-permute-start.3 = (bf16[144,256]{1,0:T(8,128)(2,1)S(1)}, bf16[144,256]{1,0:T(8,128)(2,1)S(1)}, u32[]{:S(2)}, u32[]{:S(2)}) collective-permute-start(bf16[144,256]{1,0:T(8,128)(2,1)S(1)} %shard_map.58.refs_0_), channel_id=1, source_target_pairs={{12,0},{14,2},{8,4},{10,6},{4,8},{6,10},{0,12},{2,14},{13,1},{15,3... | collective-permute-start | bytes 221192 | tf_op jit(solution)/shard_map/ppermute | solution.py:427
  10.6 0.3 %collective-permute-start.1 = (bf16[144,256]{1,0:T(8,128)(2,1)S(1)}, bf16[144,256]{1,0:T(8,128)(2,1)S(1)}, u32[]{:S(2)}, u32[]{:S(2)}) collective-permute-start(bf16[144,256]{1,0:T(8,128)(2,1)S(1)} %shard_map.58.refs_0_), channel_id=1, source_target_pairs={{4,0},{6,2},{0,4},{2,6},{12,8},{14,10},{8,12},{10,14},{5,1},{7,3},... | collective-permute-start | bytes 221192 | tf_op jit(solution)/shard_map/ppermute | solution.py:427
  10.9 1.1 %collective-permute-done.2.refs_0_.block_ref = bf16[144,256]{1,0:T(8,128)(2,1)S(1)} collective-permute-done((bf16[144,256]{1,0:T(8,128)(2,1)S(1)}, bf16[144,256]{1,0:T(8,128)(2,1)S(1)}, u32[]{:S(2)}, u32[]{:S(2)}) %collective-permute-start.2) | collective-permute-done | bytes 73760 | tf_op jit(solution)/shard_map/ppermute | solution.py:427
  12.1 0.1 collective-permute-start.6
  12.2 1.1 %collective-permute-start.7 = (bf16[512,256]{1,0:T(8,128)(2,1)S(1)}, bf16[512,256]{1,0:T(8,128)(2,1)S(1)}, u32[]{:S(2)}, u32[]{:S(2)}) collective-permute-start(bf16[512,256]{1,0:T(8,128)(2,1)S(1)} %get-tuple-element.27), channel_id=1, source_target_pairs={{0,2},{2,0},{4,6},{6,4},{8,10},{10,8},{12,14},{14,12},{1,3},{3,1},... | collective-permute-start | bytes 786440 | tf_op jit(solution)/shard_map/ppermute | solution.py:433
  13.3 2.3 %collective-permute-done.3.refs_1_ = bf16[144,256]{1,0:T(8,128)(2,1)S(1)} collective-permute-done((bf16[144,256]{1,0:T(8,128)(2,1)S(1)}, bf16[144,256]{1,0:T(8,128)(2,1)S(1)}, u32[]{:S(2)}, u32[]{:S(2)}) %collective-permute-start.3) | collective-permute-done | bytes 73760 | tf_op jit(solution)/shard_map/ppermute | solution.py:427
  15.6 0.7 %shard_map.59 = (bf16[3,288,256]{2,1,0:T(8,128)(2,1)S(1)}, f32[16,16,256]{2,1,0:T(8,128)S(1)}) custom-call(s32[2,8,8,16,256]{4,3,2,1,0:T(8,128)S(1)} %bitcast.6, f32[1,160,256]{2,1,0:T(8,128)S(1)} %collective-permute-done.edges_ref, bf16[2,16,256]{2,1,0:T(8,128)(2,1)S(1)} %copy-done.2, bf16[2,3,256,256]{3,2,1,0:T(8,128)(2,1)S(1)} %shard_map.57.matrix_ref, ...), custom_call_target="tpu_custom_call" | custom-call | flops 8000000000 | bytes 3915776 | tf_op jit(solution)/shard_map/pallas_call | solution.py:75
  16.4 0.3 %shard_map.62.refs_3_.refs_4_ = bf16[2,3,256,256]{3,2,1,0:T(8,128)(2,1)S(1)} custom-call(f32[2,8,128]{2,1,0:T(8,128)S(1)} %shard_map.55.valid_ref, f32[1,192,256]{2,1,0:T(8,128)S(1)} %get-tuple-element.22.params_ref.refs_2_.refs_3_, bf16[96,256]{1,0:T(8,128)(2,1)S(1)} %collective-permute-done.6.refs_0_), custom_call_target="tpu_custom_call" | custom-call | bytes 1040384 | tf_op jit(solution)/shard_map/pallas_call | solution.py:75
  16.7 0.1 collective-permute-done.4.refs_0_.refs_1_.refs_2_
  16.9 0.8 %shard_map.63 = (s16[144,256]{1,0:T(8,128)(2,1)S(1)}, s16[144,256]{1,0:T(8,128)(2,1)S(1)}) custom-call(bf16[3,288,256]{2,1,0:T(8,128)(2,1)S(1)} %get-tuple-element.18.source_ref, f32[16,16,256]{2,1,0:T(8,128)S(1)} %get-tuple-element.19.total_ref, bf16[544,256]{1,0:T(8,128)(2,1)S(1)} %collective-permute-done.4.refs_0_.refs_1_.refs_2_, ...), custom_call_target="tpu_custom_call" | custom-call | flops 452984832 | bytes 2392064 | tf_op jit(solution)/shard_map/pallas_call | solution.py:75
  17.7 1.9 %collective-permute-start.10 = (s16[144,256]{1,0:T(8,128)(2,1)S(1)}, s16[144,256]{1,0:T(8,128)(2,1)S(1)}, u32[]{:S(2)}, u32[]{:S(2)}) collective-permute-start(s16[144,256]{1,0:T(8,128)(2,1)S(1)} %get-tuple-element.28), channel_id=1, source_target_pairs={{0,8},{2,10},{4,12},{6,14},{8,0},{10,2},{12,4},{14,6},{1,9},{3,11}... | collective-permute-start | bytes 221192 | tf_op jit(solution)/shard_map/ppermute | solution.py:481
  19.6 2.1 %collective-permute-start.9 = (s16[144,256]{1,0:T(8,128)(2,1)S(1)}, s16[144,256]{1,0:T(8,128)(2,1)S(1)}, u32[]{:S(2)}, u32[]{:S(2)}) collective-permute-start(s16[144,256]{1,0:T(8,128)(2,1)S(1)} %get-tuple-element.24.refs_1_.refs_0_), channel_id=1, source_target_pairs={{0,12},{2,14},{4,8},{6,10},{8,4},{10,6},{12,0},{14,2},{1,13},{3,15... | collective-permute-start | bytes 221192 | tf_op jit(solution)/shard_map/ppermute | solution.py:481
  21.7 0.6 %shard_map.64 = (bf16[3,144,256]{2,1,0:T(8,128)(2,1)S(1)}, f32[8,16,256]{2,1,0:T(8,128)S(1)}) custom-call(s32[2,8,8,16,256]{4,3,2,1,0:T(8,128)S(1)} %bitcast.7, f32[1,160,256]{2,1,0:T(8,128)S(1)} %collective-permute-done.edges_ref, bf16[2,16,256]{2,1,0:T(8,128)(2,1)S(1)} %copy-done.2, bf16[2,3,256,256]{3,2,1,0:T(8,128)(2,1)S(1)} %shard_map.57.matrix_ref, ...), custom_call_target="tpu_custom_call" | custom-call | flops 226492416 | bytes 3563520 | tf_op jit(solution)/shard_map/pallas_call | solution.py:75
  22.3 0.6 %shard_map.65.refs_1_.refs_0_ = s16[144,256]{1,0:T(8,128)(2,1)S(1)} custom-call(bf16[3,144,256]{2,1,0:T(8,128)(2,1)S(1)} %get-tuple-element.25.source_ref, f32[8,16,256]{2,1,0:T(8,128)S(1)} %get-tuple-element.26.total_ref, s16[144,256]{1,0:T(8,128)(2,1)S(1)} %get-tuple-element.24.refs_1_.refs_0_, bf16[512,256]{1,0:T(8,128)(2,1)S(1)} %collective-permute-done.7.refs_1_, ...), custom_call_target="tpu_custom_call" | custom-call | flops 226492416 | bytes 2023424 | tf_op jit(solution)/shard_map/pallas_call | solution.py:75
  23.0 1.0 %collective-permute-start.8 = (s16[144,256]{1,0:T(8,128)(2,1)S(1)}, s16[144,256]{1,0:T(8,128)(2,1)S(1)}, u32[]{:S(2)}, u32[]{:S(2)}) collective-permute-start(s16[144,256]{1,0:T(8,128)(2,1)S(1)} %shard_map.65.refs_1_.refs_0_), channel_id=1, source_target_pairs={{0,4},{2,6},{4,0},{6,2},{8,12},{10,14},{12,8},{14,10},{1,5},{3,7},... | collective-permute-start | bytes 221192 | tf_op jit(solution)/shard_map/ppermute | solution.py:481
  24.0 0.6 %shard_map.66 = (bf16[3,144,256]{2,1,0:T(8,128)(2,1)S(1)}, f32[8,16,256]{2,1,0:T(8,128)S(1)}) custom-call(s32[2,8,8,16,256]{4,3,2,1,0:T(8,128)S(1)} %bitcast.8, f32[1,160,256]{2,1,0:T(8,128)S(1)} %collective-permute-done.edges_ref, bf16[2,16,256]{2,1,0:T(8,128)(2,1)S(1)} %copy-done.2, bf16[2,3,256,256]{3,2,1,0:T(8,128)(2,1)S(1)} %shard_map.57.matrix_ref, ...), custom_call_target="tpu_custom_call" | custom-call | flops 226492416 | bytes 3563520 | tf_op jit(solution)/shard_map/pallas_call | solution.py:75
  24.6 0.6 %shard_map.67.refs_2_ = f32[8,16,256]{2,1,0:T(8,128)S(1)} custom-call(bf16[3,144,256]{2,1,0:T(8,128)(2,1)S(1)} %get-tuple-element.29.source_ref, f32[8,16,256]{2,1,0:T(8,128)S(1)} %get-tuple-element.30.total_ref, s16[144,256]{1,0:T(8,128)(2,1)S(1)} %shard_map.65.refs_1_.refs_0_, bf16[512,256]{1,0:T(8,128)(2,1)S(1)} %collective-permute-done.7.refs_1_, ...), custom_call_target="tpu_custom_call" | custom-call | flops 226492416 | bytes 2080768 | tf_op jit(solution)/shard_map/pallas_call | solution.py:75
  25.3 0.6 %collective-permute-done.9.refs_0_ = s16[144,256]{1,0:T(8,128)(2,1)S(1)} collective-permute-done((s16[144,256]{1,0:T(8,128)(2,1)S(1)}, s16[144,256]{1,0:T(8,128)(2,1)S(1)}, u32[]{:S(2)}, u32[]{:S(2)}) %collective-permute-start.9) | collective-permute-done | bytes 73760 | tf_op jit(solution)/shard_map/ppermute | solution.py:481
  25.9 0.1 shard_map.68.refs_1_
  25.9 1.5 %collective-permute-done.8.refs_0_ = s16[144,256]{1,0:T(8,128)(2,1)S(1)} collective-permute-done((s16[144,256]{1,0:T(8,128)(2,1)S(1)}, s16[144,256]{1,0:T(8,128)(2,1)S(1)}, u32[]{:S(2)}, u32[]{:S(2)}) %collective-permute-start.8) | collective-permute-done | bytes 73760 | tf_op jit(solution)/shard_map/ppermute | solution.py:481
  27.4 0.7 %shard_map.69 = f32[8,16,256]{2,1,0:T(8,128)} custom-call(s16[144,256]{1,0:T(8,128)(2,1)S(1)} %collective-permute-done.8.refs_0_, f32[8,16,256]{2,1,0:T(8,128)S(1)} %shard_map.68.refs_1_), custom_call_target="tpu_custom_call" | custom-call | bytes 335872 | tf_op jit(solution)/shard_map/pallas_call | solution.py:75
  (15 shorter events, 0.1 us)
Async XLA Ops:
  0.0 0.7 %copy-start.2 = (bf16[2,16,256]{2,1,0:T(8,128)(2,1)S(1)}, bf16[2,16,256]{2,1,0:T(8,128)(2,1)}, u32[]{:S(2)}) copy-start(bf16[2,16,256]{2,1,0:T(8,128)(2,1)} %back_ref.9) | copy-start | bytes 49156
  0.0 0.9 %copy-start.3 = (bf16[8,16,256]{2,1,0:T(8,128)(2,1)S(1)}, bf16[8,16,256]{2,1,0:T(8,128)(2,1)}, u32[]{:S(2)}) copy-start(bf16[8,16,256]{2,1,0:T(8,128)(2,1)} %activity_ref.3) | copy-start | bytes 196612
  0.0 1.6 %copy-start = (s32[2,64,16,256]{3,2,1,0:T(8,128)S(1)}, s32[2,64,16,256]{3,2,1,0:T(8,128)}, u32[]{:S(2)}) copy-start(s32[2,64,16,256]{3,2,1,0:T(8,128)} %param.6) | copy-start | bytes 6291460
  0.0 2.3 %copy-start.1 = (bf16[2,3,256,32]{2,3,1,0:T(8,128)(2,1)S(1)}, bf16[2,3,256,32]{2,3,1,0:T(8,128)(2,1)}, u32[]{:S(2)}) copy-start(bf16[2,3,256,32]{2,3,1,0:T(8,128)(2,1)} %param.8) | copy-start | bytes 294916
  0.0 2.3 %copy-start.4 = (s32[2,3,256]{2,0,1:T(2,128)S(1)}, s32[2,3,256]{2,0,1:T(2,128)}, u32[]{:S(2)}) copy-start(s32[2,3,256]{2,0,1:T(2,128)} %param.9) | copy-start | bytes 18436
  1.8 3.3 %collective-permute-start = (f32[1,160,256]{2,1,0:T(8,128)S(1)}, f32[1,160,256]{2,1,0:T(8,128)S(1)}, u32[]{:S(2)}, u32[]{:S(2)}) collective-permute-start(f32[1,160,256]{2,1,0:T(8,128)S(1)} %shard_map.56), channel_id=1, source_target_pairs={{0,1},{2,3},{4,5},{6,7},{8,9},{10,11},{12,13},{14,15},{1,0},{3,2},... | collective-permute-start | bytes 491528 | tf_op jit(solution)/shard_map/ppermute | solution.py:408
  2.4 8.5 %collective-permute-start.5 = (bf16[1,192,256]{2,1,0:T(8,128)(2,1)S(1)}, bf16[1,192,256]{2,1,0:T(8,128)(2,1)S(1)}, u32[]{:S(2)}, u32[]{:S(2)}) collective-permute-start(bf16[1,192,256]{2,1,0:T(8,128)(2,1)S(1)} %get-tuple-element.21), channel_id=1, source_target_pairs={{0,3},{2,1},{4,7},{6,5},{8,11},{10,9},{12,15},{14,13},{1,2},{3,0},... | collective-permute-start | bytes 294920 | tf_op jit(solution)/shard_map/ppermute | solution.py:408
  5.1 6.9 %collective-permute-start.2 = (bf16[144,256]{1,0:T(8,128)(2,1)S(1)}, bf16[144,256]{1,0:T(8,128)(2,1)S(1)}, u32[]{:S(2)}, u32[]{:S(2)}) collective-permute-start(bf16[144,256]{1,0:T(8,128)(2,1)S(1)} %shard_map.58.refs_0_), channel_id=1, source_target_pairs={{8,0},{10,2},{12,4},{14,6},{0,8},{2,10},{4,12},{6,14},{9,1},{11,3}... | collective-permute-start | bytes 221192 | tf_op jit(solution)/shard_map/ppermute | solution.py:427
  7.8 9.1 %collective-permute-start.4 = (bf16[544,256]{1,0:T(8,128)(2,1)S(1)}, bf16[544,256]{1,0:T(8,128)(2,1)S(1)}, u32[]{:S(2)}, u32[]{:S(2)}) collective-permute-start(bf16[544,256]{1,0:T(8,128)(2,1)S(1)} %get-tuple-element.20), channel_id=1, source_target_pairs={{0,2},{2,0},{4,6},{6,4},{8,10},{10,8},{12,14},{14,12},{1,3},{3,1},... | collective-permute-start | bytes 835592 | tf_op jit(solution)/shard_map/ppermute | solution.py:418
  9.2 6.5 %collective-permute-start.3 = (bf16[144,256]{1,0:T(8,128)(2,1)S(1)}, bf16[144,256]{1,0:T(8,128)(2,1)S(1)}, u32[]{:S(2)}, u32[]{:S(2)}) collective-permute-start(bf16[144,256]{1,0:T(8,128)(2,1)S(1)} %shard_map.58.refs_0_), channel_id=1, source_target_pairs={{12,0},{14,2},{8,4},{10,6},{4,8},{6,10},{0,12},{2,14},{13,1},{15,3... | collective-permute-start | bytes 221192 | tf_op jit(solution)/shard_map/ppermute | solution.py:427
  10.6 11.1 %collective-permute-start.1 = (bf16[144,256]{1,0:T(8,128)(2,1)S(1)}, bf16[144,256]{1,0:T(8,128)(2,1)S(1)}, u32[]{:S(2)}, u32[]{:S(2)}) collective-permute-start(bf16[144,256]{1,0:T(8,128)(2,1)S(1)} %shard_map.58.refs_0_), channel_id=1, source_target_pairs={{4,0},{6,2},{0,4},{2,6},{12,8},{14,10},{8,12},{10,14},{5,1},{7,3},... | collective-permute-start | bytes 221192 | tf_op jit(solution)/shard_map/ppermute | solution.py:427
  12.1 4.3 %collective-permute-start.6 = (bf16[96,256]{1,0:T(8,128)(2,1)S(1)}, bf16[96,256]{1,0:T(8,128)(2,1)S(1)}, u32[]{:S(2)}, u32[]{:S(2)}) collective-permute-start(bf16[96,256]{1,0:T(8,128)(2,1)S(1)} %get-tuple-element.23), channel_id=1, source_target_pairs={{0,1},{2,3},{4,5},{6,7},{8,9},{10,11},{12,13},{14,15},{1,0},{3,2},... | collective-permute-start | bytes 147464 | tf_op jit(solution)/shard_map/ppermute | solution.py:408
  12.2 10.1 %collective-permute-start.7 = (bf16[512,256]{1,0:T(8,128)(2,1)S(1)}, bf16[512,256]{1,0:T(8,128)(2,1)S(1)}, u32[]{:S(2)}, u32[]{:S(2)}) collective-permute-start(bf16[512,256]{1,0:T(8,128)(2,1)S(1)} %get-tuple-element.27), channel_id=1, source_target_pairs={{0,2},{2,0},{4,6},{6,4},{8,10},{10,8},{12,14},{14,12},{1,3},{3,1},... | collective-permute-start | bytes 786440 | tf_op jit(solution)/shard_map/ppermute | solution.py:433
  17.7 7.6 %collective-permute-start.10 = (s16[144,256]{1,0:T(8,128)(2,1)S(1)}, s16[144,256]{1,0:T(8,128)(2,1)S(1)}, u32[]{:S(2)}, u32[]{:S(2)}) collective-permute-start(s16[144,256]{1,0:T(8,128)(2,1)S(1)} %get-tuple-element.28), channel_id=1, source_target_pairs={{0,8},{2,10},{4,12},{6,14},{8,0},{10,2},{12,4},{14,6},{1,9},{3,11}... | collective-permute-start | bytes 221192 | tf_op jit(solution)/shard_map/ppermute | solution.py:481
  19.6 6.3 %collective-permute-start.9 = (s16[144,256]{1,0:T(8,128)(2,1)S(1)}, s16[144,256]{1,0:T(8,128)(2,1)S(1)}, u32[]{:S(2)}, u32[]{:S(2)}) collective-permute-start(s16[144,256]{1,0:T(8,128)(2,1)S(1)} %get-tuple-element.24.refs_1_.refs_0_), channel_id=1, source_target_pairs={{0,12},{2,14},{4,8},{6,10},{8,4},{10,6},{12,0},{14,2},{1,13},{3,15... | collective-permute-start | bytes 221192 | tf_op jit(solution)/shard_map/ppermute | solution.py:481
  23.0 4.4 %collective-permute-start.8 = (s16[144,256]{1,0:T(8,128)(2,1)S(1)}, s16[144,256]{1,0:T(8,128)(2,1)S(1)}, u32[]{:S(2)}, u32[]{:S(2)}) collective-permute-start(s16[144,256]{1,0:T(8,128)(2,1)S(1)} %shard_map.65.refs_1_.refs_0_), channel_id=1, source_target_pairs={{0,4},{2,6},{4,0},{6,2},{8,12},{10,14},{12,8},{14,10},{1,5},{3,7},... | collective-permute-start | bytes 221192 | tf_op jit(solution)/shard_map/ppermute | solution.py:481
